TPU v7x, 32 devices: a whole 2x2x4 slice. The times are simulated.
32 devices in a mesh: row: 8 (over z, x), col: 4 (over y, core).
Axes of the slice: x: 2, y: 2, z: 4, core: 2. Of those that a mesh axis runs over, the one named last changes fastest.
Arguments:
- tokens: bfloat16 [320, 8192], P('row', 'col'), may hold values from -6 to 6
- out_grad: bfloat16 [320, 8192], P('row', 'col'), may hold values from -1.5 to 1.5
- gate_saved: bfloat16 [320, 26624], P(None, 'row'), may hold values from -6 to 6
- up_saved: bfloat16 [320, 26624], P(None, 'row'), may hold values from -6 to 6
- gate_weight: bfloat16 [8192, 26624], P('col', 'row'), may hold values from -0.0625 to 0.0625
- up_weight: bfloat16 [8192, 26624], P('col', 'row'), may hold values from -0.0625 to 0.0625
- down_weight: bfloat16 [26624, 8192], P('row', 'col'), may hold values from -0.0390625 to 0.0390625
Outputs:
- input_grad: bfloat16 [320, 8192], P('row', 'col')
- gate_grad: bfloat16 [8192, 26624], P('col', 'row')
- up_grad: bfloat16 [8192, 26624], P('col', 'row')
- down_grad: bfloat16 [26624, 8192], P('row', 'col')
All inputs are finite; a program needn't handle non-finite values.
Results may differ from a plain program's by a relative error of at most 0.022.
Values may be sent and summed in bfloat16 or wider, within the bound.
No kernel may reach another device: no remote copies, remote signals or barrier semaphores. Data moves between devices by JAX's collectives and lax.ppermute only.
A program may use at most 192 MiB of HBM per device.

v0:
```python
import jax
import jax.numpy as jnp
from jax import lax
from jax.sharding import PartitionSpec as P


def swiglu_back(gate, up, grad_hidden):
    sigma = jax.nn.sigmoid(gate)
    silu_gate = gate * sigma
    hidden = (silu_gate * up).astype(jnp.bfloat16)
    grad_up = (grad_hidden * silu_gate).astype(jnp.bfloat16)
    grad_gate = (grad_hidden * up * sigma * (1.0 + gate * (1.0 - sigma))).astype(jnp.bfloat16)
    return (hidden, grad_gate, grad_up)


def on_device(tokens, out_grad, gate_saved, up_saved, gate_weight, up_weight, down_weight):
    all_tokens, all_grads = (
        lax.all_gather(tokens, "row", axis=0, tiled=True),
        lax.all_gather(out_grad, "row", axis=0, tiled=True),
    )
    hidden_part = lax.dot_general(
        all_grads, down_weight, (((1,), (1,)), ((), ())), preferred_element_type=jnp.float32
    )
    grad_hidden = lax.psum(hidden_part, "col")
    hidden, grad_gate, grad_up = swiglu_back(
        gate_saved.astype(jnp.float32), up_saved.astype(jnp.float32), grad_hidden
    )
    result = lax.dot_general(
        grad_gate, gate_weight, (((1,), (1,)), ((), ())), preferred_element_type=jnp.float32
    )
    input_grad = lax.psum_scatter(
        (
            result
            + lax.dot_general(
                grad_up, up_weight, (((1,), (1,)), ((), ())), preferred_element_type=jnp.float32
            )
        ).astype(jnp.bfloat16),
        "row",
        scatter_dimension=0,
        tiled=True,
    )
    contract_rows = (((0,), (0,)), ((), ()))
    gate_grad = lax.dot_general(
        all_tokens, grad_gate, contract_rows, preferred_element_type=jnp.float32
    )
    up_grad = lax.dot_general(
        all_tokens, grad_up, contract_rows, preferred_element_type=jnp.float32
    )
    down_grad = lax.dot_general(
        hidden, all_grads, contract_rows, preferred_element_type=jnp.float32
    )
    return (
        input_grad,
        gate_grad.astype(jnp.bfloat16),
        up_grad.astype(jnp.bfloat16),
        down_grad.astype(jnp.bfloat16),
    )


def solution(mesh):
    return jax.shard_map(
        on_device,
        mesh=mesh,
        in_specs=(
            P("row", "col"),
            P("row", "col"),
            P(None, "row"),
            P(None, "row"),
            P("col", "row"),
            P("col", "row"),
            P("row", "col"),
        ),
        out_specs=(P("row", "col"), P("col", "row"), P("col", "row"), P("row", "col")),
        check_vma=False,
    )
```

profile of v0, /device:TPU:0, one launch (start us, length us, event | category | flops | bytes accessed | tf_op | source)
XLA Modules:
  0.0 270.7 jit_solution(7870343103543569609)
XLA Ops:
  7.2 0.0 all-gather.3.cloned.1.call-start
  7.2 0.7 all-gather.3.cloned.1.call-update
  7.9 0.0 all-reduce.2.cloned.1.call-start
  7.9 47.0 %all-gather.3.cloned.1.call-done = bf16[320,2048]{1,0:T(8,128)(2,1)} async-done(((bf16[40,2048]{1,0:T(8,128)(2,1)}), bf16[320,2048]{1,0:T(8,128)(2,1)}) %all-gather.3.cloned.1.call-update) | async-done | bytes 1310736 | tf_op jit(solution)/shard_map/all_gather | solution.py:19
  55.0 11.9 %fusion.13 = f32[320,3328]{1,0:T(8,128)} fusion(bf16[320,2048]{1,0:T(8,128)(2,1)} %all-gather.3.cloned.1.call-done, bf16[3328,2048]{1,0:T(8,128)(2,1)} %param.13), kind=kOutput, calls=%fused_computation.22 | convolution fusion | flops 4362076160 | bytes 19202048 | tf_op jit(solution)/shard_map/dot_general | solution.py:21
  66.9 0.0 copy-start
  66.9 0.0 copy-start.5
  66.9 0.0 all-reduce.2.cloned.1.call-update
  66.9 0.0 all-gather.5.cloned.1.call-start
  67.0 0.7 all-gather.5.cloned.1.call-update
  67.6 0.2 reduce-scatter.2.cloned.1.call-start
  67.9 0.6 copy-done
  68.5 0.4 copy-done.5
  68.8 12.6 %convolution_convert_fusion = bf16[3328,2048]{1,0:T(8,128)(2,1)} fusion(bf16[320,2048]{1,0:T(8,128)(2,1)S(1)} %copy-done.5, bf16[320,3328]{1,0:T(8,128)(2,1)S(1)} %copy-done, bf16[320,3328]{1,0:T(8,128)(2,1)} %param.9), kind=kOutput, calls=%fused_computation | convolution fusion | flops 4377411584 | bytes 19202048 | tf_op jit(solution)/shard_map/dot_general | solution.py:49
  81.5 70.8 %all-reduce.2.cloned.1.call-done = f32[320,3328]{1,0:T(8,128)} async-done(((f32[320,3328]{1,0:T(8,128)}), f32[320,3328]{1,0:T(8,128)}) %all-reduce.2.cloned.1.call-update) | async-done | bytes 4259856 | tf_op jit(solution)/shard_map/psum | solution.py:24
  152.3 4.7 %fusion.4 = bf16[320,3328]{1,0:T(8,128)(2,1)S(1)} fusion(f32[320,3328]{1,0:T(8,128)} %all-reduce.2.cloned.1.call-done, bf16[320,3328]{1,0:T(8,128)(2,1)S(1)} %copy-done, bf16[320,3328]{1,0:T(8,128)(2,1)} %param.9), kind=kLoop, calls=%fused_computation.12 | loop fusion | flops 12779520 | bytes 10649600 | tf_op jit(solution)/shard_map/convert_element_type | solution.py:12
  157.0 0.0 copy-start.2
  157.0 1.4 copy-done.2
  158.3 0.0 copy-start.1
  158.3 9.8 %fusion.14 = f32[320,2048]{1,0:T(8,128)} fusion(bf16[320,3328]{1,0:T(8,128)(2,1)S(1)} %fusion.4, bf16[2048,3328]{1,0:T(8,128)(2,1)} %param.11), kind=kOutput, calls=%fused_computation.23 | convolution fusion | flops 4362076160 | bytes 18382848 | tf_op jit(solution)/shard_map/dot_general | solution.py:28
  168.1 0.0 copy-done.1
  168.1 12.6 %fusion.10 = bf16[320,2048]{1,0:T(8,128)(2,1)} fusion(f32[320,2048]{1,0:T(8,128)} %fusion.14, bf16[2048,3328]{1,0:T(8,128)(2,1)} %param.12, f32[320,3328]{1,0:T(8,128)} %all-reduce.2.cloned.1.call-done, bf16[320,3328]{1,0:T(8,128)(2,1)S(1)} %copy-done.1), kind=kOutput, calls=%fused_computation.20 | convolution fusion | flops 4370841600 | bytes 23953408 | tf_op jit(solution)/shard_map/dot_general | solution.py:34
  180.7 0.0 reduce-scatter.2.cloned.1.call-update
  180.7 16.2 %all-gather.5.cloned.1.call-done = bf16[320,2048]{1,0:T(8,128)(2,1)} async-done(((bf16[40,2048]{1,0:T(8,128)(2,1)}), bf16[320,2048]{1,0:T(8,128)(2,1)}) %all-gather.5.cloned.1.call-update) | async-done | bytes 1310736 | tf_op jit(solution)/shard_map/all_gather | solution.py:18
  196.9 12.5 %fusion.1 = bf16[2048,3328]{0,1:T(8,128)(2,1)} fusion(bf16[320,2048]{1,0:T(8,128)(2,1)} %all-gather.5.cloned.1.call-done, f32[320,3328]{1,0:T(8,128)} %all-reduce.2.cloned.1.call-done, bf16[320,3328]{1,0:T(8,128)(2,1)S(1)} %copy-done.1), kind=kOutput, calls=%fused_computation.4 | convolution fusion | flops 4376346624 | bytes 21331968 | tf_op jit(solution)/shard_map/dot_general | solution.py:46
  209.5 0.0 copy-start.3
  209.5 0.0 copy-start.4
  209.5 17.7 %copy.12 = bf16[2048,3328]{1,0:T(8,128)(2,1)} copy(bf16[2048,3328]{0,1:T(8,128)(2,1)} %fusion.1) | data formatting | bytes 27262976
  227.1 0.0 copy-done.3
  227.1 0.0 copy-done.4
  227.1 10.4 %fusion = bf16[2048,3328]{0,1:T(8,128)(2,1)} fusion(bf16[320,3328]{1,0:T(8,128)(2,1)S(1)} %copy-done.3, bf16[320,2048]{1,0:T(8,128)(2,1)S(1)} %copy-done.4), kind=kOutput, calls=%fused_computation.3 | convolution fusion | flops 4368891904 | bytes 17072128 | tf_op jit(solution)/shard_map/dot_general | solution.py:43
  237.6 17.5 %copy.11 = bf16[2048,3328]{1,0:T(8,128)(2,1)} copy(bf16[2048,3328]{0,1:T(8,128)(2,1)} %fusion) | data formatting | bytes 27262976
  255.0 9.1 %reduce-scatter.2.cloned.1.call-done = bf16[40,2048]{1,0:T(8,128)(2,1)} async-done(((bf16[320,2048]{1,0:T(8,128)(2,1)}), bf16[40,2048]{1,0:T(8,128)(2,1)}) %reduce-scatter.2.cloned.1.call-update) | async-done | bytes 163856 | tf_op jit(solution)/shard_map/reduce_scatter | solution.py:31
Async XLA Ops:
  7.2 47.8 %all-gather.3.cloned.1.call-start = ((), (), s32[]{:S(2)}) async-start(), calls=%async_computation.1 | async-start | bytes 1474560 | tf_op jit(solution)/shard_map/all_gather | solution.py:19
  7.9 144.4 %all-reduce.2.cloned.1.call-start = ((), (), s32[]{:S(2)}) async-start(), calls=%async_computation.2 | async-start | bytes 8519680 | tf_op jit(solution)/shard_map/psum | solution.py:24
  66.9 1.6 copy-start
  66.9 2.0 copy-start.5
  66.9 130.0 %all-gather.5.cloned.1.call-start = ((), (), s32[]{:S(2)}) async-start(), calls=%async_computation.4 | async-start | bytes 1474560 | tf_op jit(solution)/shard_map/all_gather | solution.py:18
  67.6 196.5 %reduce-scatter.2.cloned.1.call-start = ((), (), s32[]{:S(2)}) async-start(), calls=%async_computation.3 | async-start | bytes 1474560 | tf_op jit(solution)/shard_map/reduce_scatter | solution.py:31
  157.0 1.4 copy-start.2
  158.3 9.8 %copy-start.1 = (bf16[320,3328]{1,0:T(8,128)(2,1)S(1)}, bf16[320,3328]{1,0:T(8,128)(2,1)}, u32[]{:S(2)}) copy-start(bf16[320,3328]{1,0:T(8,128)(2,1)} %param.9) | copy-start | bytes 6389764
  209.5 17.7 %copy-start.3 = (bf16[320,3328]{1,0:T(8,128)(2,1)S(1)}, bf16[320,3328]{1,0:T(8,128)(2,1)}, u32[]{:S(2)}) copy-start(bf16[320,3328]{1,0:T(8,128)(2,1)} %copy-done.2) | copy-start | bytes 6389764
  209.5 17.7 %copy-start.4 = (bf16[320,2048]{1,0:T(8,128)(2,1)S(1)}, bf16[320,2048]{1,0:T(8,128)(2,1)}, u32[]{:S(2)}) copy-start(bf16[320,2048]{1,0:T(8,128)(2,1)} %all-gather.5.cloned.1.call-done) | copy-start | bytes 3932164
Sparse Core Ops, SparseCore 0:
  10.2 44.7 all-gather.2
  67.0 85.2 all-reduce.1
  154.7 42.1 all-gather.4
  201.1 62.9 reduce-scatter.1
where the time goes:
time: 272 us; the launch traced here: 271 us
  waiting for transfers between devices  145 us (53%)
  matrix products  69.8 us (26%)
  local copies, waits for them, and re-layouts  37.5 us (14%)
  between operations  13.8 us (5%)
  other arithmetic  4.66 us (2%)
    psum x1, waiting for transfers between devices, on_device(): grad_hidden = lax.psum(hidden_part, 'col')  70.8 us
    all_gather x1, waiting for transfers between devices, on_device(): lax.all_gather(out_grad, 'row', axis=0, tiled=True)  47 us
    unnamed x14, local copies, waits for them, and re-layouts  37.5 us
    all_gather x1, waiting for transfers between devices, on_device(): lax.all_gather(tokens, 'row', axis=0, tiled=True)  16.2 us
    dot_general x1, matrix products, on_device(): lax.dot_general(hidden, all_grads, contract_rows, preferred_element_type=...  12.6 us
    dot_general x1, matrix products, on_device(): lax.dot_general(grad_up, up_weight, (((1,), (1,)), ((), ())), preferred_e...  12.6 us
    dot_general x1, matrix products, on_device(): lax.dot_general(all_tokens, grad_up, contract_rows, preferred_element_typ...  12.5 us
    dot_general x1, matrix products, on_device(): lax.dot_general(all_grads, down_weight, (((1,), (1,)), ((), ())), preferr...  11.9 us
  transfers between devices with their start and end apart: 4, of which 4 were waited for; matrix products, arithmetic and copies ran while one was open for 36% of the time, Pallas kernels for 0%

commit v1 on v0

v1 whole, which is shorter than its diff:
```python
import jax
import jax.numpy as jnp
from jax import lax
from jax.experimental import pallas as pl
from jax.experimental.pallas import tpu as pltpu
from jax.sharding import PartitionSpec as P

BF = jnp.bfloat16
F32 = jnp.float32
NT = (((1,), (1,)), ((), ()))
TN = (((0,), (0,)), ((), ()))
MIB = 1 << 20


def dot(a, b, dims):
    return lax.dot_general(a, b, dims, preferred_element_type=F32)


def tile(size, most, step):
    for part in range(min(most, size) // step * step, 0, -step):
        if size % part == 0:
            return part
    return size


def call(kernel, scalars, args, in_specs, out_specs, out_shape, grid, cost, vmem):
    return pl.pallas_call(
        kernel,
        out_shape=out_shape,
        grid_spec=pltpu.PrefetchScalarGridSpec(
            num_scalar_prefetch=1, grid=grid, in_specs=in_specs, out_specs=out_specs
        ),
        compiler_params=pltpu.CompilerParams(vmem_limit_bytes=vmem * MIB),
        cost_estimate=pl.CostEstimate(flops=cost[0], bytes_accessed=cost[1], transcendentals=0),
    )(scalars, *args)


def whole(shape):
    return pl.BlockSpec(tuple(shape), lambda *_: (0,) * len(shape))


def struct(shape, dtype=BF):
    return jax.ShapeDtypeStruct(tuple(shape), dtype)


def factors(scalars, gate, up):
    blocks, rows, width = gate.shape
    half = blocks // 2

    def kernel(_, gate_ref, up_ref, hidden_ref, silu_ref, slope_ref):
        g = gate_ref[...].astype(F32)
        u = up_ref[...].astype(F32)
        sig = 1.0 / (1.0 + jnp.exp(-g))
        silu = g * sig
        hidden_ref[...] = (silu * u).astype(BF)

        @pl.when(pl.program_id(0) < half)
        def _():
            silu_ref[...] = silu
            slope_ref[...] = u * sig * (1.0 + g * (1.0 - sig))

    block = (1, rows, width)
    pick = pl.BlockSpec(block, lambda i, s: (s[i], 0, 0))
    moved = pl.BlockSpec(block, lambda i, s: (lax.rem(i + s[blocks], blocks), 0, 0))
    mine = pl.BlockSpec(block, lambda i, s: (jnp.minimum(i, half - 1), 0, 0))
    return call(
        kernel, scalars, (gate, up), [pick, pick], [moved, mine, mine],
        [struct(gate.shape), struct((half, rows, width), F32), struct((half, rows, width), F32)],
        (blocks,), (10 * gate.size, 10 * gate.size), 24,
    )


def hidden_part(core, grads, weight, first, width):
    tokens, depth = grads.shape
    half = tokens // 2

    def kernel(core_ref, grads_ref, weight_ref, mine_ref, other_ref):
        total = dot(grads_ref[...], weight_ref[first : first + width], NT)
        is_first = core_ref[0] == 0
        mine_ref[...] = jnp.where(is_first, total[:half], total[half:])
        other_ref[...] = jnp.where(is_first, total[half:], total[:half]).astype(BF)

    return call(
        kernel, core, (grads, weight),
        [pl.BlockSpec(memory_space=pltpu.VMEM), pl.BlockSpec(memory_space=pltpu.VMEM)],
        [pl.BlockSpec(memory_space=pltpu.VMEM), pl.BlockSpec(memory_space=pltpu.VMEM)],
        [struct((half, width), F32), struct((half, width))],
        (), (2 * tokens * depth * width, 2 * depth * width), 40,
    )


def input_part(core, grads, gate_weight, up_weight, first, width, by_halves):
    half = grads[0][0].shape[1]
    units = gate_weight.shape[1]
    block = tile(width, 256, 128)
    n = len(grads)

    def kernel(core_ref, *refs):
        ins, (gate_ref, up_ref), (keep_ref, send_ref) = refs[: 2 * n], refs[2 * n : 2 * n + 2], refs[2 * n + 2 :]
        is_first = core_ref[0] == 0
        total = None
        at = 0
        for k in range(n):
            mine_ref, other_ref = ins[2 * k : 2 * k + 2]
            size = mine_ref.shape[2]
            for which, weight_ref in ((0, gate_ref), (1, up_ref)):
                both = jnp.concatenate([mine_ref[which], other_ref[which]], axis=0)
                part = dot(both, weight_ref[:, at : at + size], NT)
                total = part if total is None else total + part
            at += size
        low = jnp.where(is_first, total[:half], total[half:]).astype(BF)
        high = jnp.where(is_first, total[half:], total[:half]).astype(BF)
        if by_halves:
            keep_ref[0], send_ref[0] = low[: half // 2], low[half // 2 :]
            keep_ref[1], send_ref[1] = high[: half // 2], high[half // 2 :]
        else:
            keep_ref[...], send_ref[...] = low, high

    weight_spec = pl.BlockSpec((block, units), lambda i, core: (first // block + i, 0))
    shape = (2, half // 2, width) if by_halves else (half, width)
    out_block = shape[:-1] + (block,)
    out_spec = pl.BlockSpec(out_block, lambda i, core: (0,) * (len(shape) - 1) + (i,))
    return call(
        kernel, core, [a for pair in grads for a in pair] + [gate_weight, up_weight],
        [whole(a.shape) for pair in grads for a in pair] + [weight_spec, weight_spec],
        [out_spec, out_spec], [struct(shape), struct(shape)],
        (width // block,), (8 * half * units * width, 4 * units * width), 40,
    )


def weight_grads(order, tokens, grads):
    blocks, rows, features = tokens.shape
    half = grads[0][0].shape[1]
    units = sum(mine.shape[2] for mine, _ in grads)
    block = tile(features, 512, 128)
    n = len(grads)

    def kernel(order_ref, tokens_ref, *refs):
        ins, outs = refs[: 2 * n], refs[2 * n :]
        left = jnp.concatenate([tokens_ref[order_ref[i]] for i in range(blocks)], axis=0)
        at = 0
        for k in range(n):
            mine_ref, other_ref = ins[2 * k : 2 * k + 2]
            size = mine_ref.shape[2]
            for which in range(2):
                both = jnp.concatenate([mine_ref[which], other_ref[which]], axis=0)
                outs[which][:, at : at + size] = dot(left, both, TN).astype(BF)
            at += size

    out_spec = pl.BlockSpec((block, units), lambda i, order: (i, 0))
    return call(
        kernel, order, [tokens] + [a for pair in grads for a in pair],
        [pl.BlockSpec((blocks, rows, block), lambda i, order: (0, 0, i))] + [whole(a.shape) for pair in grads for a in pair],
        [out_spec, out_spec], [struct((features, units)), struct((features, units))],
        (features // block,), (8 * half * units * features, 4 * units * features), 48,
    )


def down_grads(hidden, grads):
    tokens, units = hidden.shape
    features = grads.shape[1]
    block = tile(units, 256, 128)

    def kernel(_, hidden_ref, grads_ref, out_ref):
        out_ref[...] = dot(hidden_ref[...], grads_ref[...], TN).astype(BF)

    return call(
        kernel, jnp.zeros((1,), jnp.int32), (hidden, grads),
        [pl.BlockSpec((tokens, block), lambda i, _: (0, i)), whole(grads.shape)],
        pl.BlockSpec((block, features), lambda i, _: (i, 0)), struct((units, features)),
        (units // block,), (2 * tokens * units * features, 2 * units * features), 32,
    )


def on_device(n_row, n_col, tokens, out_grad, gate_saved, up_saved, gate_weight, up_weight, down_weight):
    rows, features = tokens.shape
    units = gate_saved.shape[1]
    row = lax.axis_index("row").astype(jnp.int32)
    core = (lax.axis_index("col") % 2).astype(jnp.int32)
    core_arg = core.reshape(1)

    def swap(x, mask, axis="row"):
        n = n_row if axis == "row" else n_col
        return lax.ppermute(x, axis, [(i, i ^ mask) for i in range(n)])

    masks = []
    m = n_row // 2
    while m > 1:
        masks.append(m)
        m //= 2
    codes = [0]
    for m in masks:
        codes += [i ^ m for i in codes]
    order = jnp.array(codes + [i ^ 1 for i in codes], jnp.int32) ^ row
    order_mine = order ^ core

    held, swapped = [out_grad], [swap(out_grad, 1)]
    for m in masks:
        got = swap(jnp.concatenate(held, axis=0) if len(held) > 1 else held[0], m)
        held.append(got)
        swapped.append(swap(got, 1))
    all_grads = jnp.concatenate(held + swapped, axis=0)

    hidden, silu, slope = factors(
        jnp.concatenate([order_mine, core_arg * (n_row // 2)]),
        gate_saved.reshape(n_row, rows, units), up_saved.reshape(n_row, rows, units),
    )
    hidden = hidden.reshape(n_row * rows, units)
    half = n_row * rows // 2
    silu, slope = silu.reshape(half, units), slope.reshape(half, units)

    all_grads, later = lax.optimization_barrier((all_grads, tokens))
    all_tokens = lax.all_gather(later, "row", axis=0, tiled=True).reshape(n_row, rows, features)

    parts = 2 if (units // 2) % 128 == 0 else 1
    width = units // parts
    partial = [hidden_part(core_arg, all_grads, down_weight, k * width, width) for k in range(parts)]
    grads = []
    for k, (mine, other) in enumerate(partial):
        total = mine + swap(other, 1, "col").astype(F32)
        m = 2
        while m < n_col:
            total = total + swap(total.astype(BF), m, "col").astype(F32)
            m *= 2
        at = slice(k * width, (k + 1) * width)
        pair = jnp.stack([(total * slope[:, at]).astype(BF), (total * silu[:, at]).astype(BF)])
        grads.append((pair, swap(pair, 1, "col")))

    down_grad = down_grads(hidden, all_grads)

    wide = features // 2
    keep, send = input_part(core_arg, grads, gate_weight, up_weight, 0, wide, False)
    keep2, send2 = input_part(core_arg, grads, gate_weight, up_weight, wide, wide, True)
    left = keep + swap(send, 1)
    right = keep2 + swap(send2, masks[-1])
    n = left.shape[0] // 2
    left = left[:n] + swap(left[n:], masks[-1])
    right = right[0] + swap(right[1], 1)
    total = jnp.concatenate([left, right], axis=1)
    for m in masks[-2::-1]:
        n = total.shape[0] // 2
        total = total[:n] + swap(total[n:], m)

    gate_grad, up_grad = weight_grads(order_mine, all_tokens, grads)
    return total, gate_grad, up_grad, down_grad


def solution(mesh):
    n_row, n_col = mesh.shape["row"], mesh.shape["col"]
    return jax.shard_map(
        lambda *args: on_device(n_row, n_col, *args),
        mesh=mesh,
        in_specs=(
            P("row", "col"),
            P("row", "col"),
            P(None, "row"),
            P(None, "row"),
            P("col", "row"),
            P("col", "row"),
            P("row", "col"),
        ),
        out_specs=(P("row", "col"), P("col", "row"), P("col", "row"), P("row", "col")),
        check_vma=False,
    )
```

time: 272 us -> 164 us (0.60)
  waiting for transfers between devices: 145 us -> 47.6 us
  matrix products: 69.8 us -> 0 us
  Pallas kernels: 0 us -> 67.4 us
  local copies, waits for them, and re-layouts: 37.5 us -> 6.9 us
  starting transfers between devices: 0.34 us -> 21.8 us
    psum x1 -> x0, waiting for transfers between devices: 70.8 us -> none  [on_device(): grad_hidden = lax.psum(hidden_part, 'col')]
    dot_general x6 -> x0, matrix products: 69.8 us -> none  [the longest x1 12.6 us: on_device(): lax.dot_general(hidden, all_grads, contract_rows, preferred_element_type=...]
    pallas_call x0 -> x7, Pallas kernels: none -> 67.4 us  [call(): pl.pallas_call(kernel, out_shape=out_shape, grid_spec=pltpu.PrefetchScala...]
    all_gather x2 -> x1, waiting for transfers between devices: 63.3 us -> 0.01 us  [on_device(): lax.all_gather(later, 'row', axis=0, tiled=True)]
    ppermute x0 -> x16, waiting for transfers between devices: none -> 47.6 us  [swap(): return lax.ppermute(x, axis, [(i, i ^ mask) for i in range(n)])]
    unnamed x14 -> x25, local copies, waits for them, and re-layouts: 37.5 us -> 6.85 us
    ppermute x0 -> x16, starting transfers between devices: none -> 21.7 us  [swap(): return lax.ppermute(x, axis, [(i, i ^ mask) for i in range(n)])]
    reduce_scatter x1 -> x0, waiting for transfers between devices: 9.13 us -> none  [on_device(): lax.psum_scatter((result + lax.dot_general(grad_up, up_weight, (((1,), (1...]
  transfers between devices with their start and end apart: 4 -> 17, of which waited for: 4 -> 9; matrix products, arithmetic and copies ran while one was open for 36% -> 3% of each run, Pallas kernels for 0% -> 37%
where the time goes in v1:
time: 164 us
  Pallas kernels  67.4 us (41%)
  waiting for transfers between devices  47.6 us (29%)
  starting transfers between devices  21.8 us (13%)
  between operations  14.3 us (9%)
  local copies, waits for them, and re-layouts  6.9 us (4%)
  other arithmetic  6.12 us (4%)
    pallas_call x7, Pallas kernels, call(): pl.pallas_call(kernel, out_shape=out_shape, grid_spec=pltpu.PrefetchScala...  67.4 us
    ppermute x16, waiting for transfers between devices, swap(): return lax.ppermute(x, axis, [(i, i ^ mask) for i in range(n)])  47.6 us
    ppermute x16, starting transfers between devices, swap(): return lax.ppermute(x, axis, [(i, i ^ mask) for i in range(n)])  21.7 us
    unnamed x25, local copies, waits for them, and re-layouts  6.85 us
  transfers between devices with their start and end apart: 17, of which 9 were waited for; matrix products, arithmetic and copies ran while one was open for 3% of the time, Pallas kernels for 37%

profile of v1, /device:TPU:0, one launch (start us, length us, event | category | flops | bytes accessed | tf_op | source)
XLA Modules:
  0.0 164.0 jit_solution(14941403956780664658)
XLA Ops:
  7.2 0.0 all-gather.2.cloned.1.call-start
  7.2 4.1 %collective-permute-start = (bf16[40,2048]{1,0:T(8,128)(2,1)}, bf16[40,2048]{1,0:T(8,128)(2,1)S(1)}, u32[]{:S(2)}, u32[]{:S(2)}) collective-permute-start(bf16[40,2048]{1,0:T(8,128)(2,1)} %param.9), channel_id=1, source_target_pairs={{0,16},{4,20},{8,24},{12,28},{16,0},{20,4},{24,8},{28,12},{1,17},{... | collective-permute-start | bytes 491528 | tf_op jit(solution)/shard_map/ppermute | solution.py:184
  11.3 1.5 collective-permute-start.2
  12.8 6.4 %collective-permute-done = bf16[40,2048]{1,0:T(8,128)(2,1)S(1)} collective-permute-done((bf16[40,2048]{1,0:T(8,128)(2,1)}, bf16[40,2048]{1,0:T(8,128)(2,1)S(1)}, u32[]{:S(2)}, u32[]{:S(2)}) %collective-permute-start) | collective-permute-done | bytes 163872 | tf_op jit(solution)/shard_map/ppermute | solution.py:184
  19.2 0.9 pad_maximum_fusion.2
  20.2 0.9 collective-permute-start.1
  21.1 0.9 constant_dynamic-update-slice_fusion.5
  22.0 1.6 collective-permute-start.3
  23.6 5.6 %collective-permute-done.1 = bf16[80,2048]{1,0:T(8,128)(2,1)S(1)} collective-permute-done((bf16[80,2048]{1,0:T(8,128)(2,1)S(1)}, bf16[80,2048]{1,0:T(8,128)(2,1)S(1)}, u32[]{:S(2)}, u32[]{:S(2)}) %collective-permute-start.1) | collective-permute-done | bytes 327712 | tf_op jit(solution)/shard_map/ppermute | solution.py:184
  29.1 1.3 collective-permute-start.4
  30.5 0.0 collective-permute-done.2
  30.5 0.0 collective-permute-done.3
  30.5 6.6 %collective-permute-done.4 = bf16[80,2048]{1,0:T(8,128)(2,1)S(1)} collective-permute-done((bf16[80,2048]{1,0:T(8,128)(2,1)S(1)}, bf16[80,2048]{1,0:T(8,128)(2,1)S(1)}, u32[]{:S(2)}, u32[]{:S(2)}) %collective-permute-start.4) | collective-permute-done | bytes 327712 | tf_op jit(solution)/shard_map/ppermute | solution.py:184
  37.1 7.4 %shard_map.111 = (f32[160,1664]{1,0:T(8,128)S(1)}, bf16[160,1664]{1,0:T(8,128)(2,1)S(1)}) custom-call(s32[1]{0:T(128)} %bitcast.core_ref, bf16[320,2048]{1,0:T(8,128)(2,1)S(1)} %constant_dynamic-update-slice_fusion.grads_ref, bf16[3328,2048]{1,0:T(8,128)(2,1)} %weight_ref.3), custom_call_target="tpu_custom_call" | custom-call | flops 2181038080 | bytes 6815744 | tf_op jit(solution)/shard_map/pallas_call | solution.py:27
  44.6 0.1 collective-permute-start.5
  44.7 7.4 %shard_map.113 = (f32[160,1664]{1,0:T(8,128)S(1)}, bf16[160,1664]{1,0:T(8,128)(2,1)S(1)}) custom-call(s32[1]{0:T(128)} %bitcast.core_ref, bf16[320,2048]{1,0:T(8,128)(2,1)S(1)} %constant_dynamic-update-slice_fusion.grads_ref, bf16[3328,2048]{1,0:T(8,128)(2,1)} %weight_ref.3), custom_call_target="tpu_custom_call" | custom-call | flops 2181038080 | bytes 6815744 | tf_op jit(solution)/shard_map/pallas_call | solution.py:27
  52.1 0.6 collective-permute-start.8
  52.7 0.0 collective-permute-done.5
  52.7 1.0 fusion.4
  53.7 0.0 copy-done.5
  53.7 1.4 collective-permute-start.6
  55.1 0.0 collective-permute-done.8
  55.1 1.0 fusion.5
  56.1 0.0 copy-done.7
  56.1 0.6 collective-permute-start.9
  56.7 0.0 copy-done.9
  56.7 0.1 pad_add_fusion._
  56.8 1.6 copy-done.2
  58.4 1.6 copy-done.3
  60.0 2.8 %shard_map.112 = (bf16[8,40,3328]{2,1,0:T(8,128)(2,1)S(1)}, f32[4,40,3328]{2,1,0:T(8,128)S(1)}, f32[4,40,3328]{2,1,0:T(8,128)S(1)}) custom-call(s32[9]{0:T(128)S(1)} %pad_add_fusion._, bf16[8,40,3328]{2,1,0:T(8,128)(2,1)S(1)} %bitcast.22, bf16[8,40,3328]{2,1,0:T(8,128)(2,1)S(1)} %bitcast.23), custom_call_target="tpu_custom_call" | custom-call | flops 10649600 | bytes 10649600 | tf_op jit(solution)/shard_map/pallas_call | solution.py:27
  62.8 0.0 copy-start
  62.8 1.3 copy-done
  64.1 4.8 %collective-permute-done.6 = bf16[160,1664]{1,0:T(8,128)(2,1)} collective-permute-done((bf16[160,1664]{1,0:T(8,128)(2,1)}, bf16[160,1664]{1,0:T(8,128)(2,1)}, u32[]{:S(2)}, u32[]{:S(2)}) %collective-permute-start.6) | collective-permute-done | bytes 532512 | tf_op jit(solution)/shard_map/ppermute | solution.py:184
  69.0 10.5 %collective-permute-done.9 = bf16[160,1664]{1,0:T(8,128)(2,1)} collective-permute-done((bf16[160,1664]{1,0:T(8,128)(2,1)}, bf16[160,1664]{1,0:T(8,128)(2,1)}, u32[]{:S(2)}, u32[]{:S(2)}) %collective-permute-start.9) | collective-permute-done | bytes 532512 | tf_op jit(solution)/shard_map/ppermute | solution.py:184
  79.4 0.0 copy-done.6
  79.4 0.0 copy-done.8
  79.4 2.0 %fusion.8 = (bf16[1,160,1664]{2,1,0:T(8,128)(2,1)S(1)}, bf16[1,160,1664]{2,1,0:T(8,128)(2,1)S(1)}, bf16[1,160,1664]{2,1,0:T(8,128)(2,1)S(1)}, bf16[1,160,1664]{2,1,0:T(8,128)(2,1)S(1)}) fusion(f32[160,3328]{1,0:T(8,128)S(1)} %bitcast.25, bf16[160,1664]{1,0:T(8,128)(2,1)} %collective-permute-done.9, f32[160,1664]{1,0:T(8,128)S(1)} %get-tuple-element.24, ...), kind=kLoop, calls=%fused_computation.18 | loop fusion | flops 4259840 | bytes 10649600 | tf_op jit(solution)/shard_map/stack | solution.py:226
  81.4 0.1 pad_maximum_fusion.1.refs_2_
  81.5 0.1 collective-permute-start.10
  81.6 0.1 pad_maximum_fusion.refs_0_
  81.7 0.6 collective-permute-start.7
  82.3 0.0 all-gather.2.cloned.1.call-update
  82.3 2.1 %collective-permute-done.10.refs_3_ = bf16[2,160,1664]{2,1,0:T(8,128)(2,1)} collective-permute-done((bf16[2,160,1664]{2,1,0:T(8,128)(2,1)S(1)}, bf16[2,160,1664]{2,1,0:T(8,128)(2,1)}, u32[]{:S(2)}, u32[]{:S(2)}) %collective-permute-start.10) | collective-permute-done | bytes 1064992 | tf_op jit(solution)/shard_map/ppermute | solution.py:184
  84.4 1.5 collective-permute-done.7.refs_1_
  85.9 8.9 %shard_map.114 = (bf16[160,1024]{1,0:T(8,128)(2,1)S(1)}, bf16[160,1024]{1,0:T(8,128)(2,1)S(1)}) custom-call(s32[1]{0:T(128)} %bitcast.core_ref, bf16[2,160,1664]{2,1,0:T(8,128)(2,1)S(1)} %pad_maximum_fusion.refs_0_, bf16[2,160,1664]{2,1,0:T(8,128)(2,1)} %collective-permute-done.7.refs_1_, bf16[2,160,1664]{2,1,0:T(8,128)(2,1)S(1)} %pad_maximum_fusion.1.refs_2_, ...), custom_call_target="tpu_custom_call" | custom-call | flops 4362076160 | bytes 13631488 | tf_op jit(solution)/shard_map/pallas_call | solution.py:27
  94.9 0.0 copy-start.1
  94.9 1.4 collective-permute-start.11
  96.3 8.9 %shard_map.115 = (bf16[2,80,1024]{2,1,0:T(8,128)(2,1)S(1)}, bf16[2,80,1024]{2,1,0:T(8,128)(2,1)S(1)}) custom-call(s32[1]{0:T(128)} %bitcast.core_ref, bf16[2,160,1664]{2,1,0:T(8,128)(2,1)S(1)} %pad_maximum_fusion.refs_0_, bf16[2,160,1664]{2,1,0:T(8,128)(2,1)} %collective-permute-done.7.refs_1_, bf16[2,160,1664]{2,1,0:T(8,128)(2,1)S(1)} %pad_maximum_fusion.1.refs_2_, ...), custom_call_target="tpu_custom_call" | custom-call | flops 4362076160 | bytes 13631488 | tf_op jit(solution)/shard_map/pallas_call | solution.py:27
  105.2 2.6 %collective-permute-start.13 = (bf16[2,80,1024]{2,1,0:T(8,128)(2,1)S(1)}, bf16[2,80,1024]{2,1,0:T(8,128)(2,1)S(1)}, u32[]{:S(2)}, u32[]{:S(2)}) collective-permute-start(bf16[2,80,1024]{2,1,0:T(8,128)(2,1)S(1)} %get-tuple-element.29), channel_id=1, source_target_pairs={{0,8},{4,12},{8,0},{12,4},{16,24},{20,28},{24,16},{28,20},{1,9},{5... | collective-permute-start | bytes 983048 | tf_op jit(solution)/shard_map/ppermute | solution.py:184
  107.8 0.0 copy-done.1
  107.8 12.0 %shard_map.117 = bf16[3328,2048]{1,0:T(8,128)(2,1)} custom-call(s32[1]{0:T(128)} %constant.27.clone.1._, bf16[320,3328]{1,0:T(8,128)(2,1)S(1)} %bitcast.21, bf16[320,2048]{1,0:T(8,128)(2,1)S(1)} %constant_dynamic-update-slice_fusion.grads_ref), custom_call_target="tpu_custom_call" | custom-call | flops 4362076160 | bytes 13631488 | tf_op jit(solution)/shard_map/pallas_call | solution.py:27
  119.8 0.0 collective-permute-done.11
  119.8 0.1 add.36
  120.0 0.1 collective-permute-start.12
  120.1 0.5 collective-permute-done.13
  120.6 0.1 add.38
  120.7 0.1 collective-permute-start.14
  120.8 9.5 %collective-permute-done.12 = bf16[80,1024]{1,0:T(8,128)(2,1)S(1)} collective-permute-done((bf16[80,1024]{1,0:T(8,128)(2,1)S(1)}, bf16[80,1024]{1,0:T(8,128)(2,1)S(1)}, u32[]{:S(2)}, u32[]{:S(2)}) %collective-permute-start.12) | collective-permute-done | bytes 163872 | tf_op jit(solution)/shard_map/ppermute | solution.py:184
  130.3 0.0 collective-permute-done.14
  130.4 4.9 %collective-permute-start.15 = (bf16[40,2048]{1,0:T(8,128)(2,1)S(1)}, bf16[40,2048]{1,0:T(8,128)(2,1)S(1)}, u32[]{:S(2)}, u32[]{:S(2)}) collective-permute-start(bf16[40,2048]{1,0:T(8,128)(2,1)S(1)} %pad_maximum_fusion.3), channel_id=1, source_target_pairs={{0,16},{4,20},{8,24},{12,28},{16,0},{20,4},{24,8},{28,12},{1,17},{... | collective-permute-start | bytes 491528 | tf_op jit(solution)/shard_map/ppermute | solution.py:184
  135.3 1.3 copy-done.4
  136.7 19.8 %shard_map.116 = (bf16[2048,3328]{1,0:T(8,128)(2,1)}, bf16[2048,3328]{1,0:T(8,128)(2,1)}) custom-call(s32[8]{0:T(128)S(1)} %xor_xor_fusion.order_ref, bf16[8,40,2048]{2,1,0:T(8,128)(2,1)S(1)} %bitcast.26, bf16[2,160,1664]{2,1,0:T(8,128)(2,1)S(1)} %pad_maximum_fusion.refs_0_, bf16[2,160,1664]{2,1,0:T(8,128)(2,1)} %collective-permute-done.7.refs_1_, ...), custom_call_target="tpu_custom_call" | custom-call | flops 8724152320 | bytes 27262976 | tf_op jit(solution)/shard_map/pallas_call | solution.py:27
  156.4 0.0 collective-permute-done.15
  156.4 0.7 fusion.11
  (20 shorter events, 0.2 us)
Async XLA Ops:
  7.2 128.2 %all-gather.2.cloned.1.call-start = ((), (), s32[]{:S(2)}) async-start(), calls=%async_computation | async-start | bytes 1474560 | tf_op jit(solution)/shard_map/all_gather | solution.py:213
  7.2 12.0 %collective-permute-start = (bf16[40,2048]{1,0:T(8,128)(2,1)}, bf16[40,2048]{1,0:T(8,128)(2,1)S(1)}, u32[]{:S(2)}, u32[]{:S(2)}) collective-permute-start(bf16[40,2048]{1,0:T(8,128)(2,1)} %param.9), channel_id=1, source_target_pairs={{0,16},{4,20},{8,24},{12,28},{16,0},{20,4},{24,8},{28,12},{1,17},{... | collective-permute-start | bytes 491528 | tf_op jit(solution)/shard_map/ppermute | solution.py:184
  11.3 19.2 %collective-permute-start.2 = (bf16[40,2048]{1,0:T(8,128)(2,1)}, bf16[40,2048]{1,0:T(8,128)(2,1)S(1)}, u32[]{:S(2)}, u32[]{:S(2)}) collective-permute-start(bf16[40,2048]{1,0:T(8,128)(2,1)} %param.9), channel_id=1, source_target_pairs={{0,4},{4,0},{8,12},{12,8},{16,20},{20,16},{24,28},{28,24},{1,5},{5... | collective-permute-start | bytes 491528 | tf_op jit(solution)/shard_map/ppermute | solution.py:184
  20.2 9.0 %collective-permute-start.1 = (bf16[80,2048]{1,0:T(8,128)(2,1)S(1)}, bf16[80,2048]{1,0:T(8,128)(2,1)S(1)}, u32[]{:S(2)}, u32[]{:S(2)}) collective-permute-start(bf16[80,2048]{1,0:T(8,128)(2,1)S(1)} %pad_maximum_fusion.2), channel_id=1, source_target_pairs={{0,8},{4,12},{8,0},{12,4},{16,24},{20,28},{24,16},{28,20},{1,9},{5... | collective-permute-start | bytes 983048 | tf_op jit(solution)/shard_map/ppermute | solution.py:184
  22.0 8.5 %collective-permute-start.3 = (bf16[40,2048]{1,0:T(8,128)(2,1)S(1)}, bf16[40,2048]{1,0:T(8,128)(2,1)S(1)}, u32[]{:S(2)}, u32[]{:S(2)}) collective-permute-start(bf16[40,2048]{1,0:T(8,128)(2,1)S(1)} %collective-permute-done), channel_id=1, source_target_pairs={{0,4},{4,0},{8,12},{12,8},{16,20},{20,16},{24,28},{28,24},{1,5},{5... | collective-permute-start | bytes 491528 | tf_op jit(solution)/shard_map/ppermute | solution.py:184
  29.1 8.0 %collective-permute-start.4 = (bf16[80,2048]{1,0:T(8,128)(2,1)S(1)}, bf16[80,2048]{1,0:T(8,128)(2,1)S(1)}, u32[]{:S(2)}, u32[]{:S(2)}) collective-permute-start(bf16[80,2048]{1,0:T(8,128)(2,1)S(1)} %collective-permute-done.1), channel_id=1, source_target_pairs={{0,4},{4,0},{8,12},{12,8},{16,20},{20,16},{24,28},{28,24},{1,5},{5... | collective-permute-start | bytes 983048 | tf_op jit(solution)/shard_map/ppermute | solution.py:184
  44.6 8.1 %collective-permute-start.5 = (bf16[160,1664]{1,0:T(8,128)(2,1)S(1)}, bf16[160,1664]{1,0:T(8,128)(2,1)S(1)}, u32[]{:S(2)}, u32[]{:S(2)}) collective-permute-start(bf16[160,1664]{1,0:T(8,128)(2,1)S(1)} %get-tuple-element.21), channel_id=1, source_target_pairs={{0,1},{1,0},{2,3},{3,2},{4,5},{5,4},{6,7},{7,6},{8,9},{9,8},{10,11... | collective-permute-start | bytes 1597448 | tf_op jit(solution)/shard_map/ppermute | solution.py:184
  52.1 3.0 %collective-permute-start.8 = (bf16[160,1664]{1,0:T(8,128)(2,1)S(1)}, bf16[160,1664]{1,0:T(8,128)(2,1)S(1)}, u32[]{:S(2)}, u32[]{:S(2)}) collective-permute-start(bf16[160,1664]{1,0:T(8,128)(2,1)S(1)} %get-tuple-element.25), channel_id=1, source_target_pairs={{0,1},{1,0},{2,3},{3,2},{4,5},{5,4},{6,7},{7,6},{8,9},{9,8},{10,11... | collective-permute-start | bytes 1597448 | tf_op jit(solution)/shard_map/ppermute | solution.py:184
  52.7 1.0 copy-start.5
  53.7 15.3 %collective-permute-start.6 = (bf16[160,1664]{1,0:T(8,128)(2,1)}, bf16[160,1664]{1,0:T(8,128)(2,1)}, u32[]{:S(2)}, u32[]{:S(2)}) collective-permute-start(bf16[160,1664]{1,0:T(8,128)(2,1)} %fusion.4), channel_id=1, source_target_pairs={{0,2},{1,3},{2,0},{3,1},{4,6},{5,7},{6,4},{7,5},{8,10},{9,11},{10,... | collective-permute-start | bytes 1597448 | tf_op jit(solution)/shard_map/ppermute | solution.py:184
  55.1 1.0 copy-start.7
  55.1 1.6 copy-start.9
  56.1 23.4 %collective-permute-start.9 = (bf16[160,1664]{1,0:T(8,128)(2,1)}, bf16[160,1664]{1,0:T(8,128)(2,1)}, u32[]{:S(2)}, u32[]{:S(2)}) collective-permute-start(bf16[160,1664]{1,0:T(8,128)(2,1)} %fusion.5), channel_id=1, source_target_pairs={{0,2},{1,3},{2,0},{3,1},{4,6},{5,7},{6,4},{7,5},{8,10},{9,11},{10,... | collective-permute-start | bytes 1597448 | tf_op jit(solution)/shard_map/ppermute | solution.py:184
  56.8 1.6 copy-start.2
  58.4 1.6 copy-start.3
  60.0 19.5 %copy-start.6 = (bf16[160,1664]{1,0:T(8,128)(2,1)S(1)}, bf16[160,1664]{1,0:T(8,128)(2,1)}, u32[]{:S(2)}) copy-start(bf16[160,1664]{1,0:T(8,128)(2,1)} %copy-done.5) | copy-start | bytes 1597444
  60.0 19.5 %copy-start.8 = (bf16[160,1664]{1,0:T(8,128)(2,1)S(1)}, bf16[160,1664]{1,0:T(8,128)(2,1)}, u32[]{:S(2)}) copy-start(bf16[160,1664]{1,0:T(8,128)(2,1)} %copy-done.7) | copy-start | bytes 1597444
  62.8 1.3 copy-start
  81.5 2.9 %collective-permute-start.10 = (bf16[2,160,1664]{2,1,0:T(8,128)(2,1)S(1)}, bf16[2,160,1664]{2,1,0:T(8,128)(2,1)}, u32[]{:S(2)}, u32[]{:S(2)}) collective-permute-start(bf16[2,160,1664]{2,1,0:T(8,128)(2,1)S(1)} %pad_maximum_fusion.1.refs_2_), channel_id=1, source_target_pairs={{0,1},{1,0},{2,3},{3,2},{4,5},{5,4},{6,7},{7,6},{8,9},{9,8},{10,11... | collective-permute-start | bytes 3194888 | tf_op jit(solution)/shard_map/ppermute | solution.py:184
  81.7 4.2 %collective-permute-start.7 = (bf16[2,160,1664]{2,1,0:T(8,128)(2,1)S(1)}, bf16[2,160,1664]{2,1,0:T(8,128)(2,1)}, u32[]{:S(2)}, u32[]{:S(2)}) collective-permute-start(bf16[2,160,1664]{2,1,0:T(8,128)(2,1)S(1)} %pad_maximum_fusion.refs_0_), channel_id=1, source_target_pairs={{0,1},{1,0},{2,3},{3,2},{4,5},{5,4},{6,7},{7,6},{8,9},{9,8},{10,11... | collective-permute-start | bytes 3194888 | tf_op jit(solution)/shard_map/ppermute | solution.py:184
  94.9 12.9 %copy-start.1 = (bf16[8,40,3328]{2,1,0:T(8,128)(2,1)S(1)}, bf16[8,40,3328]{2,1,0:T(8,128)(2,1)}, u32[]{:S(2)}) copy-start(bf16[8,40,3328]{2,1,0:T(8,128)(2,1)} %copy-done) | copy-start | bytes 6389764
  94.9 24.9 %collective-permute-start.11 = (bf16[160,1024]{1,0:T(8,128)(2,1)S(1)}, bf16[160,1024]{1,0:T(8,128)(2,1)S(1)}, u32[]{:S(2)}, u32[]{:S(2)}) collective-permute-start(bf16[160,1024]{1,0:T(8,128)(2,1)S(1)} %get-tuple-element.27), channel_id=1, source_target_pairs={{0,4},{4,0},{8,12},{12,8},{16,20},{20,16},{24,28},{28,24},{1,5},{5... | collective-permute-start | bytes 983048 | tf_op jit(solution)/shard_map/ppermute | solution.py:184
  105.2 15.4 %collective-permute-start.13 = (bf16[2,80,1024]{2,1,0:T(8,128)(2,1)S(1)}, bf16[2,80,1024]{2,1,0:T(8,128)(2,1)S(1)}, u32[]{:S(2)}, u32[]{:S(2)}) collective-permute-start(bf16[2,80,1024]{2,1,0:T(8,128)(2,1)S(1)} %get-tuple-element.29), channel_id=1, source_target_pairs={{0,8},{4,12},{8,0},{12,4},{16,24},{20,28},{24,16},{28,20},{1,9},{5... | collective-permute-start | bytes 983048 | tf_op jit(solution)/shard_map/ppermute | solution.py:184
  120.0 10.4 %collective-permute-start.12 = (bf16[80,1024]{1,0:T(8,128)(2,1)S(1)}, bf16[80,1024]{1,0:T(8,128)(2,1)S(1)}, u32[]{:S(2)}, u32[]{:S(2)}) collective-permute-start(bf16[80,1024]{1,0:T(8,128)(2,1)S(1)} %slice.45), channel_id=1, source_target_pairs={{0,8},{4,12},{8,0},{12,4},{16,24},{20,28},{24,16},{28,20},{1,9},{5... | collective-permute-start | bytes 491528 | tf_op jit(solution)/shard_map/ppermute | solution.py:184
  120.7 9.6 %collective-permute-start.14 = (bf16[80,1024]{1,0:T(8,128)(2,1)S(1)}, bf16[80,1024]{1,0:T(8,128)(2,1)S(1)}, u32[]{:S(2)}, u32[]{:S(2)}) collective-permute-start(bf16[80,1024]{1,0:T(8,128)(2,1)S(1)} %slice_bitcast_fusion), channel_id=1, source_target_pairs={{0,4},{4,0},{8,12},{12,8},{16,20},{20,16},{24,28},{28,24},{1,5},{5... | collective-permute-start | bytes 491528 | tf_op jit(solution)/shard_map/ppermute | solution.py:184
  130.4 26.0 %collective-permute-start.15 = (bf16[40,2048]{1,0:T(8,128)(2,1)S(1)}, bf16[40,2048]{1,0:T(8,128)(2,1)S(1)}, u32[]{:S(2)}, u32[]{:S(2)}) collective-permute-start(bf16[40,2048]{1,0:T(8,128)(2,1)S(1)} %pad_maximum_fusion.3), channel_id=1, source_target_pairs={{0,16},{4,20},{8,24},{12,28},{16,0},{20,4},{24,8},{28,12},{1,17},{... | collective-permute-start | bytes 491528 | tf_op jit(solution)/shard_map/ppermute | solution.py:184
  135.3 1.3 copy-start.4
Sparse Core Ops, SparseCore 0:
  82.4 47.2 all-gather.1

commit v2 on v0

v2 whole, which is shorter than its diff:
```python
import jax
import jax.numpy as jnp
from jax import lax
from jax.experimental import pallas as pl
from jax.experimental.pallas import tpu as pltpu
from jax.sharding import PartitionSpec as P

BF = jnp.bfloat16
F32 = jnp.float32
NN = (((1,), (0,)), ((), ()))
NT = (((1,), (1,)), ((), ()))
MIB = 1 << 20
VMEM = pl.BlockSpec(memory_space=pltpu.VMEM)
ANY = pl.BlockSpec(memory_space=pl.ANY)
HBM = pl.BlockSpec(memory_space=pltpu.HBM)
SMEM = pl.BlockSpec(memory_space=pltpu.SMEM)


def dot(a, b, dims):
    return lax.dot_general(a, b, dims, preferred_element_type=F32)


def stack(parts):
    return jnp.concatenate(parts, axis=0) if len(parts) > 1 else parts[0]


def pieces(size, step):
    return [(at, min(step, size - at)) for at in range(0, size, step)]


def struct(shape, dtype=BF):
    return jax.ShapeDtypeStruct(tuple(shape), dtype)


def call(kernel, args, in_specs, out_specs, out_shape, cost, vmem, after=(), aliases=None, scratch=(), mark=False):
    n, m = len(args), len(out_shape)

    def body(*refs):
        outs = refs[n + len(after) :]
        if mark:
            outs[m][...] = jnp.zeros((8, 128), F32)
            outs = outs[:m] + outs[m + 1 :]
        kernel(*refs[:n], *outs)

    out = pl.pallas_call(
        body,
        out_shape=list(out_shape) + [struct((8, 128), F32)] * mark,
        in_specs=list(in_specs) + [ANY] * len(after),
        out_specs=list(out_specs) + [VMEM] * mark,
        scratch_shapes=scratch,
        input_output_aliases=aliases or {},
        compiler_params=pltpu.CompilerParams(vmem_limit_bytes=vmem * MIB),
        cost_estimate=pl.CostEstimate(flops=cost[0], bytes_accessed=cost[1], transcendentals=0),
    )(*args, *after)
    return out if len(out) > 1 else out[0]


def hold(x, after):
    def kernel(x_ref, out_ref):
        out_ref[...] = x_ref[...]

    return call(kernel, (x,), [VMEM], [VMEM], [struct(x.shape, x.dtype)], (0, 4 * x.size), 8, after)


def brought(ranges, vmem, after=()):
    n = len(ranges)

    def kernel(*refs):
        copies = [
            pltpu.make_async_copy(refs[k].at[pl.ds(first, count)], refs[n + k], refs[2 * n].at[k])
            for k, (_, first, count) in enumerate(ranges)
        ]
        for copy in copies:
            copy.start()
        for copy in copies:
            copy.wait()

    return call(
        kernel, [x for x, _, _ in ranges], [HBM] * n, [VMEM] * n, [struct((count, x.shape[1])) for x, _, count in ranges],
        (0, sum(2 * count * x.shape[1] for x, _, count in ranges)), vmem, after,
        scratch=[pltpu.SemaphoreType.DMA((n,))], mark=True,
    )


def factors(order, places, gate, up, after=()):
    blocks, rows, width = gate.shape
    half = blocks // 2

    def kernel(order_ref, places_ref, gate_ref, up_ref, hidden_ref, slope_ref, silu_ref, held, sem):
        copies = []
        for i in range(blocks):
            for k, ref in enumerate((gate_ref, up_ref)):
                copies.append(pltpu.make_async_copy(ref.at[order_ref[i]], held.at[k, i], sem.at[k, i]))
                copies[-1].start()
        for i in range(blocks):
            copies[2 * i].wait()
            copies[2 * i + 1].wait()
            g = held[0, i].astype(F32)
            u = held[1, i].astype(F32)
            sig = 1.0 / (1.0 + jnp.exp(-g))
            silu = g * sig
            hidden_ref[places_ref[i]] = (silu * u).astype(BF)
            if i < half:
                silu_ref[i] = silu
                slope_ref[i] = u * sig * (1.0 + g * (1.0 - sig))

    return call(
        kernel, (order, places, gate, up), [SMEM, SMEM, HBM, HBM], [VMEM] * 3,
        [struct(gate.shape), struct((half, rows, width), F32), struct((half, rows, width), F32)],
        (10 * gate.size, 10 * gate.size), 36, after,
        scratch=[pltpu.VMEM((2, blocks, rows, width), BF), pltpu.SemaphoreType.DMA((2, blocks))],
    )


class Blocks:
    def __init__(self):
        self.arrays, self.place = [], {}

    def add(self, x, codes):
        for i, code in enumerate(codes):
            self.place[code] = (len(self.arrays), i)
        self.arrays.append(x)

    def read(self, refs, codes, columns=slice(None)):
        return stack([refs[self.place[c][0]][self.place[c][1], :, columns] for c in codes])


def hidden_part(core, grads, weight, after=()):
    half, width = grads.shape[0] // 2, weight.shape[0]

    def kernel(core_ref, grads_ref, weight_ref, mine_ref, other_ref):
        total = dot(grads_ref[...], weight_ref[...], NT)
        is_first = core_ref[0] == 0
        mine_ref[...] = jnp.where(is_first, total[:half], total[half:])
        other_ref[...] = jnp.where(is_first, total[half:], total[:half]).astype(BF)

    return call(
        kernel, (core, grads, weight), [SMEM, VMEM, VMEM], [VMEM] * 2, [struct((half, width), F32), struct((half, width))],
        (4 * half * weight.size, 2 * weight.size), 12, after,
    )


def partial_sum(mine, arrived):
    def kernel(mine_ref, arrived_ref, out_ref):
        out_ref[...] = (mine_ref[...] + arrived_ref[...].astype(F32)).astype(BF)

    return call(kernel, (mine, arrived), [VMEM] * 2, [VMEM], [struct(mine.shape)], (mine.size, 8 * mine.size), 8)


def local_grads(mine, arrived, slope, silu, first, after=()):
    rows, width = mine.shape

    def kernel(mine_ref, *refs):
        slope_ref, silu_ref, pair_ref = refs[-3:]
        total = mine_ref[...]
        for ref in refs[:-3]:
            total = total + ref[...].astype(F32)
        pair_ref[0] = (total * slope_ref[:, :, first : first + width].reshape(rows, width)).astype(BF)
        pair_ref[1] = (total * silu_ref[:, :, first : first + width].reshape(rows, width)).astype(BF)

    args = (mine, *arrived, slope, silu)
    return call(
        kernel, args, [VMEM] * len(args), [VMEM], [struct((2, rows, width))], (6 * mine.size, 16 * mine.size), 6, after
    )


def in_order(core, pairs, after=()):
    half = pairs[0][0].shape[1]
    widths = [mine.shape[2] for mine, _ in pairs]
    n = 2 * len(pairs)

    def kernel(core_ref, *refs):
        ins, outs = refs[:n], refs[n:]

        def put(low):
            at = 0
            for k, width in enumerate(widths):
                for which, ref in enumerate(outs):
                    ref[:half, at : at + width] = ins[2 * k + low][which]
                    ref[half:, at : at + width] = ins[2 * k + 1 - low][which]
                at += width

        @pl.when(core_ref[0] == 0)
        def _():
            put(0)

        @pl.when(core_ref[0] != 0)
        def _():
            put(1)

    shape = struct((2 * half, sum(widths)))
    return call(
        kernel, (core, *[x for pair in pairs for x in pair]), [SMEM] + [VMEM] * n, [VMEM] * 2,
        [shape] * 2, (shape.size, 8 * shape.size), 8, after,
    )


def turned(blocks, codes, after=()):
    rows, width = blocks.arrays[0].shape[1:]
    total = rows * len(codes)

    def kernel(*refs):
        ins, out_ref = refs[:-1], refs[-1]
        for at, size in pieces(width, 512):
            out_ref[at : at + size] = blocks.read(ins, codes, slice(at, at + size)).T

    return call(
        kernel, blocks.arrays, [VMEM] * len(blocks.arrays), [VMEM], [struct((width, total))],
        (total * width, 4 * total * width), 6, after,
    )


def input_part(gate, up, weights, first, wide, rows, groups, place, vmem, after=()):
    tokens, units = gate.shape
    shape = (len(groups[0]), len(groups[0][0]), rows, wide)
    cuts = pieces(wide, 512)
    load = first is not None

    def kernel(gate_ref, up_ref, *refs):
        weight_refs, outs = refs[:2], refs[2:4]
        copies = []
        if load:
            held, sem = refs[4:]
            for i, (at, size) in enumerate(cuts):
                for k in (0, 1):
                    copies.append(
                        pltpu.make_async_copy(
                            weight_refs[k].at[pl.ds(first + at, size)], held.at[k, pl.ds(at, size)], sem.at[k, i]
                        )
                    )
            weight_refs = [held.at[0], held.at[1]]
        for copy in copies[:2]:
            copy.start()
        for i, (at, size) in enumerate(cuts):
            total = 0.0
            for k, ref in enumerate((gate_ref, up_ref)):
                if load:
                    copies[2 * i + k].wait()
                    if 2 * i + k + 2 < len(copies):
                        copies[2 * i + k + 2].start()
                total = total + dot(ref[...], weight_refs[k][at : at + size], NT)
            for ref, group in zip(outs, groups):
                for g, codes in enumerate(group):
                    for j, code in enumerate(codes):
                        b = place[code] * rows
                        ref[g, j, :, at : at + size] = total[b : b + rows].astype(BF)

    return call(
        kernel, (gate, up, *weights), [VMEM] * 2 + [HBM if load else VMEM] * 2, [VMEM] * 2, [struct(shape)] * 2,
        (4 * tokens * units * wide, 4 * units * wide), vmem, after,
        scratch=[pltpu.VMEM((2, wide, units), BF), pltpu.SemaphoreType.DMA((2, len(cuts)))] if load else (), mark=True,
    )


def fold(keep, arrived, after=()):
    def kernel(keep_ref, arrived_ref, a_ref, b_ref):
        a_ref[...] = keep_ref[0] + arrived_ref[0]
        b_ref[...] = keep_ref[1] + arrived_ref[1]

    shape = struct(keep.shape[1:])
    return call(kernel, (keep, arrived), [VMEM] * 2, [VMEM] * 2, [shape, shape], (keep.size, 6 * keep.size), 8, after)


def join(left, left_arrived, right, right_arrived, after=()):
    blocks, rows, wide = left.shape
    half = blocks // 2

    def kernel(a_ref, b_ref, c_ref, d_ref, *outs):
        for k, ref in enumerate(outs):
            at = slice(k * half, (k + 1) * half) if half else slice(None)
            ref[:, :, :wide] = a_ref[at] + b_ref[at]
            ref[:, :, wide:] = c_ref[at] + d_ref[at]

    shape = struct((half or blocks, rows, 2 * wide))
    out = call(
        kernel, (left, left_arrived, right, right_arrived), [VMEM] * 4, [VMEM] * (2 if half else 1),
        [shape] * (2 if half else 1), (left.size * 2, 12 * left.size), 8, after,
    )
    return out if half else (out, None)


def long_product(left, right, begin, end, into=None, after=(), ahead=None, step=512, vmem=24):
    height, depth = left.shape
    width = right.shape[1]
    cuts = [(begin + at, size) for at, size in pieces(end - begin, step)]
    slots = 2
    ahead = ahead or []
    n = len(ahead)
    m = 0 if into is None else 1

    def kernel(left_ref, right_ref, *refs):
        sources, (out_ref, *targets), (held, sem, *more) = refs[:n], refs[n + m : 2 * n + m + 1], refs[2 * n + m + 1 :]
        early = [
            pltpu.make_async_copy(a.at[pl.ds(first, count)], b, more[0].at[k])
            for k, (a, b, (_, first, count)) in enumerate(zip(sources, targets, ahead))
        ]
        for copy in early:
            copy.start()
        copies = []
        for i, (at, size) in enumerate(cuts):
            value = dot(left_ref[at : at + size], right_ref[...], NN).astype(BF)
            if i >= slots:
                copies[i - slots].wait()
            held[i % slots, :size] = value
            copies.append(
                pltpu.make_async_copy(held.at[i % slots, pl.ds(0, size)], out_ref.at[pl.ds(at, size)], sem.at[i % slots])
            )
            copies[-1].start()
        for copy in copies[-slots:] + early:
            copy.wait()

    args = [left, right] + [x for x, _, _ in ahead] + ([into] if m else [])
    return call(
        kernel, args, [VMEM] * 2 + [HBM] * (n + m), [HBM] + [VMEM] * n,
        [struct((height, width))] + [struct((count, x.shape[1])) for x, _, count in ahead],
        (2 * depth * width * (end - begin), 2 * width * (end - begin)), vmem, after, {len(args) - 1: 0} if m else None,
        scratch=[pltpu.VMEM((slots, step, width), BF), pltpu.SemaphoreType.DMA((slots,))]
        + ([pltpu.SemaphoreType.DMA((n,))] if n else []),
        mark=True,
    )


def laid(parts):
    if len(parts) == 1:
        return parts[0]

    def kernel(*refs):
        at = 0
        for ref in refs[:-1]:
            refs[-1][at : at + ref.shape[0]] = ref[...]
            at += ref.shape[0]

    count = sum(x.shape[0] for x in parts)
    return call(
        kernel, parts, [VMEM] * len(parts), [VMEM], [struct((count, *parts[0].shape[1:]))], (0, 4 * count * parts[0].size), 8
    )


def stacked(blocks, codes, after=()):
    rows, width = blocks.arrays[0].shape[1:]
    total = rows * len(codes)

    def kernel(*refs):
        refs[-1][...] = blocks.read(refs[:-1], codes)

    return call(
        kernel, blocks.arrays, [VMEM] * len(blocks.arrays), [VMEM], [struct((total, width))],
        (total * width, 4 * total * width), 8, after,
    )


def on_device(n_row, n_col, tokens, out_grad, gate_saved, up_saved, gate_weight, up_weight, down_weight):
    rows, features = tokens.shape
    units = gate_saved.shape[1]
    row = lax.axis_index("row").astype(jnp.int32)
    core_index = (lax.axis_index("col") % 2).astype(jnp.int32)
    core = core_index.reshape(1)

    def swap(x, mask, axis="row"):
        n = n_row if axis == "row" else n_col
        return lax.ppermute(x, axis, [(i, i ^ mask) for i in range(n)])

    def closure(masks):
        codes = [0]
        for m in masks:
            codes += [c ^ m for c in codes]
        return codes

    def move(codes, mask):
        return [c ^ mask for c in codes]

    masks = [m for m in (1 << i for i in range(1, 31)) if m < n_row]
    low = closure(masks)
    codes = low + move(low, 1)
    place = {c: i for i, c in enumerate(codes)}
    q = len(low)
    order = jnp.array(codes, jnp.int32) ^ row ^ core_index
    places = jnp.arange(2 * q, dtype=jnp.int32) ^ (core_index * q)

    own = out_grad.reshape(1, rows, features)
    held = [(own, [0])]
    for m in masks[:0:-1]:
        held.append((swap(stack([x for x, _ in held]), m), [c ^ m for _, cs in held for c in cs]))
    near = [(swap(held[0][0], masks[0]), move(held[0][1], masks[0]))]
    parts = 2 if (units // 2) % 128 == 0 else 1
    width = units // parts
    *weight_rows, mark = brought([(down_weight, k * width, width) for k in range(parts)], 34, (order, places))
    held = held[:1] + [(hold(x, (mark, near[0][0])), cs) for x, cs in held[1:]]
    near += [(swap(x, masks[0]), move(cs, masks[0])) for x, cs in held[1:]]
    held += near
    grads = Blocks()
    for x, cs in held + [(swap(x, 1), move(cs, 1)) for x, cs in held]:
        grads.add(x, cs)
    all_grads = stacked(grads, codes)

    def summed(mine, other):
        arrived = [swap(other, 1, "col")]
        sent, m = None, 2
        while m < n_col:
            if len(arrived) > 1:
                mine = mine + arrived.pop(0).astype(F32)
            sent = partial_sum(mine, arrived[-1])
            arrived.append(swap(sent, m, "col"))
            m *= 2
        return mine, arrived, sent

    sums = []
    for k in range(parts):
        after = (sums[-1][1],) if k else ()
        sums.append(hidden_part(core, all_grads, weight_rows[k], after))
    sums = [summed(*x) for x in sums]

    all_tokens = Blocks()
    held = [(hold(tokens.reshape(1, rows, features), (sums[-1][2],)), [0])]
    for m in masks[::-1]:
        joined = laid([x for x, _ in held])
        held.append((swap(joined, m), [c ^ m for _, cs in held for c in cs]))
    base_crossed = swap(joined, 1)
    crossed = [(base_crossed, [c ^ 1 for _, cs in held[:-1] for c in cs]), (swap(held[-1][0], 1), move(held[-1][1], 1))]
    for x, cs in held + crossed:
        all_tokens.add(x, cs)

    hidden, slope, silu = factors(
        order, places, gate_saved.reshape(n_row, rows, units), up_saved.reshape(n_row, rows, units), (sums[0][2],)
    )
    hidden_blocks = Blocks()
    hidden_blocks.add(hidden, codes)
    hidden_turned = turned(hidden_blocks, codes)
    wide = features // 2
    weights = (gate_weight, up_weight)
    down_grad, a, b, c, d, mark = long_product(
        hidden_turned, all_grads, 0, units, None, (sums[-1][2],),
        [(x, at, wide) for at in (0, wide) for x in weights], 256, 12,
    )
    left_weights, right_weights = (a, b), (c, d)
    pairs = []
    for k, (mine, arrived, _) in enumerate(sums):
        after = (mark, base_crossed, held[-1][0])
        pairs.append(local_grads(mine, arrived, slope, silu, k * width, after))
    gate, up = in_order(core, [(pair, swap(pair, 1, "col")) for pair in pairs])
    tokens_turned = turned(all_tokens, codes)

    rest = closure(masks[1:])
    m = masks[0]
    *left, mark = input_part(
        gate, up, left_weights, None, wide, rows, [[rest, move(rest, m)], [move(rest, 1), move(rest, 1 ^ m)]], place, 7
    )
    *right, mark = input_part(
        gate, up, right_weights, None, wide, rows, [[rest, move(rest, 1)], [move(rest, m), move(rest, m ^ 1)]], place, 7, (mark,)
    )
    cut = features // 2 // 512 * 512
    left_got, right_got = swap(left[1], 1), swap(right[1], m)
    left = fold(left[0], left_got)
    left_got = swap(left[1], m)
    gate_grad, mark = long_product(tokens_turned, gate, 0, cut, None, (left[1],))
    right = fold(right[0], right_got, (mark,))
    right_got = swap(right[1], 1)
    gate_grad, mark = long_product(tokens_turned, gate, cut, features, gate_grad, (left_got, right[1]))
    total, sent = join(left[0], left_got, right[0], right_got, (mark,))
    for k, m in enumerate(masks[:0:-1]):
        if k > 0:
            n = total.shape[0] // 2
            total, sent = total[:n], total[n:]
        got = swap(sent, m)
        if k == 0:
            up_grad, _ = long_product(tokens_turned, up, 0, features, None, (sent,))
        total = total + got
    return total.reshape(rows, features), gate_grad, up_grad, down_grad


def solution(mesh):
    n_row, n_col = mesh.shape["row"], mesh.shape["col"]
    return jax.shard_map(
        lambda *args: on_device(n_row, n_col, *args),
        mesh=mesh,
        in_specs=(
            P("row", "col"),
            P("row", "col"),
            P(None, "row"),
            P(None, "row"),
            P("col", "row"),
            P("col", "row"),
            P("row", "col"),
        ),
        out_specs=(P("row", "col"), P("col", "row"), P("col", "row"), P("row", "col")),
        check_vma=False,
    )
```

time: 272 us -> 115 us (0.42)
  waiting for transfers between devices: 145 us -> 22.4 us
  matrix products: 69.8 us -> 0 us
  Pallas kernels: 0 us -> 64.9 us
  local copies, waits for them, and re-layouts: 37.5 us -> 0.04 us
  starting transfers between devices: 0.34 us -> 25.3 us
  between operations: 13.8 us -> 0.9 us
  other arithmetic: 4.66 us -> 1.34 us
    psum x1 -> x0, waiting for transfers between devices: 70.8 us -> none  [on_device(): grad_hidden = lax.psum(hidden_part, 'col')]
    dot_general x6 -> x0, matrix products: 69.8 us -> none  [the longest x1 12.6 us: on_device(): lax.dot_general(hidden, all_grads, contract_rows, preferred_element_type=...]
    pallas_call x0 -> x24, Pallas kernels: none -> 64.9 us  [call(): pl.pallas_call(body, out_shape=list(out_shape) + [struct((8, 128), F32)]...]
    all_gather x2 -> x0, waiting for transfers between devices: 63.3 us -> none  [the longest x1 47 us: on_device(): lax.all_gather(out_grad, 'row', axis=0, tiled=True)]
    unnamed x14 -> x16, local copies, waits for them, and re-layouts: 37.5 us -> 0.04 us
    ppermute x0 -> x22, starting transfers between devices: none -> 25.3 us  [swap(): return lax.ppermute(x, axis, [(i, i ^ mask) for i in range(n)])]
    ppermute x0 -> x22, waiting for transfers between devices: none -> 22.4 us  [swap(): return lax.ppermute(x, axis, [(i, i ^ mask) for i in range(n)])]
    reduce_scatter x1 -> x0, waiting for transfers between devices: 9.13 us -> none  [on_device(): lax.psum_scatter((result + lax.dot_general(grad_up, up_weight, (((1,), (1...]
  transfers between devices with their start and end apart: 4 -> 22, of which waited for: 4 -> 14; matrix products, arithmetic and copies ran while one was open for 36% -> 1% of each run, Pallas kernels for 0% -> 52%
where the time goes in v2:
time: 115 us
  Pallas kernels  64.9 us (56%)
  starting transfers between devices  25.3 us (22%)
  waiting for transfers between devices  22.4 us (19%)
  other arithmetic  1.34 us (1%)
    pallas_call x24, Pallas kernels, call(): pl.pallas_call(body, out_shape=list(out_shape) + [struct((8, 128), F32)]...  64.9 us
    ppermute x22, starting transfers between devices, swap(): return lax.ppermute(x, axis, [(i, i ^ mask) for i in range(n)])  25.3 us
    ppermute x22, waiting for transfers between devices, swap(): return lax.ppermute(x, axis, [(i, i ^ mask) for i in range(n)])  22.4 us
  transfers between devices with their start and end apart: 22, of which 14 were waited for; matrix products, arithmetic and copies ran while one was open for 1% of the time, Pallas kernels for 52%

profile of v2, /device:TPU:0, one launch (start us, length us, event | category | flops | bytes accessed | tf_op | source)
XLA Modules:
  0.0 114.9 jit_solution(6029203990216490418)
XLA Ops:
  0.6 4.1 %collective-permute-start = (bf16[1,40,2048]{2,1,0:T(8,128)(2,1)}, bf16[1,40,2048]{2,1,0:T(8,128)(2,1)S(1)}, u32[]{:S(2)}, u32[]{:S(2)}) collective-permute-start(bf16[1,40,2048]{2,1,0:T(8,128)(2,1)} %bitcast.9), channel_id=1, source_target_pairs={{0,16},{4,20},{8,24},{12,28},{16,0},{20,4},{24,8},{28,12},{1,17},{... | collective-permute-start | bytes 491528 | tf_op jit(solution)/shard_map/ppermute | solution.py:361
  4.7 1.6 %collective-permute-start.1 = (bf16[1,40,2048]{2,1,0:T(8,128)(2,1)}, bf16[1,40,2048]{2,1,0:T(8,128)(2,1)S(1)}, u32[]{:S(2)}, u32[]{:S(2)}) collective-permute-start(bf16[1,40,2048]{2,1,0:T(8,128)(2,1)} %bitcast.10), channel_id=1, source_target_pairs={{0,8},{4,12},{8,0},{12,4},{16,24},{20,28},{24,16},{28,20},{1,9},{5... | collective-permute-start | bytes 491528 | tf_op jit(solution)/shard_map/ppermute | solution.py:361
  6.3 0.7 iota_xor_fusion
  7.0 4.9 %shard_map.111 = (bf16[1664,2048]{1,0:T(8,128)(2,1)S(1)}, bf16[1664,2048]{1,0:T(8,128)(2,1)S(1)}, f32[8,128]{1,0:T(8,128)S(1)}) custom-call(bf16[3328,2048]{1,0:T(8,128)(2,1)} %refs_1_.1, bf16[3328,2048]{1,0:T(8,128)(2,1)} %refs_1_.1, s32[8]{0:T(128)S(1)} %get-tuple-element.73.refs_2_.refs_0_, s32[8]{0:T(128)S(1)} %get-tuple-element.72.refs_3_.refs_1_), custom_call_target="tpu_custom_call" | custom-call | bytes 13631488 | tf_op jit(solution)/shard_map/pallas_call | solution.py:45
  11.9 0.9 collective-permute-done.refs_0_
  12.8 0.2 collective-permute-done.1.refs_2_
  13.0 1.6 %collective-permute-start.2 = (bf16[1,40,2048]{2,1,0:T(8,128)(2,1)S(1)}, bf16[1,40,2048]{2,1,0:T(8,128)(2,1)S(1)}, u32[]{:S(2)}, u32[]{:S(2)}) collective-permute-start(bf16[1,40,2048]{2,1,0:T(8,128)(2,1)S(1)} %shard_map.112.refs_1_), channel_id=1, source_target_pairs={{0,8},{4,12},{8,0},{12,4},{16,24},{20,28},{24,16},{28,20},{1,9},{5... | collective-permute-start | bytes 491528 | tf_op jit(solution)/shard_map/ppermute | solution.py:361
  14.5 1.5 %collective-permute-start.3 = (bf16[1,40,2048]{2,1,0:T(8,128)(2,1)S(1)}, bf16[1,40,2048]{2,1,0:T(8,128)(2,1)S(1)}, u32[]{:S(2)}, u32[]{:S(2)}) collective-permute-start(bf16[1,40,2048]{2,1,0:T(8,128)(2,1)S(1)} %bitcast.11), channel_id=1, source_target_pairs={{0,4},{4,0},{8,12},{12,8},{16,20},{20,16},{24,28},{28,24},{1,5},{5... | collective-permute-start | bytes 491528 | tf_op jit(solution)/shard_map/ppermute | solution.py:361
  16.0 0.5 collective-permute-start.4
  16.5 1.5 %collective-permute-start.5 = (bf16[1,40,2048]{2,1,0:T(8,128)(2,1)S(1)}, bf16[1,40,2048]{2,1,0:T(8,128)(2,1)S(1)}, u32[]{:S(2)}, u32[]{:S(2)}) collective-permute-start(bf16[1,40,2048]{2,1,0:T(8,128)(2,1)S(1)} %collective-permute-done.1.refs_2_), channel_id=1, source_target_pairs={{0,4},{4,0},{8,12},{12,8},{16,20},{20,16},{24,28},{28,24},{1,5},{5... | collective-permute-start | bytes 491528 | tf_op jit(solution)/shard_map/ppermute | solution.py:361
  18.0 0.3 collective-permute-done.2.refs_3_
  18.4 1.5 %collective-permute-start.6 = (bf16[1,40,2048]{2,1,0:T(8,128)(2,1)S(1)}, bf16[1,40,2048]{2,1,0:T(8,128)(2,1)S(1)}, u32[]{:S(2)}, u32[]{:S(2)}) collective-permute-start(bf16[1,40,2048]{2,1,0:T(8,128)(2,1)S(1)} %collective-permute-done.2.refs_3_), channel_id=1, source_target_pairs={{0,4},{4,0},{8,12},{12,8},{16,20},{20,16},{24,28},{28,24},{1,5},{5... | collective-permute-start | bytes 491528 | tf_op jit(solution)/shard_map/ppermute | solution.py:361
  19.9 1.8 %collective-permute-done.3.refs_4_ = bf16[1,40,2048]{2,1,0:T(8,128)(2,1)S(1)} collective-permute-done((bf16[1,40,2048]{2,1,0:T(8,128)(2,1)S(1)}, bf16[1,40,2048]{2,1,0:T(8,128)(2,1)S(1)}, u32[]{:S(2)}, u32[]{:S(2)}) %collective-permute-start.3) | collective-permute-done | bytes 163872 | tf_op jit(solution)/shard_map/ppermute | solution.py:361
  21.7 3.5 %collective-permute-done.4.refs_5_ = bf16[1,40,2048]{2,1,0:T(8,128)(2,1)S(1)} collective-permute-done((bf16[1,40,2048]{2,1,0:T(8,128)(2,1)S(1)}, bf16[1,40,2048]{2,1,0:T(8,128)(2,1)S(1)}, u32[]{:S(2)}, u32[]{:S(2)}) %collective-permute-start.4) | collective-permute-done | bytes 163872 | tf_op jit(solution)/shard_map/ppermute | solution.py:361
  25.2 3.0 %collective-permute-done.5.refs_6_ = bf16[1,40,2048]{2,1,0:T(8,128)(2,1)S(1)} collective-permute-done((bf16[1,40,2048]{2,1,0:T(8,128)(2,1)S(1)}, bf16[1,40,2048]{2,1,0:T(8,128)(2,1)S(1)}, u32[]{:S(2)}, u32[]{:S(2)}) %collective-permute-start.5) | collective-permute-done | bytes 163872 | tf_op jit(solution)/shard_map/ppermute | solution.py:361
  28.2 1.8 %collective-permute-done.6.refs_7_ = bf16[1,40,2048]{2,1,0:T(8,128)(2,1)S(1)} collective-permute-done((bf16[1,40,2048]{2,1,0:T(8,128)(2,1)S(1)}, bf16[1,40,2048]{2,1,0:T(8,128)(2,1)S(1)}, u32[]{:S(2)}, u32[]{:S(2)}) %collective-permute-start.6) | collective-permute-done | bytes 163872 | tf_op jit(solution)/shard_map/ppermute | solution.py:361
  29.9 0.1 shard_map.113.refs_1_
  30.0 2.6 %shard_map.114 = (f32[160,1664]{1,0:T(8,128)S(1)}, bf16[160,1664]{1,0:T(8,128)(2,1)S(1)}) custom-call(s32[1]{0:T(128)} %bitcast.refs_0_, bf16[320,2048]{1,0:T(8,128)(2,1)S(1)} %shard_map.113.refs_1_, bf16[1664,2048]{1,0:T(8,128)(2,1)S(1)} %get-tuple-element.39.refs_2_), custom_call_target="tpu_custom_call" | custom-call | flops 2181038080 | bytes 6815744 | tf_op jit(solution)/shard_map/pallas_call | solution.py:45
  32.6 2.6 %shard_map.118 = (f32[160,1664]{1,0:T(8,128)S(1)}, bf16[160,1664]{1,0:T(8,128)(2,1)S(1)}) custom-call(s32[1]{0:T(128)} %bitcast.refs_0_, bf16[320,2048]{1,0:T(8,128)(2,1)S(1)} %shard_map.113.refs_1_, bf16[1664,2048]{1,0:T(8,128)(2,1)S(1)} %get-tuple-element.45.refs_2_, bf16[160,1664]{1,0:T(8,128)(2,1)S(1)} %get-tuple-element.41.refs_3_), custom_call_target="tpu_custom_call" | custom-call | flops 2181038080 | bytes 6815744 | tf_op jit(solution)/shard_map/pallas_call | solution.py:45
  35.2 0.0 copy-start.7
  35.2 0.1 collective-permute-start.9
  35.3 0.5 collective-permute-start.7
  35.8 1.4 %collective-permute-done.9.refs_1_ = bf16[160,1664]{1,0:T(8,128)(2,1)S(1)} collective-permute-done((bf16[160,1664]{1,0:T(8,128)(2,1)S(1)}, bf16[160,1664]{1,0:T(8,128)(2,1)S(1)}, u32[]{:S(2)}, u32[]{:S(2)}) %collective-permute-start.9) | collective-permute-done | bytes 532512 | tf_op jit(solution)/shard_map/ppermute | solution.py:361
  37.2 0.1 shard_map.119.refs_6_.refs_1_
  37.4 3.3 %collective-permute-start.10 = (bf16[1,40,2048]{2,1,0:T(8,128)(2,1)S(1)}, bf16[1,40,2048]{2,1,0:T(8,128)(2,1)S(1)}, u32[]{:S(2)}, u32[]{:S(2)}) collective-permute-start(bf16[1,40,2048]{2,1,0:T(8,128)(2,1)S(1)} %shard_map.121.refs_0_), channel_id=1, source_target_pairs={{0,16},{4,20},{8,24},{12,28},{16,0},{20,4},{24,8},{28,12},{1,17},{... | collective-permute-start | bytes 491528 | tf_op jit(solution)/shard_map/ppermute | solution.py:361
  40.7 0.0 collective-permute-done.7.refs_1_
  40.7 1.0 shard_map.115.refs_4_
  41.7 1.5 %collective-permute-start.8 = (bf16[160,1664]{1,0:T(8,128)(2,1)}, bf16[160,1664]{1,0:T(8,128)(2,1)}, u32[]{:S(2)}, u32[]{:S(2)}) collective-permute-start(bf16[160,1664]{1,0:T(8,128)(2,1)} %shard_map.115.refs_4_), channel_id=1, source_target_pairs={{0,2},{1,3},{2,0},{3,1},{4,6},{5,7},{6,4},{7,5},{8,10},{9,11},{10,... | collective-permute-start | bytes 1597448 | tf_op jit(solution)/shard_map/ppermute | solution.py:361
  43.2 0.5 collective-permute-start.14
  43.7 3.1 %shard_map.116 = (bf16[8,40,3328]{2,1,0:T(8,128)(2,1)S(1)}, f32[4,40,3328]{2,1,0:T(8,128)S(1)}, f32[4,40,3328]{2,1,0:T(8,128)S(1)}) custom-call(s32[8]{0:T(128)S(1)} %get-tuple-element.73.refs_2_.refs_0_, s32[8]{0:T(128)S(1)} %get-tuple-element.72.refs_3_.refs_1_, bf16[8,40,3328]{2,1,0:T(8,128)(2,1)S(1)} %bitcast.7, bf16[8,40,3328]{2,1,0:T(8,128)(2,1)S(1)} %bitcast.8, ...), custom_call_target="tpu_custom_call" | custom-call | flops 10649600 | bytes 10649600 | tf_op jit(solution)/shard_map/pallas_call | solution.py:45
  46.8 0.7 shard_map.117.refs_0_
  47.6 1.0 collective-permute-done.10.refs_1_
  48.5 0.0 copy-start.3
  48.6 1.6 %collective-permute-start.11 = (bf16[2,40,2048]{2,1,0:T(8,128)(2,1)S(1)}, bf16[2,40,2048]{2,1,0:T(8,128)(2,1)S(1)}, u32[]{:S(2)}, u32[]{:S(2)}) collective-permute-start(bf16[2,40,2048]{2,1,0:T(8,128)(2,1)S(1)} %shard_map.122), channel_id=1, source_target_pairs={{0,4},{4,0},{8,12},{12,8},{16,20},{20,16},{24,28},{28,24},{1,5},{5... | collective-permute-start | bytes 983048 | tf_op jit(solution)/shard_map/ppermute | solution.py:361
  50.1 0.0 collective-permute-start.12
  50.1 13.5 %shard_map.120 = (bf16[3328,2048]{1,0:T(8,128)(2,1)}, bf16[1024,3328]{1,0:T(8,128)(2,1)S(1)}, bf16[1024,3328]{1,0:T(8,128)(2,1)S(1)}, bf16[1024,3328]{1,0:T(8,12...) custom-call(bf16[3328,320]{1,0:T(8,128)(2,1)S(1)} %shard_map.117.refs_0_, ...), custom_call_target="tpu_custom_call" | custom-call | flops 4362076160 | bytes 13631488 | tf_op jit(solution)/shard_map/pallas_call | solution.py:45
  63.6 0.0 collective-permute-done.11.refs_6_.refs_3_
  63.7 0.0 collective-permute-done.12.refs_7_.refs_2_
  63.7 0.0 collective-permute-done.8.refs_2_
  63.7 1.4 %shard_map.123.refs_1_ = bf16[2,160,1664]{2,1,0:T(8,128)(2,1)S(1)} custom-call(f32[160,1664]{1,0:T(8,128)S(1)} %get-tuple-element.40.refs_0_, bf16[160,1664]{1,0:T(8,128)(2,1)S(1)} %copy-done.3, bf16[160,1664]{1,0:T(8,128)(2,1)} %collective-permute-done.8.refs_2_, f32[4,40,3328]{2,1,0:T(8,128)S(1)} %get-tuple-element.42.refs_3_, ...), custom_call_target="tpu_custom_call" | custom-call | flops 1597440 | bytes 4259840 | tf_op jit(solution)/shard_map/pallas_call | solution.py:45
  65.1 0.1 collective-permute-start.13
  65.2 2.1 %collective-permute-done.14.refs_2_ = bf16[160,1664]{1,0:T(8,128)(2,1)} collective-permute-done((bf16[160,1664]{1,0:T(8,128)(2,1)S(1)}, bf16[160,1664]{1,0:T(8,128)(2,1)}, u32[]{:S(2)}, u32[]{:S(2)}) %collective-permute-start.14) | collective-permute-done | bytes 532512 | tf_op jit(solution)/shard_map/ppermute | solution.py:361
  67.3 1.4 %shard_map.124.refs_3_ = bf16[2,160,1664]{2,1,0:T(8,128)(2,1)S(1)} custom-call(f32[160,1664]{1,0:T(8,128)S(1)} %get-tuple-element.46.refs_0_, bf16[160,1664]{1,0:T(8,128)(2,1)S(1)} %copy-done.1, bf16[160,1664]{1,0:T(8,128)(2,1)} %collective-permute-done.14.refs_2_, f32[4,40,3328]{2,1,0:T(8,128)S(1)} %get-tuple-element.42.refs_3_, ...), custom_call_target="tpu_custom_call" | custom-call | flops 1597440 | bytes 4259840 | tf_op jit(solution)/shard_map/pallas_call | solution.py:45
  68.7 0.1 collective-permute-start.15
  68.7 1.6 %collective-permute-start.19 = (bf16[2,40,2048]{2,1,0:T(8,128)(2,1)S(1)}, bf16[2,40,2048]{2,1,0:T(8,128)(2,1)S(1)}, u32[]{:S(2)}, u32[]{:S(2)}) collective-permute-start(bf16[2,40,2048]{2,1,0:T(8,128)(2,1)S(1)} %collective-permute-done.12.refs_7_.refs_2_), channel_id=1, source_target_pairs={{0,4},{4,0},{8,12},{12,8},{16,20},{20,16},{24,28},{28,24},{1,5},{5... | collective-permute-start | bytes 983048 | tf_op jit(solution)/shard_map/ppermute | solution.py:361
  70.3 1.1 collective-permute-done.15.refs_4_
  71.4 0.5 shard_map.125
  71.9 4.6 %shard_map.126 = (bf16[2,2,40,1024]{3,2,1,0:T(8,128)(2,1)S(1)}, bf16[2,2,40,1024]{3,2,1,0:T(8,128)(2,1)S(1)}, f32[8,128]{1,0:T(8,128)S(1)}) custom-call(bf16[320,3328]{1,0:T(8,128)(2,1)S(1)} %get-tuple-element.49.refs_0_.refs_1_, bf16[320,3328]{1,0:T(8,128)(2,1)S(1)} %get-tuple-element.50.refs_1_, bf16[1024,3328]{1,0:T(8,128)(2,1)S(1)} %get-tuple-element.51.refs_2_, ...), custom_call_target="tpu_custom_call" | custom-call | flops 4362076160 | bytes 13631488 | tf_op jit(solution)/shard_map/pallas_call | solution.py:45
  76.5 1.6 %collective-permute-start.16 = (bf16[2,2,40,1024]{3,2,1,0:T(8,128)(2,1)S(1)}, bf16[2,2,40,1024]{3,2,1,0:T(8,128)(2,1)S(1)}, u32[]{:S(2)}, u32[]{:S(2)}) collective-permute-start(bf16[2,2,40,1024]{3,2,1,0:T(8,128)(2,1)S(1)} %get-tuple-element.54), channel_id=1, source_target_pairs={{0,4},{4,0},{8,12},{12,8},{16,20},{20,16},{24,28},{28,24},{1,5},{5... | collective-permute-start | bytes 983048 | tf_op jit(solution)/shard_map/ppermute | solution.py:361
  78.1 5.0 %shard_map.128 = (bf16[2,2,40,1024]{3,2,1,0:T(8,128)(2,1)S(1)}, bf16[2,2,40,1024]{3,2,1,0:T(8,128)(2,1)S(1)}, f32[8,128]{1,0:T(8,128)}) custom-call(bf16[320,3328]{1,0:T(8,128)(2,1)S(1)} %get-tuple-element.49.refs_0_.refs_1_, bf16[320,3328]{1,0:T(8,128)(2,1)S(1)} %get-tuple-element.50.refs_1_, bf16[1024,3328]{1,0:T(8,128)(2,1)S(1)} %get-tuple-element.57.refs_2_, ...), custom_call_target="tpu_custom_call" | custom-call | flops 4362076160 | bytes 13631488 | tf_op jit(solution)/shard_map/pallas_call | solution.py:45
  83.1 0.4 collective-permute-start.18
  83.5 0.5 shard_map.129.refs_0_
  84.0 2.4 %collective-permute-done.16.refs_1_ = bf16[2,2,40,1024]{3,2,1,0:T(8,128)(2,1)S(1)} collective-permute-done((bf16[2,2,40,1024]{3,2,1,0:T(8,128)(2,1)S(1)}, bf16[2,2,40,1024]{3,2,1,0:T(8,128)(2,1)S(1)}, u32[]{:S(2)}, u32[]{:S(2)}) %collective-permute-start.16) | collective-permute-done | bytes 327712 | tf_op jit(solution)/shard_map/ppermute | solution.py:361
  86.4 0.4 collective-permute-start.17
  86.8 5.5 %shard_map.130 = (bf16[2048,3328]{1,0:T(8,128)(2,1)}, f32[8,128]{1,0:T(8,128)S(1)}) custom-call(bf16[2048,320]{1,0:T(8,128)(2,1)S(1)} %shard_map.129.refs_0_, bf16[320,3328]{1,0:T(8,128)(2,1)S(1)} %get-tuple-element.49.refs_0_.refs_1_, bf16[2,40,1024]{2,1,0:T(8,128)(2,1)S(1)} %get-tuple-element.56.refs_2_), custom_call_target="tpu_custom_call" | custom-call | flops 2181038080 | bytes 6815744 | tf_op jit(solution)/shard_map/pallas_call | solution.py:45
  92.3 1.4 %collective-permute-done.18.refs_1_ = bf16[2,2,40,1024]{3,2,1,0:T(8,128)(2,1)S(1)} collective-permute-done((bf16[2,2,40,1024]{3,2,1,0:T(8,128)(2,1)S(1)}, bf16[2,2,40,1024]{3,2,1,0:T(8,128)(2,1)S(1)}, u32[]{:S(2)}, u32[]{:S(2)}) %collective-permute-start.18) | collective-permute-done | bytes 327712 | tf_op jit(solution)/shard_map/ppermute | solution.py:361
  93.7 0.6 collective-permute-start.20
  94.4 1.7 %collective-permute-done.17.refs_3_.refs_1_ = bf16[2,40,1024]{2,1,0:T(8,128)(2,1)S(1)} collective-permute-done((bf16[2,40,1024]{2,1,0:T(8,128)(2,1)S(1)}, bf16[2,40,1024]{2,1,0:T(8,128)(2,1)S(1)}, u32[]{:S(2)}, u32[]{:S(2)}) %collective-permute-start.17) | collective-permute-done | bytes 163872 | tf_op jit(solution)/shard_map/ppermute | solution.py:361
  96.1 5.5 %shard_map.132 = (bf16[2048,3328]{1,0:T(8,128)(2,1)}, f32[8,128]{1,0:T(8,128)S(1)}) custom-call(bf16[2048,320]{1,0:T(8,128)(2,1)S(1)} %shard_map.129.refs_0_, bf16[320,3328]{1,0:T(8,128)(2,1)S(1)} %get-tuple-element.49.refs_0_.refs_1_, bf16[2048,3328]{1,0:T(8,128)(2,1)} %get-tuple-element.65.refs_2_, ...), custom_call_target="tpu_custom_call", output_to_operand_aliasing={{0}: (2, {})} | custom-call | flops 2181038080 | bytes 6815744 | tf_op jit(solution)/shard_map/pallas_call | solution.py:45
  101.6 0.0 collective-permute-done.20.refs_3_
  101.7 0.8 collective-permute-start.21
  102.5 11.7 %shard_map.134 = (bf16[2048,3328]{1,0:T(8,128)(2,1)}, f32[8,128]{1,0:T(8,128)}) custom-call(bf16[2048,320]{1,0:T(8,128)(2,1)S(1)} %shard_map.129.refs_0_, bf16[320,3328]{1,0:T(8,128)(2,1)S(1)} %get-tuple-element.50.refs_1_, bf16[1,40,2048]{2,1,0:T(8,128)(2,1)S(1)} %get-tuple-element.68.refs_2_), custom_call_target="tpu_custom_call" | custom-call | flops 4362076160 | bytes 13631488 | tf_op jit(solution)/shard_map/pallas_call | solution.py:45
  114.2 0.0 collective-permute-done.21
  114.2 0.7 add_bitcast_fusion
  (22 shorter events, 0.2 us)
Async XLA Ops:
  0.6 12.1 %collective-permute-start = (bf16[1,40,2048]{2,1,0:T(8,128)(2,1)}, bf16[1,40,2048]{2,1,0:T(8,128)(2,1)S(1)}, u32[]{:S(2)}, u32[]{:S(2)}) collective-permute-start(bf16[1,40,2048]{2,1,0:T(8,128)(2,1)} %bitcast.9), channel_id=1, source_target_pairs={{0,16},{4,20},{8,24},{12,28},{16,0},{20,4},{24,8},{28,12},{1,17},{... | collective-permute-start | bytes 491528 | tf_op jit(solution)/shard_map/ppermute | solution.py:361
  4.7 8.2 %collective-permute-start.1 = (bf16[1,40,2048]{2,1,0:T(8,128)(2,1)}, bf16[1,40,2048]{2,1,0:T(8,128)(2,1)S(1)}, u32[]{:S(2)}, u32[]{:S(2)}) collective-permute-start(bf16[1,40,2048]{2,1,0:T(8,128)(2,1)} %bitcast.10), channel_id=1, source_target_pairs={{0,8},{4,12},{8,0},{12,4},{16,24},{20,28},{24,16},{28,20},{1,9},{5... | collective-permute-start | bytes 491528 | tf_op jit(solution)/shard_map/ppermute | solution.py:361
  7.0 7.6 %copy-start.6 = (bf16[40,2048]{1,0:T(8,128)(2,1)S(1)}, bf16[40,2048]{1,0:T(8,128)(2,1)}, u32[]{:S(2)}) copy-start(bf16[40,2048]{1,0:T(8,128)(2,1)} %param.9) | copy-start | bytes 491524
  13.0 5.4 %collective-permute-start.2 = (bf16[1,40,2048]{2,1,0:T(8,128)(2,1)S(1)}, bf16[1,40,2048]{2,1,0:T(8,128)(2,1)S(1)}, u32[]{:S(2)}, u32[]{:S(2)}) collective-permute-start(bf16[1,40,2048]{2,1,0:T(8,128)(2,1)S(1)} %shard_map.112.refs_1_), channel_id=1, source_target_pairs={{0,8},{4,12},{8,0},{12,4},{16,24},{20,28},{24,16},{28,20},{1,9},{5... | collective-permute-start | bytes 491528 | tf_op jit(solution)/shard_map/ppermute | solution.py:361
  14.5 7.1 %collective-permute-start.3 = (bf16[1,40,2048]{2,1,0:T(8,128)(2,1)S(1)}, bf16[1,40,2048]{2,1,0:T(8,128)(2,1)S(1)}, u32[]{:S(2)}, u32[]{:S(2)}) collective-permute-start(bf16[1,40,2048]{2,1,0:T(8,128)(2,1)S(1)} %bitcast.11), channel_id=1, source_target_pairs={{0,4},{4,0},{8,12},{12,8},{16,20},{20,16},{24,28},{28,24},{1,5},{5... | collective-permute-start | bytes 491528 | tf_op jit(solution)/shard_map/ppermute | solution.py:361
  16.0 9.2 %collective-permute-start.4 = (bf16[1,40,2048]{2,1,0:T(8,128)(2,1)S(1)}, bf16[1,40,2048]{2,1,0:T(8,128)(2,1)S(1)}, u32[]{:S(2)}, u32[]{:S(2)}) collective-permute-start(bf16[1,40,2048]{2,1,0:T(8,128)(2,1)S(1)} %shard_map.112.refs_1_), channel_id=1, source_target_pairs={{0,4},{4,0},{8,12},{12,8},{16,20},{20,16},{24,28},{28,24},{1,5},{5... | collective-permute-start | bytes 491528 | tf_op jit(solution)/shard_map/ppermute | solution.py:361
  16.5 11.6 %collective-permute-start.5 = (bf16[1,40,2048]{2,1,0:T(8,128)(2,1)S(1)}, bf16[1,40,2048]{2,1,0:T(8,128)(2,1)S(1)}, u32[]{:S(2)}, u32[]{:S(2)}) collective-permute-start(bf16[1,40,2048]{2,1,0:T(8,128)(2,1)S(1)} %collective-permute-done.1.refs_2_), channel_id=1, source_target_pairs={{0,4},{4,0},{8,12},{12,8},{16,20},{20,16},{24,28},{28,24},{1,5},{5... | collective-permute-start | bytes 491528 | tf_op jit(solution)/shard_map/ppermute | solution.py:361
  18.4 11.6 %collective-permute-start.6 = (bf16[1,40,2048]{2,1,0:T(8,128)(2,1)S(1)}, bf16[1,40,2048]{2,1,0:T(8,128)(2,1)S(1)}, u32[]{:S(2)}, u32[]{:S(2)}) collective-permute-start(bf16[1,40,2048]{2,1,0:T(8,128)(2,1)S(1)} %collective-permute-done.2.refs_3_), channel_id=1, source_target_pairs={{0,4},{4,0},{8,12},{12,8},{16,20},{20,16},{24,28},{28,24},{1,5},{5... | collective-permute-start | bytes 491528 | tf_op jit(solution)/shard_map/ppermute | solution.py:361
  35.2 2.1 %copy-start.7 = (bf16[40,2048]{1,0:T(8,128)(2,1)S(1)}, bf16[40,2048]{1,0:T(8,128)(2,1)}, u32[]{:S(2)}) copy-start(bf16[40,2048]{1,0:T(8,128)(2,1)} %param.8) | copy-start | bytes 491524
  35.2 2.0 %collective-permute-start.9 = (bf16[160,1664]{1,0:T(8,128)(2,1)S(1)}, bf16[160,1664]{1,0:T(8,128)(2,1)S(1)}, u32[]{:S(2)}, u32[]{:S(2)}) collective-permute-start(bf16[160,1664]{1,0:T(8,128)(2,1)S(1)} %get-tuple-element.47), channel_id=1, source_target_pairs={{0,1},{1,0},{2,3},{3,2},{4,5},{5,4},{6,7},{7,6},{8,9},{9,8},{10,11... | collective-permute-start | bytes 1597448 | tf_op jit(solution)/shard_map/ppermute | solution.py:361
  35.3 5.4 %collective-permute-start.7 = (bf16[160,1664]{1,0:T(8,128)(2,1)S(1)}, bf16[160,1664]{1,0:T(8,128)(2,1)S(1)}, u32[]{:S(2)}, u32[]{:S(2)}) collective-permute-start(bf16[160,1664]{1,0:T(8,128)(2,1)S(1)} %get-tuple-element.41.refs_3_), channel_id=1, source_target_pairs={{0,1},{1,0},{2,3},{3,2},{4,5},{5,4},{6,7},{7,6},{8,9},{9,8},{10,11... | collective-permute-start | bytes 1597448 | tf_op jit(solution)/shard_map/ppermute | solution.py:361
  37.2 4.5 %copy-start = (bf16[160,1664]{1,0:T(8,128)(2,1)}, bf16[160,1664]{1,0:T(8,128)(2,1)S(1)}, u32[]{:S(2)}) copy-start(bf16[160,1664]{1,0:T(8,128)(2,1)S(1)} %collective-permute-done.9.refs_1_) | copy-start | bytes 1597444
  37.2 6.5 %copy-start.4 = (bf16[320,3328]{1,0:T(8,128)(2,1)S(1)}, bf16[320,3328]{1,0:T(8,128)(2,1)}, u32[]{:S(2)}) copy-start(bf16[320,3328]{1,0:T(8,128)(2,1)} %param.10) | copy-start | bytes 6389764
  37.2 6.5 %copy-start.5 = (bf16[320,3328]{1,0:T(8,128)(2,1)S(1)}, bf16[320,3328]{1,0:T(8,128)(2,1)}, u32[]{:S(2)}) copy-start(bf16[320,3328]{1,0:T(8,128)(2,1)} %param.11) | copy-start | bytes 6389764
  37.4 11.2 %collective-permute-start.10 = (bf16[1,40,2048]{2,1,0:T(8,128)(2,1)S(1)}, bf16[1,40,2048]{2,1,0:T(8,128)(2,1)S(1)}, u32[]{:S(2)}, u32[]{:S(2)}) collective-permute-start(bf16[1,40,2048]{2,1,0:T(8,128)(2,1)S(1)} %shard_map.121.refs_0_), channel_id=1, source_target_pairs={{0,16},{4,20},{8,24},{12,28},{16,0},{20,4},{24,8},{28,12},{1,17},{... | collective-permute-start | bytes 491528 | tf_op jit(solution)/shard_map/ppermute | solution.py:361
  40.7 6.1 %copy-start.2 = (bf16[160,1664]{1,0:T(8,128)(2,1)}, bf16[160,1664]{1,0:T(8,128)(2,1)S(1)}, u32[]{:S(2)}) copy-start(bf16[160,1664]{1,0:T(8,128)(2,1)S(1)} %collective-permute-done.7.refs_1_) | copy-start | bytes 1597444
  41.7 22.0 %collective-permute-start.8 = (bf16[160,1664]{1,0:T(8,128)(2,1)}, bf16[160,1664]{1,0:T(8,128)(2,1)}, u32[]{:S(2)}, u32[]{:S(2)}) collective-permute-start(bf16[160,1664]{1,0:T(8,128)(2,1)} %shard_map.115.refs_4_), channel_id=1, source_target_pairs={{0,2},{1,3},{2,0},{3,1},{4,6},{5,7},{6,4},{7,5},{8,10},{9,11},{10,... | collective-permute-start | bytes 1597448 | tf_op jit(solution)/shard_map/ppermute | solution.py:361
  43.2 24.1 %collective-permute-start.14 = (bf16[160,1664]{1,0:T(8,128)(2,1)S(1)}, bf16[160,1664]{1,0:T(8,128)(2,1)}, u32[]{:S(2)}, u32[]{:S(2)}) collective-permute-start(bf16[160,1664]{1,0:T(8,128)(2,1)S(1)} %shard_map.119.refs_6_.refs_1_), channel_id=1, source_target_pairs={{0,2},{1,3},{2,0},{3,1},{4,6},{5,7},{6,4},{7,5},{8,10},{9,11},{10,... | collective-permute-start | bytes 1597448 | tf_op jit(solution)/shard_map/ppermute | solution.py:361
  48.5 15.1 %copy-start.3 = (bf16[160,1664]{1,0:T(8,128)(2,1)S(1)}, bf16[160,1664]{1,0:T(8,128)(2,1)}, u32[]{:S(2)}) copy-start(bf16[160,1664]{1,0:T(8,128)(2,1)} %copy-done.2) | copy-start | bytes 1597444
  48.6 15.1 %collective-permute-start.11 = (bf16[2,40,2048]{2,1,0:T(8,128)(2,1)S(1)}, bf16[2,40,2048]{2,1,0:T(8,128)(2,1)S(1)}, u32[]{:S(2)}, u32[]{:S(2)}) collective-permute-start(bf16[2,40,2048]{2,1,0:T(8,128)(2,1)S(1)} %shard_map.122), channel_id=1, source_target_pairs={{0,4},{4,0},{8,12},{12,8},{16,20},{20,16},{24,28},{28,24},{1,5},{5... | collective-permute-start | bytes 983048 | tf_op jit(solution)/shard_map/ppermute | solution.py:361
  50.1 13.5 %collective-permute-start.12 = (bf16[2,40,2048]{2,1,0:T(8,128)(2,1)S(1)}, bf16[2,40,2048]{2,1,0:T(8,128)(2,1)S(1)}, u32[]{:S(2)}, u32[]{:S(2)}) collective-permute-start(bf16[2,40,2048]{2,1,0:T(8,128)(2,1)S(1)} %shard_map.122), channel_id=1, source_target_pairs={{0,8},{4,12},{8,0},{12,4},{16,24},{20,28},{24,16},{28,20},{1,9},{5... | collective-permute-start | bytes 983048 | tf_op jit(solution)/shard_map/ppermute | solution.py:361
  63.7 3.6 %copy-start.1 = (bf16[160,1664]{1,0:T(8,128)(2,1)S(1)}, bf16[160,1664]{1,0:T(8,128)(2,1)}, u32[]{:S(2)}) copy-start(bf16[160,1664]{1,0:T(8,128)(2,1)} %copy-done) | copy-start | bytes 1597444
  65.1 5.2 %collective-permute-start.13 = (bf16[2,160,1664]{2,1,0:T(8,128)(2,1)S(1)}, bf16[2,160,1664]{2,1,0:T(8,128)(2,1)S(1)}, u32[]{:S(2)}, u32[]{:S(2)}) collective-permute-start(bf16[2,160,1664]{2,1,0:T(8,128)(2,1)S(1)} %shard_map.123.refs_1_), channel_id=1, source_target_pairs={{0,1},{1,0},{2,3},{3,2},{4,5},{5,4},{6,7},{7,6},{8,9},{9,8},{10,11... | collective-permute-start | bytes 3194888 | tf_op jit(solution)/shard_map/ppermute | solution.py:361
  68.7 2.7 %collective-permute-start.15 = (bf16[2,160,1664]{2,1,0:T(8,128)(2,1)S(1)}, bf16[2,160,1664]{2,1,0:T(8,128)(2,1)S(1)}, u32[]{:S(2)}, u32[]{:S(2)}) collective-permute-start(bf16[2,160,1664]{2,1,0:T(8,128)(2,1)S(1)} %shard_map.124.refs_3_), channel_id=1, source_target_pairs={{0,1},{1,0},{2,3},{3,2},{4,5},{5,4},{6,7},{7,6},{8,9},{9,8},{10,11... | collective-permute-start | bytes 3194888 | tf_op jit(solution)/shard_map/ppermute | solution.py:361
  68.7 14.7 %collective-permute-start.19 = (bf16[2,40,2048]{2,1,0:T(8,128)(2,1)S(1)}, bf16[2,40,2048]{2,1,0:T(8,128)(2,1)S(1)}, u32[]{:S(2)}, u32[]{:S(2)}) collective-permute-start(bf16[2,40,2048]{2,1,0:T(8,128)(2,1)S(1)} %collective-permute-done.12.refs_7_.refs_2_), channel_id=1, source_target_pairs={{0,4},{4,0},{8,12},{12,8},{16,20},{20,16},{24,28},{28,24},{1,5},{5... | collective-permute-start | bytes 983048 | tf_op jit(solution)/shard_map/ppermute | solution.py:361
  76.5 9.8 %collective-permute-start.16 = (bf16[2,2,40,1024]{3,2,1,0:T(8,128)(2,1)S(1)}, bf16[2,2,40,1024]{3,2,1,0:T(8,128)(2,1)S(1)}, u32[]{:S(2)}, u32[]{:S(2)}) collective-permute-start(bf16[2,2,40,1024]{3,2,1,0:T(8,128)(2,1)S(1)} %get-tuple-element.54), channel_id=1, source_target_pairs={{0,4},{4,0},{8,12},{12,8},{16,20},{20,16},{24,28},{28,24},{1,5},{5... | collective-permute-start | bytes 983048 | tf_op jit(solution)/shard_map/ppermute | solution.py:361
  83.1 10.6 %collective-permute-start.18 = (bf16[2,2,40,1024]{3,2,1,0:T(8,128)(2,1)S(1)}, bf16[2,2,40,1024]{3,2,1,0:T(8,128)(2,1)S(1)}, u32[]{:S(2)}, u32[]{:S(2)}) collective-permute-start(bf16[2,2,40,1024]{3,2,1,0:T(8,128)(2,1)S(1)} %get-tuple-element.61), channel_id=1, source_target_pairs={{0,8},{4,12},{8,0},{12,4},{16,24},{20,28},{24,16},{28,20},{1,9},{5... | collective-permute-start | bytes 983048 | tf_op jit(solution)/shard_map/ppermute | solution.py:361
  86.4 9.7 %collective-permute-start.17 = (bf16[2,40,1024]{2,1,0:T(8,128)(2,1)S(1)}, bf16[2,40,1024]{2,1,0:T(8,128)(2,1)S(1)}, u32[]{:S(2)}, u32[]{:S(2)}) collective-permute-start(bf16[2,40,1024]{2,1,0:T(8,128)(2,1)S(1)} %get-tuple-element.56.refs_2_), channel_id=1, source_target_pairs={{0,8},{4,12},{8,0},{12,4},{16,24},{20,28},{24,16},{28,20},{1,9},{5... | collective-permute-start | bytes 491528 | tf_op jit(solution)/shard_map/ppermute | solution.py:361
  93.7 7.9 %collective-permute-start.20 = (bf16[2,40,1024]{2,1,0:T(8,128)(2,1)S(1)}, bf16[2,40,1024]{2,1,0:T(8,128)(2,1)S(1)}, u32[]{:S(2)}, u32[]{:S(2)}) collective-permute-start(bf16[2,40,1024]{2,1,0:T(8,128)(2,1)S(1)} %get-tuple-element.64.refs_4_), channel_id=1, source_target_pairs={{0,4},{4,0},{8,12},{12,8},{16,20},{20,16},{24,28},{28,24},{1,5},{5... | collective-permute-start | bytes 491528 | tf_op jit(solution)/shard_map/ppermute | solution.py:361
  101.7 12.6 %collective-permute-start.21 = (bf16[1,40,2048]{2,1,0:T(8,128)(2,1)S(1)}, bf16[1,40,2048]{2,1,0:T(8,128)(2,1)S(1)}, u32[]{:S(2)}, u32[]{:S(2)}) collective-permute-start(bf16[1,40,2048]{2,1,0:T(8,128)(2,1)S(1)} %get-tuple-element.68.refs_2_), channel_id=1, source_target_pairs={{0,16},{4,20},{8,24},{12,28},{16,0},{20,4},{24,8},{28,12},{1,17},{... | collective-permute-start | bytes 491528 | tf_op jit(solution)/shard_map/ppermute | solution.py:361

commit v3 on v2

--- a/solution.py
+++ b/solution.py
@@ -86,7 +86,7 @@
     blocks, rows, width = gate.shape
     half = blocks // 2
 
-    def kernel(order_ref, places_ref, gate_ref, up_ref, hidden_ref, slope_ref, silu_ref, held, sem):
+    def kernel(order_ref, places_ref, gate_ref, up_ref, turned_ref, slope_ref, silu_ref, held, hidden_ref, sem):
         copies = []
         for i in range(blocks):
             for k, ref in enumerate((gate_ref, up_ref)):
@@ -103,12 +103,14 @@
             if i < half:
                 silu_ref[i] = silu
                 slope_ref[i] = u * sig * (1.0 + g * (1.0 - sig))
+        for at, size in pieces(width, 512):
+            turned_ref[at : at + size] = stack([hidden_ref[i, :, at : at + size] for i in range(blocks)]).T
 
     return call(
         kernel, (order, places, gate, up), [SMEM, SMEM, HBM, HBM], [VMEM] * 3,
-        [struct(gate.shape), struct((half, rows, width), F32), struct((half, rows, width), F32)],
-        (10 * gate.size, 10 * gate.size), 36, after,
-        scratch=[pltpu.VMEM((2, blocks, rows, width), BF), pltpu.SemaphoreType.DMA((2, blocks))],
+        [struct((width, blocks * rows)), struct((half, rows, width), F32), struct((half, rows, width), F32)],
+        (10 * gate.size, 10 * gate.size), 20, after,
+        scratch=[pltpu.VMEM((2, blocks, rows, width), BF), pltpu.VMEM(gate.shape, BF), pltpu.SemaphoreType.DMA((2, blocks))],
     )
 
 
@@ -140,11 +142,11 @@
     )
 
 
-def partial_sum(mine, arrived):
+def partial_sum(mine, arrived, after=()):
     def kernel(mine_ref, arrived_ref, out_ref):
         out_ref[...] = (mine_ref[...] + arrived_ref[...].astype(F32)).astype(BF)
 
-    return call(kernel, (mine, arrived), [VMEM] * 2, [VMEM], [struct(mine.shape)], (mine.size, 8 * mine.size), 8)
+    return call(kernel, (mine, arrived), [VMEM] * 2, [VMEM], [struct(mine.shape)], (mine.size, 8 * mine.size), 8, after)
 
 
 def local_grads(mine, arrived, slope, silu, first, after=()):
@@ -279,11 +281,11 @@
     return out if half else (out, None)
 
 
-def long_product(left, right, begin, end, into=None, after=(), ahead=None, step=512, vmem=24):
+def long_product(left, right, begin, end, into=None, after=(), ahead=None, slots=16, vmem=32):
     height, depth = left.shape
     width = right.shape[1]
-    cuts = [(begin + at, size) for at, size in pieces(end - begin, step)]
-    slots = 2
+    cuts = [(begin + at, size) for at, size in pieces(end - begin, 256)]
+    slots = min(slots, len(cuts))
     ahead = ahead or []
     n = len(ahead)
     m = 0 if into is None else 1
@@ -314,7 +316,7 @@
         kernel, args, [VMEM] * 2 + [HBM] * (n + m), [HBM] + [VMEM] * n,
         [struct((height, width))] + [struct((count, x.shape[1])) for x, _, count in ahead],
         (2 * depth * width * (end - begin), 2 * width * (end - begin)), vmem, after, {len(args) - 1: 0} if m else None,
-        scratch=[pltpu.VMEM((slots, step, width), BF), pltpu.SemaphoreType.DMA((slots,))]
+        scratch=[pltpu.VMEM((slots, 256, width), BF), pltpu.SemaphoreType.DMA((slots,))]
         + ([pltpu.SemaphoreType.DMA((n,))] if n else []),
         mark=True,
     )
@@ -381,37 +383,24 @@
     held = [(own, [0])]
     for m in masks[:0:-1]:
         held.append((swap(stack([x for x, _ in held]), m), [c ^ m for _, cs in held for c in cs]))
+    crossed = swap(own, 1)
     near = [(swap(held[0][0], masks[0]), move(held[0][1], masks[0]))]
     parts = 2 if (units // 2) % 128 == 0 else 1
     width = units // parts
     *weight_rows, mark = brought([(down_weight, k * width, width) for k in range(parts)], 34, (order, places))
-    held = held[:1] + [(hold(x, (mark, near[0][0])), cs) for x, cs in held[1:]]
+    held = held[:1] + [(hold(x, (mark, near[0][0], crossed)), cs) for x, cs in held[1:]]
     near += [(swap(x, masks[0]), move(cs, masks[0])) for x, cs in held[1:]]
     held += near
     grads = Blocks()
-    for x, cs in held + [(swap(x, 1), move(cs, 1)) for x, cs in held]:
+    for x, cs in held + [(crossed, [1])] + [(swap(x, 1), move(cs, 1)) for x, cs in held[1:]]:
         grads.add(x, cs)
-    all_grads = stacked(grads, codes)
-
-    def summed(mine, other):
-        arrived = [swap(other, 1, "col")]
-        sent, m = None, 2
-        while m < n_col:
-            if len(arrived) > 1:
-                mine = mine + arrived.pop(0).astype(F32)
-            sent = partial_sum(mine, arrived[-1])
-            arrived.append(swap(sent, m, "col"))
-            m *= 2
-        return mine, arrived, sent
-
-    sums = []
-    for k in range(parts):
-        after = (sums[-1][1],) if k else ()
-        sums.append(hidden_part(core, all_grads, weight_rows[k], after))
-    sums = [summed(*x) for x in sums]
+    hidden_turned, slope, silu = factors(
+        order, places, gate_saved.reshape(n_row, rows, units), up_saved.reshape(n_row, rows, units), (near[-1][0],)
+    )
+    all_grads = stacked(grads, codes, (hidden_turned,))
 
     all_tokens = Blocks()
-    held = [(hold(tokens.reshape(1, rows, features), (sums[-1][2],)), [0])]
+    held = [(hold(tokens.reshape(1, rows, features), (near[-1][0],)), [0])]
     for m in masks[::-1]:
         joined = laid([x for x, _ in held])
         held.append((swap(joined, m), [c ^ m for _, cs in held for c in cs]))
@@ -420,17 +409,31 @@
     for x, cs in held + crossed:
         all_tokens.add(x, cs)
 
-    hidden, slope, silu = factors(
-        order, places, gate_saved.reshape(n_row, rows, units), up_saved.reshape(n_row, rows, units), (sums[0][2],)
-    )
-    hidden_blocks = Blocks()
-    hidden_blocks.add(hidden, codes)
-    hidden_turned = turned(hidden_blocks, codes)
+    def summed(mine, other, after):
+        arrived = [swap(other, 1, "col")]
+        sent, m = None, 2
+        while m < n_col:
+            if len(arrived) > 1:
+                mine = mine + arrived.pop(0).astype(F32)
+            sent = partial_sum(mine, arrived[-1], after)
+            arrived.append(swap(sent, m, "col"))
+            m *= 2
+        return mine, arrived, sent
+
+    sums, after = [], ()
+    for k in range(parts):
+        sums.append(hidden_part(core, all_grads, weight_rows[k], after))
+        after = (sums[-1][1], all_tokens.arrays[1])
+    after = ()
+    for k in range(parts):
+        sums[k] = summed(*sums[k], after)
+        after = (sums[k][2],)
+
     wide = features // 2
     weights = (gate_weight, up_weight)
     down_grad, a, b, c, d, mark = long_product(
         hidden_turned, all_grads, 0, units, None, (sums[-1][2],),
-        [(x, at, wide) for at in (0, wide) for x in weights], 256, 12,
+        [(x, at, wide) for at in (0, wide) for x in weights], 4, 12,
     )
     left_weights, right_weights = (a, b), (c, d)
     pairs = []
@@ -450,12 +453,12 @@
     )
     cut = features // 2 // 512 * 512
     left_got, right_got = swap(left[1], 1), swap(right[1], m)
-    left = fold(left[0], left_got)
+    gate_grad, mark = long_product(tokens_turned, gate, 0, cut, None, (mark,))
+    left = fold(left[0], left_got, (mark,))
     left_got = swap(left[1], m)
-    gate_grad, mark = long_product(tokens_turned, gate, 0, cut, None, (left[1],))
     right = fold(right[0], right_got, (mark,))
     right_got = swap(right[1], 1)
-    gate_grad, mark = long_product(tokens_turned, gate, cut, features, gate_grad, (left_got, right[1]))
+    gate_grad, mark = long_product(tokens_turned, gate, cut, features, gate_grad, (left[1], right[1]))
     total, sent = join(left[0], left_got, right[0], right_got, (mark,))
     for k, m in enumerate(masks[:0:-1]):
         if k > 0:

time: 115 us -> 102 us (0.89)
  waiting for transfers between devices: 22.4 us -> 14 us
  Pallas kernels: 64.9 us -> 57.8 us
  starting transfers between devices: 25.3 us -> 27.7 us
    ppermute x22, waiting for transfers between devices: 22.4 us -> 14 us  [swap(): return lax.ppermute(x, axis, [(i, i ^ mask) for i in range(n)])]
    pallas_call x24 -> x23, Pallas kernels: 64.9 us -> 57.8 us  [call(): pl.pallas_call(body, out_shape=list(out_shape) + [struct((8, 128), F32)]...]
    ppermute x22, starting transfers between devices: 25.3 us -> 27.7 us  [swap(): return lax.ppermute(x, axis, [(i, i ^ mask) for i in range(n)])]
  transfers between devices with their start and end apart: 22 -> 22, of which waited for: 14 -> 6; matrix products, arithmetic and copies ran while one was open for 1% -> 1% of each run, Pallas kernels for 52% -> 57%
where the time goes in v3:
time: 102 us
  Pallas kernels  57.8 us (57%)
  starting transfers between devices  27.7 us (27%)
  waiting for transfers between devices  14 us (14%)
  other arithmetic  1.34 us (1%)
    pallas_call x23, Pallas kernels, call(): pl.pallas_call(body, out_shape=list(out_shape) + [struct((8, 128), F32)]...  57.8 us
    ppermute x22, starting transfers between devices, swap(): return lax.ppermute(x, axis, [(i, i ^ mask) for i in range(n)])  27.7 us
    ppermute x22, waiting for transfers between devices, swap(): return lax.ppermute(x, axis, [(i, i ^ mask) for i in range(n)])  14 us
  transfers between devices with their start and end apart: 22, of which 6 were waited for; matrix products, arithmetic and copies ran while one was open for 1% of the time, Pallas kernels for 57%

profile of v3, /device:TPU:0, one launch (start us, length us, event | category | flops | bytes accessed | tf_op | source)
XLA Modules:
  0.0 101.7 jit_solution(4707442368747109673)
XLA Ops:
  0.6 4.1 %collective-permute-start = (bf16[1,40,2048]{2,1,0:T(8,128)(2,1)}, bf16[1,40,2048]{2,1,0:T(8,128)(2,1)S(1)}, u32[]{:S(2)}, u32[]{:S(2)}) collective-permute-start(bf16[1,40,2048]{2,1,0:T(8,128)(2,1)} %bitcast.9), channel_id=1, source_target_pairs={{0,16},{4,20},{8,24},{12,28},{16,0},{20,4},{24,8},{28,12},{1,17},{... | collective-permute-start | bytes 491528 | tf_op jit(solution)/shard_map/ppermute | solution.py:363
  4.7 1.6 %collective-permute-start.1 = (bf16[1,40,2048]{2,1,0:T(8,128)(2,1)}, bf16[1,40,2048]{2,1,0:T(8,128)(2,1)S(1)}, u32[]{:S(2)}, u32[]{:S(2)}) collective-permute-start(bf16[1,40,2048]{2,1,0:T(8,128)(2,1)} %bitcast.10), channel_id=1, source_target_pairs={{0,8},{4,12},{8,0},{12,4},{16,24},{20,28},{24,16},{28,20},{1,9},{5... | collective-permute-start | bytes 491528 | tf_op jit(solution)/shard_map/ppermute | solution.py:363
  6.3 1.5 %collective-permute-start.2 = (bf16[1,40,2048]{2,1,0:T(8,128)(2,1)}, bf16[1,40,2048]{2,1,0:T(8,128)(2,1)S(1)}, u32[]{:S(2)}, u32[]{:S(2)}) collective-permute-start(bf16[1,40,2048]{2,1,0:T(8,128)(2,1)} %bitcast.11), channel_id=1, source_target_pairs={{0,4},{4,0},{8,12},{12,8},{16,20},{20,16},{24,28},{28,24},{1,5},{5... | collective-permute-start | bytes 491528 | tf_op jit(solution)/shard_map/ppermute | solution.py:363
  7.8 0.7 iota_xor_fusion
  8.5 5.0 %shard_map.111 = (bf16[1664,2048]{1,0:T(8,128)(2,1)S(1)}, bf16[1664,2048]{1,0:T(8,128)(2,1)S(1)}, f32[8,128]{1,0:T(8,128)S(1)}) custom-call(bf16[3328,2048]{1,0:T(8,128)(2,1)} %refs_1_.1, bf16[3328,2048]{1,0:T(8,128)(2,1)} %refs_1_.1, s32[8]{0:T(128)S(1)} %get-tuple-element.75.refs_2_.refs_0_, s32[8]{0:T(128)S(1)} %get-tuple-element.74.refs_3_.refs_1_), custom_call_target="tpu_custom_call" | custom-call | bytes 13631488 | tf_op jit(solution)/shard_map/pallas_call | solution.py:45
  13.5 0.0 collective-permute-done.refs_0_
  13.5 0.0 collective-permute-done.1.refs_2_
  13.5 0.0 collective-permute-done.2.refs_3_.refs_4_
  13.6 0.0 copy-start.2
  13.6 0.9 collective-permute-start.3
  14.5 1.5 %collective-permute-start.4 = (bf16[1,40,2048]{2,1,0:T(8,128)(2,1)S(1)}, bf16[1,40,2048]{2,1,0:T(8,128)(2,1)S(1)}, u32[]{:S(2)}, u32[]{:S(2)}) collective-permute-start(bf16[1,40,2048]{2,1,0:T(8,128)(2,1)S(1)} %shard_map.112.refs_1_), channel_id=1, source_target_pairs={{0,4},{4,0},{8,12},{12,8},{16,20},{20,16},{24,28},{28,24},{1,5},{5... | collective-permute-start | bytes 491528 | tf_op jit(solution)/shard_map/ppermute | solution.py:363
  16.0 0.5 collective-permute-start.5
  16.6 2.4 %collective-permute-done.3.refs_4_.refs_3_.refs_1_ = bf16[1,40,2048]{2,1,0:T(8,128)(2,1)S(1)} collective-permute-done((bf16[1,40,2048]{2,1,0:T(8,128)(2,1)S(1)}, bf16[1,40,2048]{2,1,0:T(8,128)(2,1)S(1)}, u32[]{:S(2)}, u32[]{:S(2)}) %collective-permute-start.3) | collective-permute-done | bytes 163872 | tf_op jit(solution)/shard_map/ppermute | solution.py:363
  19.0 0.9 collective-permute-start.6
  19.9 2.9 %collective-permute-start.9 = (bf16[1,40,2048]{2,1,0:T(8,128)(2,1)S(1)}, bf16[1,40,2048]{2,1,0:T(8,128)(2,1)S(1)}, u32[]{:S(2)}, u32[]{:S(2)}) collective-permute-start(bf16[1,40,2048]{2,1,0:T(8,128)(2,1)S(1)} %shard_map.117.refs_0_), channel_id=1, source_target_pairs={{0,16},{4,20},{8,24},{12,28},{16,0},{20,4},{24,8},{28,12},{1,17},{... | collective-permute-start | bytes 491528 | tf_op jit(solution)/shard_map/ppermute | solution.py:363
  22.8 3.7 %shard_map.113 = (bf16[3328,320]{1,0:T(8,128)(2,1)S(1)}, f32[4,40,3328]{2,1,0:T(8,128)S(1)}, f32[4,40,3328]{2,1,0:T(8,128)S(1)}) custom-call(s32[8]{0:T(128)S(1)} %get-tuple-element.75.refs_2_.refs_0_, s32[8]{0:T(128)S(1)} %get-tuple-element.74.refs_3_.refs_1_, bf16[8,40,3328]{2,1,0:T(8,128)(2,1)S(1)} %bitcast.7, bf16[8,40,3328]{2,1,0:T(8,128)(2,1)S(1)} %bitcast.8, ...), custom_call_target="tpu_custom_call" | custom-call | flops 10649600 | bytes 10649600 | tf_op jit(solution)/shard_map/pallas_call | solution.py:45
  26.5 0.0 collective-permute-done.4.refs_5_
  26.5 0.0 collective-permute-done.5.refs_6_
  26.5 0.0 collective-permute-done.6.refs_7_
  26.5 0.1 shard_map.114.refs_1_
  26.6 2.6 %shard_map.115 = (f32[160,1664]{1,0:T(8,128)S(1)}, bf16[160,1664]{1,0:T(8,128)(2,1)S(1)}) custom-call(s32[1]{0:T(128)} %bitcast.refs_0_, bf16[320,2048]{1,0:T(8,128)(2,1)S(1)} %shard_map.114.refs_1_, bf16[1664,2048]{1,0:T(8,128)(2,1)S(1)} %get-tuple-element.41.refs_2_), custom_call_target="tpu_custom_call" | custom-call | flops 2181038080 | bytes 6815744 | tf_op jit(solution)/shard_map/pallas_call | solution.py:45
  29.3 0.1 collective-permute-start.7
  29.4 0.5 collective-permute-done.9.refs_4_.refs_1_
  29.9 2.6 %shard_map.118 = (f32[160,1664]{1,0:T(8,128)S(1)}, bf16[160,1664]{1,0:T(8,128)(2,1)S(1)}) custom-call(s32[1]{0:T(128)} %bitcast.refs_0_, bf16[320,2048]{1,0:T(8,128)(2,1)S(1)} %shard_map.114.refs_1_, bf16[1664,2048]{1,0:T(8,128)(2,1)S(1)} %get-tuple-element.46.refs_2_, bf16[160,1664]{1,0:T(8,128)(2,1)S(1)} %get-tuple-element.43.refs_3_, ...), custom_call_target="tpu_custom_call" | custom-call | flops 2181038080 | bytes 6815744 | tf_op jit(solution)/shard_map/pallas_call | solution.py:45
  32.5 0.1 collective-permute-start.10
  32.6 0.0 collective-permute-done.7.refs_1_
  32.6 0.1 shard_map.116.refs_2_
  32.7 1.6 %collective-permute-start.8 = (bf16[160,1664]{1,0:T(8,128)(2,1)S(1)}, bf16[160,1664]{1,0:T(8,128)(2,1)S(1)}, u32[]{:S(2)}, u32[]{:S(2)}) collective-permute-start(bf16[160,1664]{1,0:T(8,128)(2,1)S(1)} %shard_map.116.refs_2_), channel_id=1, source_target_pairs={{0,2},{1,3},{2,0},{3,1},{4,6},{5,7},{6,4},{7,5},{8,10},{9,11},{10,... | collective-permute-start | bytes 1597448 | tf_op jit(solution)/shard_map/ppermute | solution.py:363
  34.3 0.2 collective-permute-done.10.refs_1_
  34.5 0.1 shard_map.119.refs_6_
  34.6 1.6 %collective-permute-start.14 = (bf16[160,1664]{1,0:T(8,128)(2,1)S(1)}, bf16[160,1664]{1,0:T(8,128)(2,1)S(1)}, u32[]{:S(2)}, u32[]{:S(2)}) collective-permute-start(bf16[160,1664]{1,0:T(8,128)(2,1)S(1)} %shard_map.119.refs_6_), channel_id=1, source_target_pairs={{0,2},{1,3},{2,0},{3,1},{4,6},{5,7},{6,4},{7,5},{8,10},{9,11},{10,... | collective-permute-start | bytes 1597448 | tf_op jit(solution)/shard_map/ppermute | solution.py:363
  36.2 1.1 %collective-permute-start.11 = (bf16[2,40,2048]{2,1,0:T(8,128)(2,1)S(1)}, bf16[2,40,2048]{2,1,0:T(8,128)(2,1)S(1)}, u32[]{:S(2)}, u32[]{:S(2)}) collective-permute-start(bf16[2,40,2048]{2,1,0:T(8,128)(2,1)S(1)} %shard_map.121), channel_id=1, source_target_pairs={{0,4},{4,0},{8,12},{12,8},{16,20},{20,16},{24,28},{28,24},{1,5},{5... | collective-permute-start | bytes 983048 | tf_op jit(solution)/shard_map/ppermute | solution.py:363
  37.3 0.9 collective-permute-start.12
  38.1 13.6 %shard_map.120 = (bf16[3328,2048]{1,0:T(8,128)(2,1)}, bf16[1024,3328]{1,0:T(8,128)(2,1)S(1)}, bf16[1024,3328]{1,0:T(8,128)(2,1)S(1)}, bf16[1024,3328]{1,0:T(8,12...) custom-call(bf16[3328,320]{1,0:T(8,128)(2,1)S(1)} %get-tuple-element.40.refs_8_.refs_0_, ...), custom_call_target="tpu_custom_call" | custom-call | flops 4362076160 | bytes 13631488 | tf_op jit(solution)/shard_map/pallas_call | solution.py:45
  51.7 0.0 collective-permute-done.11.refs_6_.refs_3_
  51.8 0.0 collective-permute-done.12.refs_7_.refs_2_
  51.8 0.0 collective-permute-done.8.refs_2_
  51.8 0.4 shard_map.122.refs_1_
  52.2 0.1 collective-permute-start.13
  52.3 6.4 %collective-permute-done.14.refs_2_ = bf16[160,1664]{1,0:T(8,128)(2,1)S(1)} collective-permute-done((bf16[160,1664]{1,0:T(8,128)(2,1)S(1)}, bf16[160,1664]{1,0:T(8,128)(2,1)S(1)}, u32[]{:S(2)}, u32[]{:S(2)}) %collective-permute-start.14) | collective-permute-done | bytes 532512 | tf_op jit(solution)/shard_map/ppermute | solution.py:363
  58.7 0.4 shard_map.123.refs_3_
  59.0 0.1 collective-permute-start.15
  59.1 0.9 collective-permute-start.17
  60.0 0.0 collective-permute-done.13.refs_2_
  60.0 1.7 %collective-permute-done.15.refs_4_ = bf16[2,160,1664]{2,1,0:T(8,128)(2,1)S(1)} collective-permute-done((bf16[2,160,1664]{2,1,0:T(8,128)(2,1)S(1)}, bf16[2,160,1664]{2,1,0:T(8,128)(2,1)S(1)}, u32[]{:S(2)}, u32[]{:S(2)}) %collective-permute-start.15) | collective-permute-done | bytes 1064992 | tf_op jit(solution)/shard_map/ppermute | solution.py:363
  61.8 0.3 shard_map.124
  62.1 4.6 %shard_map.125 = (bf16[2,2,40,1024]{3,2,1,0:T(8,128)(2,1)S(1)}, bf16[2,2,40,1024]{3,2,1,0:T(8,128)(2,1)S(1)}, f32[8,128]{1,0:T(8,128)S(1)}) custom-call(bf16[320,3328]{1,0:T(8,128)(2,1)S(1)} %get-tuple-element.50.refs_0_.refs_1_, bf16[320,3328]{1,0:T(8,128)(2,1)S(1)} %get-tuple-element.51.refs_1_, bf16[1024,3328]{1,0:T(8,128)(2,1)S(1)} %get-tuple-element.52.refs_2_, ...), custom_call_target="tpu_custom_call" | custom-call | flops 4362076160 | bytes 13631488 | tf_op jit(solution)/shard_map/pallas_call | solution.py:45
  66.7 0.9 collective-permute-start.16
  67.6 4.6 %shard_map.127 = (bf16[2,2,40,1024]{3,2,1,0:T(8,128)(2,1)S(1)}, bf16[2,2,40,1024]{3,2,1,0:T(8,128)(2,1)S(1)}, f32[8,128]{1,0:T(8,128)S(1)}) custom-call(bf16[320,3328]{1,0:T(8,128)(2,1)S(1)} %get-tuple-element.50.refs_0_.refs_1_, bf16[320,3328]{1,0:T(8,128)(2,1)S(1)} %get-tuple-element.51.refs_1_, bf16[1024,3328]{1,0:T(8,128)(2,1)S(1)} %get-tuple-element.56.refs_2_, ...), custom_call_target="tpu_custom_call" | custom-call | flops 4362076160 | bytes 13631488 | tf_op jit(solution)/shard_map/pallas_call | solution.py:45
  72.2 0.9 collective-permute-start.19
  73.1 0.0 collective-permute-done.17.refs_4_
  73.1 0.5 shard_map.126.refs_0_
  73.6 5.0 %shard_map.128 = (bf16[2048,3328]{1,0:T(8,128)(2,1)}, f32[8,128]{1,0:T(8,128)S(1)}) custom-call(bf16[2048,320]{1,0:T(8,128)(2,1)S(1)} %shard_map.126.refs_0_, bf16[320,3328]{1,0:T(8,128)(2,1)S(1)} %get-tuple-element.50.refs_0_.refs_1_, f32[8,128]{1,0:T(8,128)S(1)} %get-tuple-element.59.refs_2_), custom_call_target="tpu_custom_call" | custom-call | flops 2181038080 | bytes 6815744 | tf_op jit(solution)/shard_map/pallas_call | solution.py:45
  78.6 0.0 collective-permute-done.16.refs_1_
  78.6 1.2 %collective-permute-start.18 = (bf16[2,40,1024]{2,1,0:T(8,128)(2,1)S(1)}, bf16[2,40,1024]{2,1,0:T(8,128)(2,1)S(1)}, u32[]{:S(2)}, u32[]{:S(2)}) collective-permute-start(bf16[2,40,1024]{2,1,0:T(8,128)(2,1)S(1)} %get-tuple-element.62.refs_3_), channel_id=1, source_target_pairs={{0,8},{4,12},{8,0},{12,4},{16,24},{20,28},{24,16},{28,20},{1,9},{5... | collective-permute-start | bytes 491528 | tf_op jit(solution)/shard_map/ppermute | solution.py:363
  79.9 2.7 %collective-permute-done.19.refs_1_ = bf16[2,2,40,1024]{3,2,1,0:T(8,128)(2,1)S(1)} collective-permute-done((bf16[2,2,40,1024]{3,2,1,0:T(8,128)(2,1)S(1)}, bf16[2,2,40,1024]{3,2,1,0:T(8,128)(2,1)S(1)}, u32[]{:S(2)}, u32[]{:S(2)}) %collective-permute-start.19) | collective-permute-done | bytes 327712 | tf_op jit(solution)/shard_map/ppermute | solution.py:363
  82.6 0.9 collective-permute-start.20
  83.4 5.0 %shard_map.131 = (bf16[2048,3328]{1,0:T(8,128)(2,1)}, f32[8,128]{1,0:T(8,128)S(1)}) custom-call(bf16[2048,320]{1,0:T(8,128)(2,1)S(1)} %shard_map.126.refs_0_, bf16[320,3328]{1,0:T(8,128)(2,1)S(1)} %get-tuple-element.50.refs_0_.refs_1_, bf16[2048,3328]{1,0:T(8,128)(2,1)} %get-tuple-element.67.refs_2_, ...), custom_call_target="tpu_custom_call", output_to_operand_aliasing={{0}: (2, {})} | custom-call | flops 2181038080 | bytes 6815744 | tf_op jit(solution)/shard_map/pallas_call | solution.py:45
  88.4 0.0 collective-permute-done.18.refs_1_
  88.4 0.0 collective-permute-done.20.refs_3_
  88.5 3.4 %collective-permute-start.21 = (bf16[1,40,2048]{2,1,0:T(8,128)(2,1)S(1)}, bf16[1,40,2048]{2,1,0:T(8,128)(2,1)S(1)}, u32[]{:S(2)}, u32[]{:S(2)}) collective-permute-start(bf16[1,40,2048]{2,1,0:T(8,128)(2,1)S(1)} %get-tuple-element.70.refs_2_), channel_id=1, source_target_pairs={{0,16},{4,20},{8,24},{12,28},{16,0},{20,4},{24,8},{28,12},{1,17},{... | collective-permute-start | bytes 491528 | tf_op jit(solution)/shard_map/ppermute | solution.py:363
  91.9 9.2 %shard_map.133 = (bf16[2048,3328]{1,0:T(8,128)(2,1)}, f32[8,128]{1,0:T(8,128)}) custom-call(bf16[2048,320]{1,0:T(8,128)(2,1)S(1)} %shard_map.126.refs_0_, bf16[320,3328]{1,0:T(8,128)(2,1)S(1)} %get-tuple-element.51.refs_1_, bf16[1,40,2048]{2,1,0:T(8,128)(2,1)S(1)} %get-tuple-element.70.refs_2_), custom_call_target="tpu_custom_call" | custom-call | flops 4362076160 | bytes 13631488 | tf_op jit(solution)/shard_map/pallas_call | solution.py:45
  101.0 0.0 collective-permute-done.21
  101.0 0.7 add_bitcast_fusion
  (13 shorter events, 0.2 us)
Async XLA Ops:
  0.6 12.9 %collective-permute-start = (bf16[1,40,2048]{2,1,0:T(8,128)(2,1)}, bf16[1,40,2048]{2,1,0:T(8,128)(2,1)S(1)}, u32[]{:S(2)}, u32[]{:S(2)}) collective-permute-start(bf16[1,40,2048]{2,1,0:T(8,128)(2,1)} %bitcast.9), channel_id=1, source_target_pairs={{0,16},{4,20},{8,24},{12,28},{16,0},{20,4},{24,8},{28,12},{1,17},{... | collective-permute-start | bytes 491528 | tf_op jit(solution)/shard_map/ppermute | solution.py:363
  4.7 8.8 %collective-permute-start.1 = (bf16[1,40,2048]{2,1,0:T(8,128)(2,1)}, bf16[1,40,2048]{2,1,0:T(8,128)(2,1)S(1)}, u32[]{:S(2)}, u32[]{:S(2)}) collective-permute-start(bf16[1,40,2048]{2,1,0:T(8,128)(2,1)} %bitcast.10), channel_id=1, source_target_pairs={{0,8},{4,12},{8,0},{12,4},{16,24},{20,28},{24,16},{28,20},{1,9},{5... | collective-permute-start | bytes 491528 | tf_op jit(solution)/shard_map/ppermute | solution.py:363
  6.3 7.2 %collective-permute-start.2 = (bf16[1,40,2048]{2,1,0:T(8,128)(2,1)}, bf16[1,40,2048]{2,1,0:T(8,128)(2,1)S(1)}, u32[]{:S(2)}, u32[]{:S(2)}) collective-permute-start(bf16[1,40,2048]{2,1,0:T(8,128)(2,1)} %bitcast.11), channel_id=1, source_target_pairs={{0,4},{4,0},{8,12},{12,8},{16,20},{20,16},{24,28},{28,24},{1,5},{5... | collective-permute-start | bytes 491528 | tf_op jit(solution)/shard_map/ppermute | solution.py:363
  8.5 11.5 %copy-start.3 = (bf16[40,2048]{1,0:T(8,128)(2,1)S(1)}, bf16[40,2048]{1,0:T(8,128)(2,1)}, u32[]{:S(2)}) copy-start(bf16[40,2048]{1,0:T(8,128)(2,1)} %param.8) | copy-start | bytes 491524
  8.5 14.4 %copy-start = (bf16[320,3328]{1,0:T(8,128)(2,1)S(1)}, bf16[320,3328]{1,0:T(8,128)(2,1)}, u32[]{:S(2)}) copy-start(bf16[320,3328]{1,0:T(8,128)(2,1)} %param.10) | copy-start | bytes 6389764
  8.5 14.4 %copy-start.1 = (bf16[320,3328]{1,0:T(8,128)(2,1)S(1)}, bf16[320,3328]{1,0:T(8,128)(2,1)}, u32[]{:S(2)}) copy-start(bf16[320,3328]{1,0:T(8,128)(2,1)} %param.11) | copy-start | bytes 6389764
  13.6 12.9 %copy-start.2 = (bf16[40,2048]{1,0:T(8,128)(2,1)S(1)}, bf16[40,2048]{1,0:T(8,128)(2,1)}, u32[]{:S(2)}) copy-start(bf16[40,2048]{1,0:T(8,128)(2,1)} %param.9) | copy-start | bytes 491524
  13.6 5.4 %collective-permute-start.3 = (bf16[1,40,2048]{2,1,0:T(8,128)(2,1)S(1)}, bf16[1,40,2048]{2,1,0:T(8,128)(2,1)S(1)}, u32[]{:S(2)}, u32[]{:S(2)}) collective-permute-start(bf16[1,40,2048]{2,1,0:T(8,128)(2,1)S(1)} %shard_map.112.refs_1_), channel_id=1, source_target_pairs={{0,8},{4,12},{8,0},{12,4},{16,24},{20,28},{24,16},{28,20},{1,9},{5... | collective-permute-start | bytes 491528 | tf_op jit(solution)/shard_map/ppermute | solution.py:363
  14.5 12.0 %collective-permute-start.4 = (bf16[1,40,2048]{2,1,0:T(8,128)(2,1)S(1)}, bf16[1,40,2048]{2,1,0:T(8,128)(2,1)S(1)}, u32[]{:S(2)}, u32[]{:S(2)}) collective-permute-start(bf16[1,40,2048]{2,1,0:T(8,128)(2,1)S(1)} %shard_map.112.refs_1_), channel_id=1, source_target_pairs={{0,4},{4,0},{8,12},{12,8},{16,20},{20,16},{24,28},{28,24},{1,5},{5... | collective-permute-start | bytes 491528 | tf_op jit(solution)/shard_map/ppermute | solution.py:363
  16.0 10.5 %collective-permute-start.5 = (bf16[1,40,2048]{2,1,0:T(8,128)(2,1)S(1)}, bf16[1,40,2048]{2,1,0:T(8,128)(2,1)S(1)}, u32[]{:S(2)}, u32[]{:S(2)}) collective-permute-start(bf16[1,40,2048]{2,1,0:T(8,128)(2,1)S(1)} %collective-permute-done.1.refs_2_), channel_id=1, source_target_pairs={{0,4},{4,0},{8,12},{12,8},{16,20},{20,16},{24,28},{28,24},{1,5},{5... | collective-permute-start | bytes 491528 | tf_op jit(solution)/shard_map/ppermute | solution.py:363
  19.0 7.5 %collective-permute-start.6 = (bf16[1,40,2048]{2,1,0:T(8,128)(2,1)S(1)}, bf16[1,40,2048]{2,1,0:T(8,128)(2,1)S(1)}, u32[]{:S(2)}, u32[]{:S(2)}) collective-permute-start(bf16[1,40,2048]{2,1,0:T(8,128)(2,1)S(1)} %collective-permute-done.3.refs_4_.refs_3_.refs_1_), channel_id=1, source_target_pairs={{0,4},{4,0},{8,12},{12,8},{16,20},{20,16},{24,28},{28,24},{1,5},{5... | collective-permute-start | bytes 491528 | tf_op jit(solution)/shard_map/ppermute | solution.py:363
  19.9 10.0 %collective-permute-start.9 = (bf16[1,40,2048]{2,1,0:T(8,128)(2,1)S(1)}, bf16[1,40,2048]{2,1,0:T(8,128)(2,1)S(1)}, u32[]{:S(2)}, u32[]{:S(2)}) collective-permute-start(bf16[1,40,2048]{2,1,0:T(8,128)(2,1)S(1)} %shard_map.117.refs_0_), channel_id=1, source_target_pairs={{0,16},{4,20},{8,24},{12,28},{16,0},{20,4},{24,8},{28,12},{1,17},{... | collective-permute-start | bytes 491528 | tf_op jit(solution)/shard_map/ppermute | solution.py:363
  29.3 3.3 %collective-permute-start.7 = (bf16[160,1664]{1,0:T(8,128)(2,1)S(1)}, bf16[160,1664]{1,0:T(8,128)(2,1)S(1)}, u32[]{:S(2)}, u32[]{:S(2)}) collective-permute-start(bf16[160,1664]{1,0:T(8,128)(2,1)S(1)} %get-tuple-element.43.refs_3_), channel_id=1, source_target_pairs={{0,1},{1,0},{2,3},{3,2},{4,5},{5,4},{6,7},{7,6},{8,9},{9,8},{10,11... | collective-permute-start | bytes 1597448 | tf_op jit(solution)/shard_map/ppermute | solution.py:363
  32.5 2.0 %collective-permute-start.10 = (bf16[160,1664]{1,0:T(8,128)(2,1)S(1)}, bf16[160,1664]{1,0:T(8,128)(2,1)S(1)}, u32[]{:S(2)}, u32[]{:S(2)}) collective-permute-start(bf16[160,1664]{1,0:T(8,128)(2,1)S(1)} %get-tuple-element.48), channel_id=1, source_target_pairs={{0,1},{1,0},{2,3},{3,2},{4,5},{5,4},{6,7},{7,6},{8,9},{9,8},{10,11... | collective-permute-start | bytes 1597448 | tf_op jit(solution)/shard_map/ppermute | solution.py:363
  32.7 19.1 %collective-permute-start.8 = (bf16[160,1664]{1,0:T(8,128)(2,1)S(1)}, bf16[160,1664]{1,0:T(8,128)(2,1)S(1)}, u32[]{:S(2)}, u32[]{:S(2)}) collective-permute-start(bf16[160,1664]{1,0:T(8,128)(2,1)S(1)} %shard_map.116.refs_2_), channel_id=1, source_target_pairs={{0,2},{1,3},{2,0},{3,1},{4,6},{5,7},{6,4},{7,5},{8,10},{9,11},{10,... | collective-permute-start | bytes 1597448 | tf_op jit(solution)/shard_map/ppermute | solution.py:363
  34.6 24.0 %collective-permute-start.14 = (bf16[160,1664]{1,0:T(8,128)(2,1)S(1)}, bf16[160,1664]{1,0:T(8,128)(2,1)S(1)}, u32[]{:S(2)}, u32[]{:S(2)}) collective-permute-start(bf16[160,1664]{1,0:T(8,128)(2,1)S(1)} %shard_map.119.refs_6_), channel_id=1, source_target_pairs={{0,2},{1,3},{2,0},{3,1},{4,6},{5,7},{6,4},{7,5},{8,10},{9,11},{10,... | collective-permute-start | bytes 1597448 | tf_op jit(solution)/shard_map/ppermute | solution.py:363
  36.2 15.5 %collective-permute-start.11 = (bf16[2,40,2048]{2,1,0:T(8,128)(2,1)S(1)}, bf16[2,40,2048]{2,1,0:T(8,128)(2,1)S(1)}, u32[]{:S(2)}, u32[]{:S(2)}) collective-permute-start(bf16[2,40,2048]{2,1,0:T(8,128)(2,1)S(1)} %shard_map.121), channel_id=1, source_target_pairs={{0,4},{4,0},{8,12},{12,8},{16,20},{20,16},{24,28},{28,24},{1,5},{5... | collective-permute-start | bytes 983048 | tf_op jit(solution)/shard_map/ppermute | solution.py:363
  37.3 14.5 %collective-permute-start.12 = (bf16[2,40,2048]{2,1,0:T(8,128)(2,1)S(1)}, bf16[2,40,2048]{2,1,0:T(8,128)(2,1)S(1)}, u32[]{:S(2)}, u32[]{:S(2)}) collective-permute-start(bf16[2,40,2048]{2,1,0:T(8,128)(2,1)S(1)} %shard_map.121), channel_id=1, source_target_pairs={{0,8},{4,12},{8,0},{12,4},{16,24},{20,28},{24,16},{28,20},{1,9},{5... | collective-permute-start | bytes 983048 | tf_op jit(solution)/shard_map/ppermute | solution.py:363
  52.2 7.9 %collective-permute-start.13 = (bf16[2,160,1664]{2,1,0:T(8,128)(2,1)S(1)}, bf16[2,160,1664]{2,1,0:T(8,128)(2,1)S(1)}, u32[]{:S(2)}, u32[]{:S(2)}) collective-permute-start(bf16[2,160,1664]{2,1,0:T(8,128)(2,1)S(1)} %shard_map.122.refs_1_), channel_id=1, source_target_pairs={{0,1},{1,0},{2,3},{3,2},{4,5},{5,4},{6,7},{7,6},{8,9},{9,8},{10,11... | collective-permute-start | bytes 3194888 | tf_op jit(solution)/shard_map/ppermute | solution.py:363
  59.0 2.7 %collective-permute-start.15 = (bf16[2,160,1664]{2,1,0:T(8,128)(2,1)S(1)}, bf16[2,160,1664]{2,1,0:T(8,128)(2,1)S(1)}, u32[]{:S(2)}, u32[]{:S(2)}) collective-permute-start(bf16[2,160,1664]{2,1,0:T(8,128)(2,1)S(1)} %shard_map.123.refs_3_), channel_id=1, source_target_pairs={{0,1},{1,0},{2,3},{3,2},{4,5},{5,4},{6,7},{7,6},{8,9},{9,8},{10,11... | collective-permute-start | bytes 3194888 | tf_op jit(solution)/shard_map/ppermute | solution.py:363
  59.1 14.0 %collective-permute-start.17 = (bf16[2,40,2048]{2,1,0:T(8,128)(2,1)S(1)}, bf16[2,40,2048]{2,1,0:T(8,128)(2,1)S(1)}, u32[]{:S(2)}, u32[]{:S(2)}) collective-permute-start(bf16[2,40,2048]{2,1,0:T(8,128)(2,1)S(1)} %collective-permute-done.12.refs_7_.refs_2_), channel_id=1, source_target_pairs={{0,4},{4,0},{8,12},{12,8},{16,20},{20,16},{24,28},{28,24},{1,5},{5... | collective-permute-start | bytes 983048 | tf_op jit(solution)/shard_map/ppermute | solution.py:363
  66.7 11.9 %collective-permute-start.16 = (bf16[2,2,40,1024]{3,2,1,0:T(8,128)(2,1)S(1)}, bf16[2,2,40,1024]{3,2,1,0:T(8,128)(2,1)S(1)}, u32[]{:S(2)}, u32[]{:S(2)}) collective-permute-start(bf16[2,2,40,1024]{3,2,1,0:T(8,128)(2,1)S(1)} %get-tuple-element.55), channel_id=1, source_target_pairs={{0,4},{4,0},{8,12},{12,8},{16,20},{20,16},{24,28},{28,24},{1,5},{5... | collective-permute-start | bytes 983048 | tf_op jit(solution)/shard_map/ppermute | solution.py:363
  72.2 10.3 %collective-permute-start.19 = (bf16[2,2,40,1024]{3,2,1,0:T(8,128)(2,1)S(1)}, bf16[2,2,40,1024]{3,2,1,0:T(8,128)(2,1)S(1)}, u32[]{:S(2)}, u32[]{:S(2)}) collective-permute-start(bf16[2,2,40,1024]{3,2,1,0:T(8,128)(2,1)S(1)} %get-tuple-element.64), channel_id=1, source_target_pairs={{0,8},{4,12},{8,0},{12,4},{16,24},{20,28},{24,16},{28,20},{1,9},{5... | collective-permute-start | bytes 983048 | tf_op jit(solution)/shard_map/ppermute | solution.py:363
  78.6 9.8 %collective-permute-start.18 = (bf16[2,40,1024]{2,1,0:T(8,128)(2,1)S(1)}, bf16[2,40,1024]{2,1,0:T(8,128)(2,1)S(1)}, u32[]{:S(2)}, u32[]{:S(2)}) collective-permute-start(bf16[2,40,1024]{2,1,0:T(8,128)(2,1)S(1)} %get-tuple-element.62.refs_3_), channel_id=1, source_target_pairs={{0,8},{4,12},{8,0},{12,4},{16,24},{20,28},{24,16},{28,20},{1,9},{5... | collective-permute-start | bytes 491528 | tf_op jit(solution)/shard_map/ppermute | solution.py:363
  82.6 5.9 %collective-permute-start.20 = (bf16[2,40,1024]{2,1,0:T(8,128)(2,1)S(1)}, bf16[2,40,1024]{2,1,0:T(8,128)(2,1)S(1)}, u32[]{:S(2)}, u32[]{:S(2)}) collective-permute-start(bf16[2,40,1024]{2,1,0:T(8,128)(2,1)S(1)} %get-tuple-element.66.refs_4_), channel_id=1, source_target_pairs={{0,4},{4,0},{8,12},{12,8},{16,20},{20,16},{24,28},{28,24},{1,5},{5... | collective-permute-start | bytes 491528 | tf_op jit(solution)/shard_map/ppermute | solution.py:363
  88.5 12.6 %collective-permute-start.21 = (bf16[1,40,2048]{2,1,0:T(8,128)(2,1)S(1)}, bf16[1,40,2048]{2,1,0:T(8,128)(2,1)S(1)}, u32[]{:S(2)}, u32[]{:S(2)}) collective-permute-start(bf16[1,40,2048]{2,1,0:T(8,128)(2,1)S(1)} %get-tuple-element.70.refs_2_), channel_id=1, source_target_pairs={{0,16},{4,20},{8,24},{12,28},{16,0},{20,4},{24,8},{28,12},{1,17},{... | collective-permute-start | bytes 491528 | tf_op jit(solution)/shard_map/ppermute | solution.py:363

commit v4 on v3

--- a/solution.py
+++ b/solution.py
@@ -451,14 +451,15 @@
     *right, mark = input_part(
         gate, up, right_weights, None, wide, rows, [[rest, move(rest, 1)], [move(rest, m), move(rest, m ^ 1)]], place, 7, (mark,)
     )
-    cut = features // 2 // 512 * 512
+    some = max(features // 4 // 256 * 256, 256)
     left_got, right_got = swap(left[1], 1), swap(right[1], m)
-    gate_grad, mark = long_product(tokens_turned, gate, 0, cut, None, (mark,))
+    gate_grad, mark = long_product(tokens_turned, gate, 0, features - some, None, (mark,))
     left = fold(left[0], left_got, (mark,))
     left_got = swap(left[1], m)
-    right = fold(right[0], right_got, (mark,))
+    right = fold(right[0], right_got, (mark, left[1]))
     right_got = swap(right[1], 1)
-    gate_grad, mark = long_product(tokens_turned, gate, cut, features, gate_grad, (left[1], right[1]))
+    gate_grad, mark = long_product(tokens_turned, gate, features - some, features, gate_grad, (left[1], right[1]))
+    up_grad, mark = long_product(tokens_turned, up, 0, some, None, (mark,))
     total, sent = join(left[0], left_got, right[0], right_got, (mark,))
     for k, m in enumerate(masks[:0:-1]):
         if k > 0:
@@ -466,7 +467,7 @@
             total, sent = total[:n], total[n:]
         got = swap(sent, m)
         if k == 0:
-            up_grad, _ = long_product(tokens_turned, up, 0, features, None, (sent,))
+            up_grad, _ = long_product(tokens_turned, up, some, features, up_grad, (sent,))
         total = total + got
     return total.reshape(rows, features), gate_grad, up_grad, down_grad
 

time: 102 us -> 100 us (0.980)
  starting transfers between devices: 27.7 us -> 23.8 us
  Pallas kernels: 57.8 us -> 59.3 us
    ppermute x22, starting transfers between devices: 27.7 us -> 23.8 us  [swap(): return lax.ppermute(x, axis, [(i, i ^ mask) for i in range(n)])]
    pallas_call x23 -> x24, Pallas kernels: 57.8 us -> 59.3 us  [call(): pl.pallas_call(body, out_shape=list(out_shape) + [struct((8, 128), F32)]...]
  transfers between devices with their start and end apart: 22 -> 22, of which waited for: 6 -> 7; matrix products, arithmetic and copies ran while one was open for 1% -> 1% of each run, Pallas kernels for 57% -> 59%
where the time goes in v4:
time: 100 us; the launch traced here: 99.9 us
  Pallas kernels  59.3 us (59%)
  starting transfers between devices  23.8 us (24%)
  waiting for transfers between devices  14.6 us (15%)
  other arithmetic  1.34 us (1%)
    pallas_call x24, Pallas kernels, call(): pl.pallas_call(body, out_shape=list(out_shape) + [struct((8, 128), F32)]...  59.3 us
    ppermute x22, starting transfers between devices, swap(): return lax.ppermute(x, axis, [(i, i ^ mask) for i in range(n)])  23.8 us
    ppermute x22, waiting for transfers between devices, swap(): return lax.ppermute(x, axis, [(i, i ^ mask) for i in range(n)])  14.6 us
  transfers between devices with their start and end apart: 22, of which 7 were waited for; matrix products, arithmetic and copies ran while one was open for 1% of the time, Pallas kernels for 59%

profile of v4, /device:TPU:0, one launch (start us, length us, event | category | flops | bytes accessed | tf_op | source)
XLA Modules:
  0.0 99.9 jit_solution(11463709800910592254)
XLA Ops:
  0.6 3.0 %collective-permute-start.2 = (bf16[1,40,2048]{2,1,0:T(8,128)(2,1)}, bf16[1,40,2048]{2,1,0:T(8,128)(2,1)S(1)}, u32[]{:S(2)}, u32[]{:S(2)}) collective-permute-start(bf16[1,40,2048]{2,1,0:T(8,128)(2,1)} %bitcast.9), channel_id=1, source_target_pairs={{0,4},{4,0},{8,12},{12,8},{16,20},{20,16},{24,28},{28,24},{1,5},{5... | collective-permute-start | bytes 491528 | tf_op jit(solution)/shard_map/ppermute | solution.py:363
  3.6 1.6 %collective-permute-start.1 = (bf16[1,40,2048]{2,1,0:T(8,128)(2,1)}, bf16[1,40,2048]{2,1,0:T(8,128)(2,1)S(1)}, u32[]{:S(2)}, u32[]{:S(2)}) collective-permute-start(bf16[1,40,2048]{2,1,0:T(8,128)(2,1)} %bitcast.10), channel_id=1, source_target_pairs={{0,8},{4,12},{8,0},{12,4},{16,24},{20,28},{24,16},{28,20},{1,9},{5... | collective-permute-start | bytes 491528 | tf_op jit(solution)/shard_map/ppermute | solution.py:363
  5.2 2.6 %collective-permute-start = (bf16[1,40,2048]{2,1,0:T(8,128)(2,1)}, bf16[1,40,2048]{2,1,0:T(8,128)(2,1)S(1)}, u32[]{:S(2)}, u32[]{:S(2)}) collective-permute-start(bf16[1,40,2048]{2,1,0:T(8,128)(2,1)} %bitcast.11), channel_id=1, source_target_pairs={{0,16},{4,20},{8,24},{12,28},{16,0},{20,4},{24,8},{28,12},{1,17},{... | collective-permute-start | bytes 491528 | tf_op jit(solution)/shard_map/ppermute | solution.py:363
  7.8 0.7 iota_xor_fusion
  8.5 5.0 %shard_map.111 = (bf16[1664,2048]{1,0:T(8,128)(2,1)S(1)}, bf16[1664,2048]{1,0:T(8,128)(2,1)S(1)}, f32[8,128]{1,0:T(8,128)S(1)}) custom-call(bf16[3328,2048]{1,0:T(8,128)(2,1)} %refs_1_.1, bf16[3328,2048]{1,0:T(8,128)(2,1)} %refs_1_.1, s32[8]{0:T(128)S(1)} %get-tuple-element.79.refs_2_.refs_0_, s32[8]{0:T(128)S(1)} %get-tuple-element.78.refs_3_.refs_1_), custom_call_target="tpu_custom_call" | custom-call | bytes 13631488 | tf_op jit(solution)/shard_map/pallas_call | solution.py:45
  13.5 0.0 collective-permute-done.2.refs_3_.refs_4_
  13.5 0.0 collective-permute-done.1.refs_2_
  13.5 1.7 %collective-permute-done.refs_0_ = bf16[1,40,2048]{2,1,0:T(8,128)(2,1)S(1)} collective-permute-done((bf16[1,40,2048]{2,1,0:T(8,128)(2,1)}, bf16[1,40,2048]{2,1,0:T(8,128)(2,1)S(1)}, u32[]{:S(2)}, u32[]{:S(2)}) %collective-permute-start) | collective-permute-done | bytes 163872 | tf_op jit(solution)/shard_map/ppermute | solution.py:363
  15.3 0.0 copy-start.2
  15.3 0.5 collective-permute-start.3
  15.8 0.5 collective-permute-start.4
  16.3 1.5 %collective-permute-start.5 = (bf16[1,40,2048]{2,1,0:T(8,128)(2,1)S(1)}, bf16[1,40,2048]{2,1,0:T(8,128)(2,1)S(1)}, u32[]{:S(2)}, u32[]{:S(2)}) collective-permute-start(bf16[1,40,2048]{2,1,0:T(8,128)(2,1)S(1)} %collective-permute-done.1.refs_2_), channel_id=1, source_target_pairs={{0,4},{4,0},{8,12},{12,8},{16,20},{20,16},{24,28},{28,24},{1,5},{5... | collective-permute-start | bytes 491528 | tf_op jit(solution)/shard_map/ppermute | solution.py:363
  17.8 2.9 %collective-permute-done.3.refs_4_.refs_3_.refs_1_ = bf16[1,40,2048]{2,1,0:T(8,128)(2,1)S(1)} collective-permute-done((bf16[1,40,2048]{2,1,0:T(8,128)(2,1)S(1)}, bf16[1,40,2048]{2,1,0:T(8,128)(2,1)S(1)}, u32[]{:S(2)}, u32[]{:S(2)}) %collective-permute-start.3) | collective-permute-done | bytes 163872 | tf_op jit(solution)/shard_map/ppermute | solution.py:363
  20.7 0.5 collective-permute-start.6
  21.2 1.2 %collective-permute-start.9 = (bf16[1,40,2048]{2,1,0:T(8,128)(2,1)S(1)}, bf16[1,40,2048]{2,1,0:T(8,128)(2,1)S(1)}, u32[]{:S(2)}, u32[]{:S(2)}) collective-permute-start(bf16[1,40,2048]{2,1,0:T(8,128)(2,1)S(1)} %shard_map.117.refs_0_), channel_id=1, source_target_pairs={{0,16},{4,20},{8,24},{12,28},{16,0},{20,4},{24,8},{28,12},{1,17},{... | collective-permute-start | bytes 491528 | tf_op jit(solution)/shard_map/ppermute | solution.py:363
  22.4 3.7 %shard_map.113 = (bf16[3328,320]{1,0:T(8,128)(2,1)S(1)}, f32[4,40,3328]{2,1,0:T(8,128)S(1)}, f32[4,40,3328]{2,1,0:T(8,128)S(1)}) custom-call(s32[8]{0:T(128)S(1)} %get-tuple-element.79.refs_2_.refs_0_, s32[8]{0:T(128)S(1)} %get-tuple-element.78.refs_3_.refs_1_, bf16[8,40,3328]{2,1,0:T(8,128)(2,1)S(1)} %bitcast.7, bf16[8,40,3328]{2,1,0:T(8,128)(2,1)S(1)} %bitcast.8, ...), custom_call_target="tpu_custom_call" | custom-call | flops 10649600 | bytes 10649600 | tf_op jit(solution)/shard_map/pallas_call | solution.py:45
  26.1 0.0 collective-permute-done.5.refs_6_
  26.1 0.0 collective-permute-done.4.refs_5_
  26.1 1.1 %collective-permute-done.6.refs_7_ = bf16[1,40,2048]{2,1,0:T(8,128)(2,1)S(1)} collective-permute-done((bf16[1,40,2048]{2,1,0:T(8,128)(2,1)S(1)}, bf16[1,40,2048]{2,1,0:T(8,128)(2,1)S(1)}, u32[]{:S(2)}, u32[]{:S(2)}) %collective-permute-start.6) | collective-permute-done | bytes 163872 | tf_op jit(solution)/shard_map/ppermute | solution.py:363
  27.2 0.1 shard_map.114.refs_1_
  27.3 2.6 %shard_map.115 = (f32[160,1664]{1,0:T(8,128)S(1)}, bf16[160,1664]{1,0:T(8,128)(2,1)S(1)}) custom-call(s32[1]{0:T(128)} %bitcast.refs_0_, bf16[320,2048]{1,0:T(8,128)(2,1)S(1)} %shard_map.114.refs_1_, bf16[1664,2048]{1,0:T(8,128)(2,1)S(1)} %get-tuple-element.43.refs_2_), custom_call_target="tpu_custom_call" | custom-call | flops 2181038080 | bytes 6815744 | tf_op jit(solution)/shard_map/pallas_call | solution.py:45
  29.9 0.1 collective-permute-start.7
  30.0 0.0 collective-permute-done.9.refs_4_.refs_1_
  30.0 2.6 %shard_map.118 = (f32[160,1664]{1,0:T(8,128)S(1)}, bf16[160,1664]{1,0:T(8,128)(2,1)S(1)}) custom-call(s32[1]{0:T(128)} %bitcast.refs_0_, bf16[320,2048]{1,0:T(8,128)(2,1)S(1)} %shard_map.114.refs_1_, bf16[1664,2048]{1,0:T(8,128)(2,1)S(1)} %get-tuple-element.48.refs_2_, bf16[160,1664]{1,0:T(8,128)(2,1)S(1)} %get-tuple-element.45.refs_3_, ...), custom_call_target="tpu_custom_call" | custom-call | flops 2181038080 | bytes 6815744 | tf_op jit(solution)/shard_map/pallas_call | solution.py:45
  32.6 0.6 collective-permute-start.10
  33.2 0.0 collective-permute-done.7.refs_1_
  33.2 0.1 shard_map.116.refs_2_
  33.3 1.6 %collective-permute-start.8 = (bf16[160,1664]{1,0:T(8,128)(2,1)S(1)}, bf16[160,1664]{1,0:T(8,128)(2,1)S(1)}, u32[]{:S(2)}, u32[]{:S(2)}) collective-permute-start(bf16[160,1664]{1,0:T(8,128)(2,1)S(1)} %shard_map.116.refs_2_), channel_id=1, source_target_pairs={{0,2},{1,3},{2,0},{3,1},{4,6},{5,7},{6,4},{7,5},{8,10},{9,11},{10,... | collective-permute-start | bytes 1597448 | tf_op jit(solution)/shard_map/ppermute | solution.py:363
  34.9 0.0 collective-permute-done.10.refs_1_
  34.9 0.1 shard_map.119.refs_6_
  35.0 1.5 %collective-permute-start.14 = (bf16[160,1664]{1,0:T(8,128)(2,1)S(1)}, bf16[160,1664]{1,0:T(8,128)(2,1)S(1)}, u32[]{:S(2)}, u32[]{:S(2)}) collective-permute-start(bf16[160,1664]{1,0:T(8,128)(2,1)S(1)} %shard_map.119.refs_6_), channel_id=1, source_target_pairs={{0,2},{1,3},{2,0},{3,1},{4,6},{5,7},{6,4},{7,5},{8,10},{9,11},{10,... | collective-permute-start | bytes 1597448 | tf_op jit(solution)/shard_map/ppermute | solution.py:363
  36.5 1.0 %collective-permute-start.12 = (bf16[2,40,2048]{2,1,0:T(8,128)(2,1)S(1)}, bf16[2,40,2048]{2,1,0:T(8,128)(2,1)S(1)}, u32[]{:S(2)}, u32[]{:S(2)}) collective-permute-start(bf16[2,40,2048]{2,1,0:T(8,128)(2,1)S(1)} %shard_map.121), channel_id=1, source_target_pairs={{0,8},{4,12},{8,0},{12,4},{16,24},{20,28},{24,16},{28,20},{1,9},{5... | collective-permute-start | bytes 983048 | tf_op jit(solution)/shard_map/ppermute | solution.py:363
  37.5 1.5 %collective-permute-start.11 = (bf16[2,40,2048]{2,1,0:T(8,128)(2,1)S(1)}, bf16[2,40,2048]{2,1,0:T(8,128)(2,1)S(1)}, u32[]{:S(2)}, u32[]{:S(2)}) collective-permute-start(bf16[2,40,2048]{2,1,0:T(8,128)(2,1)S(1)} %shard_map.121), channel_id=1, source_target_pairs={{0,4},{4,0},{8,12},{12,8},{16,20},{20,16},{24,28},{28,24},{1,5},{5... | collective-permute-start | bytes 983048 | tf_op jit(solution)/shard_map/ppermute | solution.py:363
  39.0 13.6 %shard_map.120 = (bf16[3328,2048]{1,0:T(8,128)(2,1)}, bf16[1024,3328]{1,0:T(8,128)(2,1)S(1)}, bf16[1024,3328]{1,0:T(8,128)(2,1)S(1)}, bf16[1024,3328]{1,0:T(8,12...) custom-call(bf16[3328,320]{1,0:T(8,128)(2,1)S(1)} %get-tuple-element.42.refs_8_.refs_0_, ...), custom_call_target="tpu_custom_call" | custom-call | flops 4362076160 | bytes 13631488 | tf_op jit(solution)/shard_map/pallas_call | solution.py:45
  52.6 0.0 collective-permute-done.12.refs_7_.refs_2_
  52.6 0.0 collective-permute-done.11.refs_6_.refs_3_
  52.6 0.0 collective-permute-done.8.refs_2_
  52.6 0.4 shard_map.122.refs_1_
  53.0 0.1 collective-permute-start.13
  53.1 5.7 %collective-permute-done.14.refs_2_ = bf16[160,1664]{1,0:T(8,128)(2,1)S(1)} collective-permute-done((bf16[160,1664]{1,0:T(8,128)(2,1)S(1)}, bf16[160,1664]{1,0:T(8,128)(2,1)S(1)}, u32[]{:S(2)}, u32[]{:S(2)}) %collective-permute-start.14) | collective-permute-done | bytes 532512 | tf_op jit(solution)/shard_map/ppermute | solution.py:363
  58.8 0.4 shard_map.123.refs_3_
  59.2 0.1 collective-permute-start.15
  59.2 0.7 collective-permute-start.17
  59.9 0.0 collective-permute-done.13.refs_2_
  59.9 2.0 %collective-permute-done.15.refs_4_ = bf16[2,160,1664]{2,1,0:T(8,128)(2,1)S(1)} collective-permute-done((bf16[2,160,1664]{2,1,0:T(8,128)(2,1)S(1)}, bf16[2,160,1664]{2,1,0:T(8,128)(2,1)S(1)}, u32[]{:S(2)}, u32[]{:S(2)}) %collective-permute-start.15) | collective-permute-done | bytes 1064992 | tf_op jit(solution)/shard_map/ppermute | solution.py:363
  61.9 0.3 shard_map.124
  62.2 4.6 %shard_map.125 = (bf16[2,2,40,1024]{3,2,1,0:T(8,128)(2,1)S(1)}, bf16[2,2,40,1024]{3,2,1,0:T(8,128)(2,1)S(1)}, f32[8,128]{1,0:T(8,128)S(1)}) custom-call(bf16[320,3328]{1,0:T(8,128)(2,1)S(1)} %get-tuple-element.52.refs_0_.refs_1_, bf16[320,3328]{1,0:T(8,128)(2,1)S(1)} %get-tuple-element.53.refs_1_, bf16[1024,3328]{1,0:T(8,128)(2,1)S(1)} %get-tuple-element.54.refs_2_, ...), custom_call_target="tpu_custom_call" | custom-call | flops 4362076160 | bytes 13631488 | tf_op jit(solution)/shard_map/pallas_call | solution.py:45
  66.8 0.7 collective-permute-start.16
  67.5 4.6 %shard_map.127 = (bf16[2,2,40,1024]{3,2,1,0:T(8,128)(2,1)S(1)}, bf16[2,2,40,1024]{3,2,1,0:T(8,128)(2,1)S(1)}, f32[8,128]{1,0:T(8,128)S(1)}) custom-call(bf16[320,3328]{1,0:T(8,128)(2,1)S(1)} %get-tuple-element.52.refs_0_.refs_1_, bf16[320,3328]{1,0:T(8,128)(2,1)S(1)} %get-tuple-element.53.refs_1_, bf16[1024,3328]{1,0:T(8,128)(2,1)S(1)} %get-tuple-element.58.refs_2_, ...), custom_call_target="tpu_custom_call" | custom-call | flops 4362076160 | bytes 13631488 | tf_op jit(solution)/shard_map/pallas_call | solution.py:45
  72.1 1.9 %collective-permute-start.19 = (bf16[2,2,40,1024]{3,2,1,0:T(8,128)(2,1)S(1)}, bf16[2,2,40,1024]{3,2,1,0:T(8,128)(2,1)S(1)}, u32[]{:S(2)}, u32[]{:S(2)}) collective-permute-start(bf16[2,2,40,1024]{3,2,1,0:T(8,128)(2,1)S(1)} %get-tuple-element.66), channel_id=1, source_target_pairs={{0,8},{4,12},{8,0},{12,4},{16,24},{20,28},{24,16},{28,20},{1,9},{5... | collective-permute-start | bytes 983048 | tf_op jit(solution)/shard_map/ppermute | solution.py:363
  74.0 0.0 collective-permute-done.17.refs_4_
  74.0 0.5 shard_map.126.refs_0_
  74.4 6.8 %shard_map.128 = (bf16[2048,3328]{1,0:T(8,128)(2,1)}, f32[8,128]{1,0:T(8,128)S(1)}) custom-call(bf16[2048,320]{1,0:T(8,128)(2,1)S(1)} %shard_map.126.refs_0_, bf16[320,3328]{1,0:T(8,128)(2,1)S(1)} %get-tuple-element.52.refs_0_.refs_1_, f32[8,128]{1,0:T(8,128)S(1)} %get-tuple-element.61.refs_2_), custom_call_target="tpu_custom_call" | custom-call | flops 3271557120 | bytes 10223616 | tf_op jit(solution)/shard_map/pallas_call | solution.py:45
  81.2 0.0 collective-permute-done.16.refs_1_
  81.3 0.3 collective-permute-start.18
  81.5 0.2 collective-permute-done.19.refs_1_
  81.7 1.4 %collective-permute-start.20 = (bf16[2,40,1024]{2,1,0:T(8,128)(2,1)S(1)}, bf16[2,40,1024]{2,1,0:T(8,128)(2,1)S(1)}, u32[]{:S(2)}, u32[]{:S(2)}) collective-permute-start(bf16[2,40,1024]{2,1,0:T(8,128)(2,1)S(1)} %get-tuple-element.68.refs_4_), channel_id=1, source_target_pairs={{0,4},{4,0},{8,12},{12,8},{16,20},{20,16},{24,28},{28,24},{1,5},{5... | collective-permute-start | bytes 491528 | tf_op jit(solution)/shard_map/ppermute | solution.py:363
  83.1 3.1 %shard_map.131 = (bf16[2048,3328]{1,0:T(8,128)(2,1)}, f32[8,128]{1,0:T(8,128)S(1)}) custom-call(bf16[2048,320]{1,0:T(8,128)(2,1)S(1)} %shard_map.126.refs_0_, bf16[320,3328]{1,0:T(8,128)(2,1)S(1)} %get-tuple-element.52.refs_0_.refs_1_, bf16[2048,3328]{1,0:T(8,128)(2,1)} %get-tuple-element.69.refs_2_, ...), custom_call_target="tpu_custom_call", output_to_operand_aliasing={{0}: (2, {})} | custom-call | flops 1090519040 | bytes 3407872 | tf_op jit(solution)/shard_map/pallas_call | solution.py:45
  86.3 3.4 %shard_map.132 = (bf16[2048,3328]{1,0:T(8,128)(2,1)}, f32[8,128]{1,0:T(8,128)S(1)}) custom-call(bf16[2048,320]{1,0:T(8,128)(2,1)S(1)} %shard_map.126.refs_0_, bf16[320,3328]{1,0:T(8,128)(2,1)S(1)} %get-tuple-element.53.refs_1_, f32[8,128]{1,0:T(8,128)S(1)} %get-tuple-element.70.refs_2_), custom_call_target="tpu_custom_call" | custom-call | flops 1090519040 | bytes 3407872 | tf_op jit(solution)/shard_map/pallas_call | solution.py:45
  89.7 0.0 collective-permute-done.20.refs_3_
  89.7 1.2 %collective-permute-start.21 = (bf16[1,40,2048]{2,1,0:T(8,128)(2,1)S(1)}, bf16[1,40,2048]{2,1,0:T(8,128)(2,1)S(1)}, u32[]{:S(2)}, u32[]{:S(2)}) collective-permute-start(bf16[1,40,2048]{2,1,0:T(8,128)(2,1)S(1)} %get-tuple-element.73.refs_3_), channel_id=1, source_target_pairs={{0,16},{4,20},{8,24},{12,28},{16,0},{20,4},{24,8},{28,12},{1,17},{... | collective-permute-start | bytes 491528 | tf_op jit(solution)/shard_map/ppermute | solution.py:363
  90.9 7.3 %shard_map.134 = (bf16[2048,3328]{1,0:T(8,128)(2,1)}, f32[8,128]{1,0:T(8,128)}) custom-call(bf16[2048,320]{1,0:T(8,128)(2,1)S(1)} %shard_map.126.refs_0_, bf16[320,3328]{1,0:T(8,128)(2,1)S(1)} %get-tuple-element.53.refs_1_, bf16[2048,3328]{1,0:T(8,128)(2,1)} %get-tuple-element.75.refs_2_, ...), custom_call_target="tpu_custom_call", output_to_operand_aliasing={{0}: (2, {})} | custom-call | flops 3271557120 | bytes 10223616 | tf_op jit(solution)/shard_map/pallas_call | solution.py:45
  98.2 1.0 %collective-permute-done.21 = bf16[1,40,2048]{2,1,0:T(8,128)(2,1)S(1)} collective-permute-done((bf16[1,40,2048]{2,1,0:T(8,128)(2,1)S(1)}, bf16[1,40,2048]{2,1,0:T(8,128)(2,1)S(1)}, u32[]{:S(2)}, u32[]{:S(2)}) %collective-permute-start.21) | collective-permute-done | bytes 163872 | tf_op jit(solution)/shard_map/ppermute | solution.py:363
  99.3 0.7 add_bitcast_fusion
  (14 shorter events, 0.2 us)
Async XLA Ops:
  0.6 12.9 %collective-permute-start.2 = (bf16[1,40,2048]{2,1,0:T(8,128)(2,1)}, bf16[1,40,2048]{2,1,0:T(8,128)(2,1)S(1)}, u32[]{:S(2)}, u32[]{:S(2)}) collective-permute-start(bf16[1,40,2048]{2,1,0:T(8,128)(2,1)} %bitcast.9), channel_id=1, source_target_pairs={{0,4},{4,0},{8,12},{12,8},{16,20},{20,16},{24,28},{28,24},{1,5},{5... | collective-permute-start | bytes 491528 | tf_op jit(solution)/shard_map/ppermute | solution.py:363
  3.6 9.9 %collective-permute-start.1 = (bf16[1,40,2048]{2,1,0:T(8,128)(2,1)}, bf16[1,40,2048]{2,1,0:T(8,128)(2,1)S(1)}, u32[]{:S(2)}, u32[]{:S(2)}) collective-permute-start(bf16[1,40,2048]{2,1,0:T(8,128)(2,1)} %bitcast.10), channel_id=1, source_target_pairs={{0,8},{4,12},{8,0},{12,4},{16,24},{20,28},{24,16},{28,20},{1,9},{5... | collective-permute-start | bytes 491528 | tf_op jit(solution)/shard_map/ppermute | solution.py:363
  5.2 10.1 %collective-permute-start = (bf16[1,40,2048]{2,1,0:T(8,128)(2,1)}, bf16[1,40,2048]{2,1,0:T(8,128)(2,1)S(1)}, u32[]{:S(2)}, u32[]{:S(2)}) collective-permute-start(bf16[1,40,2048]{2,1,0:T(8,128)(2,1)} %bitcast.11), channel_id=1, source_target_pairs={{0,16},{4,20},{8,24},{12,28},{16,0},{20,4},{24,8},{28,12},{1,17},{... | collective-permute-start | bytes 491528 | tf_op jit(solution)/shard_map/ppermute | solution.py:363
  8.5 12.8 %copy-start.3 = (bf16[40,2048]{1,0:T(8,128)(2,1)S(1)}, bf16[40,2048]{1,0:T(8,128)(2,1)}, u32[]{:S(2)}) copy-start(bf16[40,2048]{1,0:T(8,128)(2,1)} %param.8) | copy-start | bytes 491524
  8.5 13.9 %copy-start = (bf16[320,3328]{1,0:T(8,128)(2,1)S(1)}, bf16[320,3328]{1,0:T(8,128)(2,1)}, u32[]{:S(2)}) copy-start(bf16[320,3328]{1,0:T(8,128)(2,1)} %param.10) | copy-start | bytes 6389764
  8.5 13.9 %copy-start.1 = (bf16[320,3328]{1,0:T(8,128)(2,1)S(1)}, bf16[320,3328]{1,0:T(8,128)(2,1)}, u32[]{:S(2)}) copy-start(bf16[320,3328]{1,0:T(8,128)(2,1)} %param.11) | copy-start | bytes 6389764
  15.3 11.9 %copy-start.2 = (bf16[40,2048]{1,0:T(8,128)(2,1)S(1)}, bf16[40,2048]{1,0:T(8,128)(2,1)}, u32[]{:S(2)}) copy-start(bf16[40,2048]{1,0:T(8,128)(2,1)} %param.9) | copy-start | bytes 491524
  15.3 5.4 %collective-permute-start.3 = (bf16[1,40,2048]{2,1,0:T(8,128)(2,1)S(1)}, bf16[1,40,2048]{2,1,0:T(8,128)(2,1)S(1)}, u32[]{:S(2)}, u32[]{:S(2)}) collective-permute-start(bf16[1,40,2048]{2,1,0:T(8,128)(2,1)S(1)} %shard_map.112.refs_1_), channel_id=1, source_target_pairs={{0,8},{4,12},{8,0},{12,4},{16,24},{20,28},{24,16},{28,20},{1,9},{5... | collective-permute-start | bytes 491528 | tf_op jit(solution)/shard_map/ppermute | solution.py:363
  15.8 10.3 %collective-permute-start.4 = (bf16[1,40,2048]{2,1,0:T(8,128)(2,1)S(1)}, bf16[1,40,2048]{2,1,0:T(8,128)(2,1)S(1)}, u32[]{:S(2)}, u32[]{:S(2)}) collective-permute-start(bf16[1,40,2048]{2,1,0:T(8,128)(2,1)S(1)} %shard_map.112.refs_1_), channel_id=1, source_target_pairs={{0,4},{4,0},{8,12},{12,8},{16,20},{20,16},{24,28},{28,24},{1,5},{5... | collective-permute-start | bytes 491528 | tf_op jit(solution)/shard_map/ppermute | solution.py:363
  16.3 9.7 %collective-permute-start.5 = (bf16[1,40,2048]{2,1,0:T(8,128)(2,1)S(1)}, bf16[1,40,2048]{2,1,0:T(8,128)(2,1)S(1)}, u32[]{:S(2)}, u32[]{:S(2)}) collective-permute-start(bf16[1,40,2048]{2,1,0:T(8,128)(2,1)S(1)} %collective-permute-done.1.refs_2_), channel_id=1, source_target_pairs={{0,4},{4,0},{8,12},{12,8},{16,20},{20,16},{24,28},{28,24},{1,5},{5... | collective-permute-start | bytes 491528 | tf_op jit(solution)/shard_map/ppermute | solution.py:363
  20.7 6.5 %collective-permute-start.6 = (bf16[1,40,2048]{2,1,0:T(8,128)(2,1)S(1)}, bf16[1,40,2048]{2,1,0:T(8,128)(2,1)S(1)}, u32[]{:S(2)}, u32[]{:S(2)}) collective-permute-start(bf16[1,40,2048]{2,1,0:T(8,128)(2,1)S(1)} %collective-permute-done.3.refs_4_.refs_3_.refs_1_), channel_id=1, source_target_pairs={{0,4},{4,0},{8,12},{12,8},{16,20},{20,16},{24,28},{28,24},{1,5},{5... | collective-permute-start | bytes 491528 | tf_op jit(solution)/shard_map/ppermute | solution.py:363
  21.2 8.8 %collective-permute-start.9 = (bf16[1,40,2048]{2,1,0:T(8,128)(2,1)S(1)}, bf16[1,40,2048]{2,1,0:T(8,128)(2,1)S(1)}, u32[]{:S(2)}, u32[]{:S(2)}) collective-permute-start(bf16[1,40,2048]{2,1,0:T(8,128)(2,1)S(1)} %shard_map.117.refs_0_), channel_id=1, source_target_pairs={{0,16},{4,20},{8,24},{12,28},{16,0},{20,4},{24,8},{28,12},{1,17},{... | collective-permute-start | bytes 491528 | tf_op jit(solution)/shard_map/ppermute | solution.py:363
  29.9 3.2 %collective-permute-start.7 = (bf16[160,1664]{1,0:T(8,128)(2,1)S(1)}, bf16[160,1664]{1,0:T(8,128)(2,1)S(1)}, u32[]{:S(2)}, u32[]{:S(2)}) collective-permute-start(bf16[160,1664]{1,0:T(8,128)(2,1)S(1)} %get-tuple-element.45.refs_3_), channel_id=1, source_target_pairs={{0,1},{1,0},{2,3},{3,2},{4,5},{5,4},{6,7},{7,6},{8,9},{9,8},{10,11... | collective-permute-start | bytes 1597448 | tf_op jit(solution)/shard_map/ppermute | solution.py:363
  32.6 2.2 %collective-permute-start.10 = (bf16[160,1664]{1,0:T(8,128)(2,1)S(1)}, bf16[160,1664]{1,0:T(8,128)(2,1)S(1)}, u32[]{:S(2)}, u32[]{:S(2)}) collective-permute-start(bf16[160,1664]{1,0:T(8,128)(2,1)S(1)} %get-tuple-element.50), channel_id=1, source_target_pairs={{0,1},{1,0},{2,3},{3,2},{4,5},{5,4},{6,7},{7,6},{8,9},{9,8},{10,11... | collective-permute-start | bytes 1597448 | tf_op jit(solution)/shard_map/ppermute | solution.py:363
  33.3 19.3 %collective-permute-start.8 = (bf16[160,1664]{1,0:T(8,128)(2,1)S(1)}, bf16[160,1664]{1,0:T(8,128)(2,1)S(1)}, u32[]{:S(2)}, u32[]{:S(2)}) collective-permute-start(bf16[160,1664]{1,0:T(8,128)(2,1)S(1)} %shard_map.116.refs_2_), channel_id=1, source_target_pairs={{0,2},{1,3},{2,0},{3,1},{4,6},{5,7},{6,4},{7,5},{8,10},{9,11},{10,... | collective-permute-start | bytes 1597448 | tf_op jit(solution)/shard_map/ppermute | solution.py:363
  35.0 23.8 %collective-permute-start.14 = (bf16[160,1664]{1,0:T(8,128)(2,1)S(1)}, bf16[160,1664]{1,0:T(8,128)(2,1)S(1)}, u32[]{:S(2)}, u32[]{:S(2)}) collective-permute-start(bf16[160,1664]{1,0:T(8,128)(2,1)S(1)} %shard_map.119.refs_6_), channel_id=1, source_target_pairs={{0,2},{1,3},{2,0},{3,1},{4,6},{5,7},{6,4},{7,5},{8,10},{9,11},{10,... | collective-permute-start | bytes 1597448 | tf_op jit(solution)/shard_map/ppermute | solution.py:363
  36.5 16.1 %collective-permute-start.12 = (bf16[2,40,2048]{2,1,0:T(8,128)(2,1)S(1)}, bf16[2,40,2048]{2,1,0:T(8,128)(2,1)S(1)}, u32[]{:S(2)}, u32[]{:S(2)}) collective-permute-start(bf16[2,40,2048]{2,1,0:T(8,128)(2,1)S(1)} %shard_map.121), channel_id=1, source_target_pairs={{0,8},{4,12},{8,0},{12,4},{16,24},{20,28},{24,16},{28,20},{1,9},{5... | collective-permute-start | bytes 983048 | tf_op jit(solution)/shard_map/ppermute | solution.py:363
  37.5 15.1 %collective-permute-start.11 = (bf16[2,40,2048]{2,1,0:T(8,128)(2,1)S(1)}, bf16[2,40,2048]{2,1,0:T(8,128)(2,1)S(1)}, u32[]{:S(2)}, u32[]{:S(2)}) collective-permute-start(bf16[2,40,2048]{2,1,0:T(8,128)(2,1)S(1)} %shard_map.121), channel_id=1, source_target_pairs={{0,4},{4,0},{8,12},{12,8},{16,20},{20,16},{24,28},{28,24},{1,5},{5... | collective-permute-start | bytes 983048 | tf_op jit(solution)/shard_map/ppermute | solution.py:363
  53.0 6.9 %collective-permute-start.13 = (bf16[2,160,1664]{2,1,0:T(8,128)(2,1)S(1)}, bf16[2,160,1664]{2,1,0:T(8,128)(2,1)S(1)}, u32[]{:S(2)}, u32[]{:S(2)}) collective-permute-start(bf16[2,160,1664]{2,1,0:T(8,128)(2,1)S(1)} %shard_map.122.refs_1_), channel_id=1, source_target_pairs={{0,1},{1,0},{2,3},{3,2},{4,5},{5,4},{6,7},{7,6},{8,9},{9,8},{10,11... | collective-permute-start | bytes 3194888 | tf_op jit(solution)/shard_map/ppermute | solution.py:363
  59.2 2.7 %collective-permute-start.15 = (bf16[2,160,1664]{2,1,0:T(8,128)(2,1)S(1)}, bf16[2,160,1664]{2,1,0:T(8,128)(2,1)S(1)}, u32[]{:S(2)}, u32[]{:S(2)}) collective-permute-start(bf16[2,160,1664]{2,1,0:T(8,128)(2,1)S(1)} %shard_map.123.refs_3_), channel_id=1, source_target_pairs={{0,1},{1,0},{2,3},{3,2},{4,5},{5,4},{6,7},{7,6},{8,9},{9,8},{10,11... | collective-permute-start | bytes 3194888 | tf_op jit(solution)/shard_map/ppermute | solution.py:363
  59.2 14.7 %collective-permute-start.17 = (bf16[2,40,2048]{2,1,0:T(8,128)(2,1)S(1)}, bf16[2,40,2048]{2,1,0:T(8,128)(2,1)S(1)}, u32[]{:S(2)}, u32[]{:S(2)}) collective-permute-start(bf16[2,40,2048]{2,1,0:T(8,128)(2,1)S(1)} %collective-permute-done.12.refs_7_.refs_2_), channel_id=1, source_target_pairs={{0,4},{4,0},{8,12},{12,8},{16,20},{20,16},{24,28},{28,24},{1,5},{5... | collective-permute-start | bytes 983048 | tf_op jit(solution)/shard_map/ppermute | solution.py:363
  66.8 14.4 %collective-permute-start.16 = (bf16[2,2,40,1024]{3,2,1,0:T(8,128)(2,1)S(1)}, bf16[2,2,40,1024]{3,2,1,0:T(8,128)(2,1)S(1)}, u32[]{:S(2)}, u32[]{:S(2)}) collective-permute-start(bf16[2,2,40,1024]{3,2,1,0:T(8,128)(2,1)S(1)} %get-tuple-element.57), channel_id=1, source_target_pairs={{0,4},{4,0},{8,12},{12,8},{16,20},{20,16},{24,28},{28,24},{1,5},{5... | collective-permute-start | bytes 983048 | tf_op jit(solution)/shard_map/ppermute | solution.py:363
  72.1 9.6 %collective-permute-start.19 = (bf16[2,2,40,1024]{3,2,1,0:T(8,128)(2,1)S(1)}, bf16[2,2,40,1024]{3,2,1,0:T(8,128)(2,1)S(1)}, u32[]{:S(2)}, u32[]{:S(2)}) collective-permute-start(bf16[2,2,40,1024]{3,2,1,0:T(8,128)(2,1)S(1)} %get-tuple-element.66), channel_id=1, source_target_pairs={{0,8},{4,12},{8,0},{12,4},{16,24},{20,28},{24,16},{28,20},{1,9},{5... | collective-permute-start | bytes 983048 | tf_op jit(solution)/shard_map/ppermute | solution.py:363
  81.3 8.4 %collective-permute-start.18 = (bf16[2,40,1024]{2,1,0:T(8,128)(2,1)S(1)}, bf16[2,40,1024]{2,1,0:T(8,128)(2,1)S(1)}, u32[]{:S(2)}, u32[]{:S(2)}) collective-permute-start(bf16[2,40,1024]{2,1,0:T(8,128)(2,1)S(1)} %get-tuple-element.64.refs_3_), channel_id=1, source_target_pairs={{0,8},{4,12},{8,0},{12,4},{16,24},{20,28},{24,16},{28,20},{1,9},{5... | collective-permute-start | bytes 491528 | tf_op jit(solution)/shard_map/ppermute | solution.py:363
  81.7 7.9 %collective-permute-start.20 = (bf16[2,40,1024]{2,1,0:T(8,128)(2,1)S(1)}, bf16[2,40,1024]{2,1,0:T(8,128)(2,1)S(1)}, u32[]{:S(2)}, u32[]{:S(2)}) collective-permute-start(bf16[2,40,1024]{2,1,0:T(8,128)(2,1)S(1)} %get-tuple-element.68.refs_4_), channel_id=1, source_target_pairs={{0,4},{4,0},{8,12},{12,8},{16,20},{20,16},{24,28},{28,24},{1,5},{5... | collective-permute-start | bytes 491528 | tf_op jit(solution)/shard_map/ppermute | solution.py:363
  89.7 9.5 %collective-permute-start.21 = (bf16[1,40,2048]{2,1,0:T(8,128)(2,1)S(1)}, bf16[1,40,2048]{2,1,0:T(8,128)(2,1)S(1)}, u32[]{:S(2)}, u32[]{:S(2)}) collective-permute-start(bf16[1,40,2048]{2,1,0:T(8,128)(2,1)S(1)} %get-tuple-element.73.refs_3_), channel_id=1, source_target_pairs={{0,16},{4,20},{8,24},{12,28},{16,0},{20,4},{24,8},{28,12},{1,17},{... | collective-permute-start | bytes 491528 | tf_op jit(solution)/shard_map/ppermute | solution.py:363

commit v5 on v4

--- a/solution.py
+++ b/solution.py
@@ -322,6 +322,30 @@
     )
 
 
+def two_products(left, right, begin, into, next_right, next_end, after=()):
+    height, depth = left.shape
+    width = right.shape[1]
+    cuts = [(0, begin + at, size) for at, size in pieces(height - begin, 256)]
+    cuts += [(1, at, size) for at, size in pieces(next_end, 256)]
+
+    def kernel(left_ref, right_ref, next_ref, _, out_ref, next_out_ref, held, sem):
+        copies = []
+        for i, (k, at, size) in enumerate(cuts):
+            held[i, :size] = dot(left_ref[at : at + size], (right_ref, next_ref)[k][...], NN).astype(BF)
+            target = (out_ref, next_out_ref)[k]
+            copies.append(pltpu.make_async_copy(held.at[i, pl.ds(0, size)], target.at[pl.ds(at, size)], sem.at[i]))
+            copies[-1].start()
+        for copy in copies:
+            copy.wait()
+
+    rows = height - begin + next_end
+    return call(
+        kernel, (left, right, next_right, into), [VMEM] * 3 + [HBM], [HBM] * 2, [struct((height, width))] * 2,
+        (2 * depth * width * rows, 2 * width * rows), 32, after, {3: 0},
+        scratch=[pltpu.VMEM((len(cuts), 256, width), BF), pltpu.SemaphoreType.DMA((len(cuts),))], mark=True,
+    )
+
+
 def laid(parts):
     if len(parts) == 1:
         return parts[0]
@@ -420,19 +444,19 @@
             m *= 2
         return mine, arrived, sent
 
-    sums, after = [], ()
-    for k in range(parts):
-        sums.append(hidden_part(core, all_grads, weight_rows[k], after))
-        after = (sums[-1][1], all_tokens.arrays[1])
+    sums, after = [None] * parts, ()
+    for k in reversed(range(parts)):
+        sums[k] = hidden_part(core, all_grads, weight_rows[k], after)
+        after = (sums[k][1], all_tokens.arrays[1])
     after = ()
-    for k in range(parts):
+    for k in reversed(range(parts)):
         sums[k] = summed(*sums[k], after)
         after = (sums[k][2],)
 
     wide = features // 2
     weights = (gate_weight, up_weight)
     down_grad, a, b, c, d, mark = long_product(
-        hidden_turned, all_grads, 0, units, None, (sums[-1][2],),
+        hidden_turned, all_grads, 0, units, None, (sums[0][2],),
         [(x, at, wide) for at in (0, wide) for x in weights], 4, 12,
     )
     left_weights, right_weights = (a, b), (c, d)
@@ -458,8 +482,9 @@
     left_got = swap(left[1], m)
     right = fold(right[0], right_got, (mark, left[1]))
     right_got = swap(right[1], 1)
-    gate_grad, mark = long_product(tokens_turned, gate, features - some, features, gate_grad, (left[1], right[1]))
-    up_grad, mark = long_product(tokens_turned, up, 0, some, None, (mark,))
+    gate_grad, up_grad, mark = two_products(
+        tokens_turned, gate, features - some, gate_grad, up, some, (left[1], right[1])
+    )
     total, sent = join(left[0], left_got, right[0], right_got, (mark,))
     for k, m in enumerate(masks[:0:-1]):
         if k > 0:

time: 100 us -> 99.7 us (level)
  starting transfers between devices: 23.8 us -> 25.8 us
  Pallas kernels: 59.3 us -> 58 us
  waiting for transfers between devices: 14.6 us -> 13.5 us
    ppermute x22, starting transfers between devices: 23.8 us -> 25.8 us  [swap(): return lax.ppermute(x, axis, [(i, i ^ mask) for i in range(n)])]
    pallas_call x24 -> x23, Pallas kernels: 59.3 us -> 58 us  [call(): pl.pallas_call(body, out_shape=list(out_shape) + [struct((8, 128), F32)]...]
    ppermute x22, waiting for transfers between devices: 14.6 us -> 13.5 us  [swap(): return lax.ppermute(x, axis, [(i, i ^ mask) for i in range(n)])]
  transfers between devices with their start and end apart: 22 -> 22, of which waited for: 7 -> 6; matrix products, arithmetic and copies ran while one was open for 1% -> 1% of each run, Pallas kernels for 59% -> 58%
where the time goes in v5:
time: 99.7 us; the launch traced here: 99.5 us
  Pallas kernels  58 us (58%)
  starting transfers between devices  25.8 us (26%)
  waiting for transfers between devices  13.5 us (14%)
  other arithmetic  1.34 us (1%)
    pallas_call x23, Pallas kernels, call(): pl.pallas_call(body, out_shape=list(out_shape) + [struct((8, 128), F32)]...  58 us
    ppermute x22, starting transfers between devices, swap(): return lax.ppermute(x, axis, [(i, i ^ mask) for i in range(n)])  25.8 us
    ppermute x22, waiting for transfers between devices, swap(): return lax.ppermute(x, axis, [(i, i ^ mask) for i in range(n)])  13.5 us
  transfers between devices with their start and end apart: 22, of which 6 were waited for; matrix products, arithmetic and copies ran while one was open for 1% of the time, Pallas kernels for 58%

profile of v5, /device:TPU:0, one launch (start us, length us, event | category | flops | bytes accessed | tf_op | source)
XLA Modules:
  0.0 99.5 jit_solution(8891599868629920081)
XLA Ops:
  0.6 3.1 %collective-permute-start.1 = (bf16[1,40,2048]{2,1,0:T(8,128)(2,1)}, bf16[1,40,2048]{2,1,0:T(8,128)(2,1)S(1)}, u32[]{:S(2)}, u32[]{:S(2)}) collective-permute-start(bf16[1,40,2048]{2,1,0:T(8,128)(2,1)} %bitcast.9), channel_id=1, source_target_pairs={{0,8},{4,12},{8,0},{12,4},{16,24},{20,28},{24,16},{28,20},{1,9},{5... | collective-permute-start | bytes 491528 | tf_op jit(solution)/shard_map/ppermute | solution.py:387
  3.7 1.5 %collective-permute-start.2 = (bf16[1,40,2048]{2,1,0:T(8,128)(2,1)}, bf16[1,40,2048]{2,1,0:T(8,128)(2,1)S(1)}, u32[]{:S(2)}, u32[]{:S(2)}) collective-permute-start(bf16[1,40,2048]{2,1,0:T(8,128)(2,1)} %bitcast.10), channel_id=1, source_target_pairs={{0,4},{4,0},{8,12},{12,8},{16,20},{20,16},{24,28},{28,24},{1,5},{5... | collective-permute-start | bytes 491528 | tf_op jit(solution)/shard_map/ppermute | solution.py:387
  5.2 2.6 %collective-permute-start = (bf16[1,40,2048]{2,1,0:T(8,128)(2,1)}, bf16[1,40,2048]{2,1,0:T(8,128)(2,1)S(1)}, u32[]{:S(2)}, u32[]{:S(2)}) collective-permute-start(bf16[1,40,2048]{2,1,0:T(8,128)(2,1)} %bitcast.11), channel_id=1, source_target_pairs={{0,16},{4,20},{8,24},{12,28},{16,0},{20,4},{24,8},{28,12},{1,17},{... | collective-permute-start | bytes 491528 | tf_op jit(solution)/shard_map/ppermute | solution.py:387
  7.8 0.7 iota_xor_fusion
  8.5 5.0 %shard_map.111 = (bf16[1664,2048]{1,0:T(8,128)(2,1)S(1)}, bf16[1664,2048]{1,0:T(8,128)(2,1)S(1)}, f32[8,128]{1,0:T(8,128)S(1)}) custom-call(bf16[3328,2048]{1,0:T(8,128)(2,1)} %refs_1_.1, bf16[3328,2048]{1,0:T(8,128)(2,1)} %refs_1_.1, s32[8]{0:T(128)S(1)} %get-tuple-element.77.refs_2_.refs_0_, s32[8]{0:T(128)S(1)} %get-tuple-element.76.refs_3_.refs_1_), custom_call_target="tpu_custom_call" | custom-call | bytes 13631488 | tf_op jit(solution)/shard_map/pallas_call | solution.py:45
  13.5 0.0 collective-permute-done.1.refs_2_
  13.5 0.0 collective-permute-done.2.refs_3_.refs_4_
  13.5 1.7 %collective-permute-done.refs_0_ = bf16[1,40,2048]{2,1,0:T(8,128)(2,1)S(1)} collective-permute-done((bf16[1,40,2048]{2,1,0:T(8,128)(2,1)}, bf16[1,40,2048]{2,1,0:T(8,128)(2,1)S(1)}, u32[]{:S(2)}, u32[]{:S(2)}) %collective-permute-start) | collective-permute-done | bytes 163872 | tf_op jit(solution)/shard_map/ppermute | solution.py:387
  15.2 0.0 copy-start.2
  15.3 0.1 collective-permute-start.3
  15.3 0.7 collective-permute-start.4
  16.1 1.3 %collective-permute-start.5 = (bf16[1,40,2048]{2,1,0:T(8,128)(2,1)S(1)}, bf16[1,40,2048]{2,1,0:T(8,128)(2,1)S(1)}, u32[]{:S(2)}, u32[]{:S(2)}) collective-permute-start(bf16[1,40,2048]{2,1,0:T(8,128)(2,1)S(1)} %collective-permute-done.1.refs_2_), channel_id=1, source_target_pairs={{0,4},{4,0},{8,12},{12,8},{16,20},{20,16},{24,28},{28,24},{1,5},{5... | collective-permute-start | bytes 491528 | tf_op jit(solution)/shard_map/ppermute | solution.py:387
  17.4 3.2 %collective-permute-done.3.refs_4_.refs_3_.refs_1_ = bf16[1,40,2048]{2,1,0:T(8,128)(2,1)S(1)} collective-permute-done((bf16[1,40,2048]{2,1,0:T(8,128)(2,1)S(1)}, bf16[1,40,2048]{2,1,0:T(8,128)(2,1)S(1)}, u32[]{:S(2)}, u32[]{:S(2)}) %collective-permute-start.3) | collective-permute-done | bytes 163872 | tf_op jit(solution)/shard_map/ppermute | solution.py:387
  20.6 0.6 collective-permute-start.6
  21.2 1.1 %collective-permute-start.7 = (bf16[1,40,2048]{2,1,0:T(8,128)(2,1)S(1)}, bf16[1,40,2048]{2,1,0:T(8,128)(2,1)S(1)}, u32[]{:S(2)}, u32[]{:S(2)}) collective-permute-start(bf16[1,40,2048]{2,1,0:T(8,128)(2,1)S(1)} %shard_map.116.refs_0_), channel_id=1, source_target_pairs={{0,16},{4,20},{8,24},{12,28},{16,0},{20,4},{24,8},{28,12},{1,17},{... | collective-permute-start | bytes 491528 | tf_op jit(solution)/shard_map/ppermute | solution.py:387
  22.3 3.7 %shard_map.113 = (bf16[3328,320]{1,0:T(8,128)(2,1)S(1)}, f32[4,40,3328]{2,1,0:T(8,128)S(1)}, f32[4,40,3328]{2,1,0:T(8,128)S(1)}) custom-call(s32[8]{0:T(128)S(1)} %get-tuple-element.77.refs_2_.refs_0_, s32[8]{0:T(128)S(1)} %get-tuple-element.76.refs_3_.refs_1_, bf16[8,40,3328]{2,1,0:T(8,128)(2,1)S(1)} %bitcast.7, bf16[8,40,3328]{2,1,0:T(8,128)(2,1)S(1)} %bitcast.8, ...), custom_call_target="tpu_custom_call" | custom-call | flops 10649600 | bytes 10649600 | tf_op jit(solution)/shard_map/pallas_call | solution.py:45
  26.0 0.0 collective-permute-done.4.refs_5_
  26.0 0.0 collective-permute-done.5.refs_6_
  26.0 0.9 collective-permute-done.6.refs_7_
  26.9 0.1 shard_map.114.refs_1_
  27.0 2.6 %shard_map.115 = (f32[160,1664]{1,0:T(8,128)S(1)}, bf16[160,1664]{1,0:T(8,128)(2,1)S(1)}) custom-call(s32[1]{0:T(128)} %bitcast.refs_0_, bf16[320,2048]{1,0:T(8,128)(2,1)S(1)} %shard_map.114.refs_1_, bf16[1664,2048]{1,0:T(8,128)(2,1)S(1)} %get-tuple-element.43.refs_2_), custom_call_target="tpu_custom_call" | custom-call | flops 2181038080 | bytes 6815744 | tf_op jit(solution)/shard_map/pallas_call | solution.py:45
  29.6 0.1 collective-permute-start.9
  29.7 0.0 collective-permute-done.7.refs_4_.refs_1_
  29.7 2.6 %shard_map.117 = (f32[160,1664]{1,0:T(8,128)S(1)}, bf16[160,1664]{1,0:T(8,128)(2,1)S(1)}) custom-call(s32[1]{0:T(128)} %bitcast.refs_0_, bf16[320,2048]{1,0:T(8,128)(2,1)S(1)} %shard_map.114.refs_1_, bf16[1664,2048]{1,0:T(8,128)(2,1)S(1)} %get-tuple-element.42.refs_2_, bf16[160,1664]{1,0:T(8,128)(2,1)S(1)} %get-tuple-element.44.refs_3_, ...), custom_call_target="tpu_custom_call" | custom-call | flops 2181038080 | bytes 6815744 | tf_op jit(solution)/shard_map/pallas_call | solution.py:45
  32.4 0.6 collective-permute-start.8
  32.9 0.0 collective-permute-done.9.refs_1_
  32.9 0.1 shard_map.118.refs_2_
  33.0 1.9 %collective-permute-start.14 = (bf16[160,1664]{1,0:T(8,128)(2,1)S(1)}, bf16[160,1664]{1,0:T(8,128)(2,1)S(1)}, u32[]{:S(2)}, u32[]{:S(2)}) collective-permute-start(bf16[160,1664]{1,0:T(8,128)(2,1)S(1)} %shard_map.118.refs_2_), channel_id=1, source_target_pairs={{0,2},{1,3},{2,0},{3,1},{4,6},{5,7},{6,4},{7,5},{8,10},{9,11},{10,... | collective-permute-start | bytes 1597448 | tf_op jit(solution)/shard_map/ppermute | solution.py:387
  35.0 0.0 collective-permute-done.8.refs_1_
  35.0 0.1 shard_map.119.refs_6_
  35.1 1.4 %collective-permute-start.10 = (bf16[160,1664]{1,0:T(8,128)(2,1)S(1)}, bf16[160,1664]{1,0:T(8,128)(2,1)S(1)}, u32[]{:S(2)}, u32[]{:S(2)}) collective-permute-start(bf16[160,1664]{1,0:T(8,128)(2,1)S(1)} %shard_map.119.refs_6_), channel_id=1, source_target_pairs={{0,2},{1,3},{2,0},{3,1},{4,6},{5,7},{6,4},{7,5},{8,10},{9,11},{10,... | collective-permute-start | bytes 1597448 | tf_op jit(solution)/shard_map/ppermute | solution.py:387
  36.5 0.6 collective-permute-start.11
  37.1 1.7 %collective-permute-start.12 = (bf16[2,40,2048]{2,1,0:T(8,128)(2,1)S(1)}, bf16[2,40,2048]{2,1,0:T(8,128)(2,1)S(1)}, u32[]{:S(2)}, u32[]{:S(2)}) collective-permute-start(bf16[2,40,2048]{2,1,0:T(8,128)(2,1)S(1)} %shard_map.121), channel_id=1, source_target_pairs={{0,8},{4,12},{8,0},{12,4},{16,24},{20,28},{24,16},{28,20},{1,9},{5... | collective-permute-start | bytes 983048 | tf_op jit(solution)/shard_map/ppermute | solution.py:387
  38.9 13.6 %shard_map.120 = (bf16[3328,2048]{1,0:T(8,128)(2,1)}, bf16[1024,3328]{1,0:T(8,128)(2,1)S(1)}, bf16[1024,3328]{1,0:T(8,128)(2,1)S(1)}, bf16[1024,3328]{1,0:T(8,12...) custom-call(bf16[3328,320]{1,0:T(8,128)(2,1)S(1)} %get-tuple-element.41.refs_8_.refs_0_, ...), custom_call_target="tpu_custom_call" | custom-call | flops 4362076160 | bytes 13631488 | tf_op jit(solution)/shard_map/pallas_call | solution.py:45
  52.5 0.0 collective-permute-done.11.refs_6_.refs_3_
  52.5 0.0 collective-permute-done.12.refs_7_.refs_2_
  52.5 0.0 collective-permute-done.14.refs_2_
  52.5 0.4 shard_map.123.refs_3_
  52.9 0.1 collective-permute-start.15
  52.9 5.7 %collective-permute-done.10.refs_2_ = bf16[160,1664]{1,0:T(8,128)(2,1)S(1)} collective-permute-done((bf16[160,1664]{1,0:T(8,128)(2,1)S(1)}, bf16[160,1664]{1,0:T(8,128)(2,1)S(1)}, u32[]{:S(2)}, u32[]{:S(2)}) %collective-permute-start.10) | collective-permute-done | bytes 532512 | tf_op jit(solution)/shard_map/ppermute | solution.py:387
  58.7 0.4 shard_map.122.refs_1_
  59.0 0.1 collective-permute-start.13
  59.1 0.8 collective-permute-start.17
  60.0 0.0 collective-permute-done.15.refs_4_
  60.0 1.8 %collective-permute-done.13.refs_2_ = bf16[2,160,1664]{2,1,0:T(8,128)(2,1)S(1)} collective-permute-done((bf16[2,160,1664]{2,1,0:T(8,128)(2,1)S(1)}, bf16[2,160,1664]{2,1,0:T(8,128)(2,1)S(1)}, u32[]{:S(2)}, u32[]{:S(2)}) %collective-permute-start.13) | collective-permute-done | bytes 1064992 | tf_op jit(solution)/shard_map/ppermute | solution.py:387
  61.8 0.3 shard_map.124
  62.1 4.6 %shard_map.125 = (bf16[2,2,40,1024]{3,2,1,0:T(8,128)(2,1)S(1)}, bf16[2,2,40,1024]{3,2,1,0:T(8,128)(2,1)S(1)}, f32[8,128]{1,0:T(8,128)S(1)}) custom-call(bf16[320,3328]{1,0:T(8,128)(2,1)S(1)} %get-tuple-element.51.refs_0_.refs_1_, bf16[320,3328]{1,0:T(8,128)(2,1)S(1)} %get-tuple-element.52.refs_1_.refs_2_, bf16[1024,3328]{1,0:T(8,128)(2,1)S(1)} %get-tuple-element.53.refs_2_, ...), custom_call_target="tpu_custom_call" | custom-call | flops 4362076160 | bytes 13631488 | tf_op jit(solution)/shard_map/pallas_call | solution.py:45
  66.7 0.9 collective-permute-start.16
  67.5 4.6 %shard_map.127 = (bf16[2,2,40,1024]{3,2,1,0:T(8,128)(2,1)S(1)}, bf16[2,2,40,1024]{3,2,1,0:T(8,128)(2,1)S(1)}, f32[8,128]{1,0:T(8,128)S(1)}) custom-call(bf16[320,3328]{1,0:T(8,128)(2,1)S(1)} %get-tuple-element.51.refs_0_.refs_1_, bf16[320,3328]{1,0:T(8,128)(2,1)S(1)} %get-tuple-element.52.refs_1_.refs_2_, bf16[1024,3328]{1,0:T(8,128)(2,1)S(1)} %get-tuple-element.57.refs_2_, ...), custom_call_target="tpu_custom_call" | custom-call | flops 4362076160 | bytes 13631488 | tf_op jit(solution)/shard_map/pallas_call | solution.py:45
  72.1 1.8 %collective-permute-start.19 = (bf16[2,2,40,1024]{3,2,1,0:T(8,128)(2,1)S(1)}, bf16[2,2,40,1024]{3,2,1,0:T(8,128)(2,1)S(1)}, u32[]{:S(2)}, u32[]{:S(2)}) collective-permute-start(bf16[2,2,40,1024]{3,2,1,0:T(8,128)(2,1)S(1)} %get-tuple-element.65), channel_id=1, source_target_pairs={{0,8},{4,12},{8,0},{12,4},{16,24},{20,28},{24,16},{28,20},{1,9},{5... | collective-permute-start | bytes 983048 | tf_op jit(solution)/shard_map/ppermute | solution.py:387
  73.9 0.0 collective-permute-done.17.refs_4_
  73.9 0.5 shard_map.126.refs_0_
  74.4 6.8 %shard_map.128 = (bf16[2048,3328]{1,0:T(8,128)(2,1)}, f32[8,128]{1,0:T(8,128)S(1)}) custom-call(bf16[2048,320]{1,0:T(8,128)(2,1)S(1)} %shard_map.126.refs_0_, bf16[320,3328]{1,0:T(8,128)(2,1)S(1)} %get-tuple-element.51.refs_0_.refs_1_, f32[8,128]{1,0:T(8,128)S(1)} %get-tuple-element.60.refs_2_), custom_call_target="tpu_custom_call" | custom-call | flops 3271557120 | bytes 10223616 | tf_op jit(solution)/shard_map/pallas_call | solution.py:45
  81.1 0.0 collective-permute-done.16.refs_1_
  81.2 0.4 collective-permute-start.18
  81.6 0.1 collective-permute-done.19.refs_1_
  81.7 1.3 %collective-permute-start.20 = (bf16[2,40,1024]{2,1,0:T(8,128)(2,1)S(1)}, bf16[2,40,1024]{2,1,0:T(8,128)(2,1)S(1)}, u32[]{:S(2)}, u32[]{:S(2)}) collective-permute-start(bf16[2,40,1024]{2,1,0:T(8,128)(2,1)S(1)} %get-tuple-element.67.refs_5_), channel_id=1, source_target_pairs={{0,4},{4,0},{8,12},{12,8},{16,20},{20,16},{24,28},{28,24},{1,5},{5... | collective-permute-start | bytes 491528 | tf_op jit(solution)/shard_map/ppermute | solution.py:387
  83.0 5.2 %shard_map.131 = (bf16[2048,3328]{1,0:T(8,128)(2,1)}, bf16[2048,3328]{1,0:T(8,128)(2,1)}, f32[8,128]{1,0:T(8,128)S(1)}) custom-call(bf16[2048,320]{1,0:T(8,128)(2,1)S(1)} %shard_map.126.refs_0_, bf16[320,3328]{1,0:T(8,128)(2,1)S(1)} %get-tuple-element.51.refs_0_.refs_1_, ...), custom_call_target="tpu_custom_call", output_to_operand_aliasing={{0}: (3, {})} | custom-call | flops 2181038080 | bytes 6815744 | tf_op jit(solution)/shard_map/pallas_call | solution.py:45
  88.2 0.0 collective-permute-done.20.refs_3_
  88.2 0.0 collective-permute-done.18.refs_1_
  88.3 3.2 %collective-permute-start.21 = (bf16[1,40,2048]{2,1,0:T(8,128)(2,1)S(1)}, bf16[1,40,2048]{2,1,0:T(8,128)(2,1)S(1)}, u32[]{:S(2)}, u32[]{:S(2)}) collective-permute-start(bf16[1,40,2048]{2,1,0:T(8,128)(2,1)S(1)} %get-tuple-element.71.refs_3_), channel_id=1, source_target_pairs={{0,16},{4,20},{8,24},{12,28},{16,0},{20,4},{24,8},{28,12},{1,17},{... | collective-permute-start | bytes 491528 | tf_op jit(solution)/shard_map/ppermute | solution.py:387
  91.5 7.3 %shard_map.133 = (bf16[2048,3328]{1,0:T(8,128)(2,1)}, f32[8,128]{1,0:T(8,128)}) custom-call(bf16[2048,320]{1,0:T(8,128)(2,1)S(1)} %shard_map.126.refs_0_, bf16[320,3328]{1,0:T(8,128)(2,1)S(1)} %get-tuple-element.52.refs_1_.refs_2_, bf16[2048,3328]{1,0:T(8,128)(2,1)} %get-tuple-element.73.refs_2_, ...), custom_call_target="tpu_custom_call", output_to_operand_aliasing={{0}: (2, {})} | custom-call | flops 3271557120 | bytes 10223616 | tf_op jit(solution)/shard_map/pallas_call | solution.py:45
  98.8 0.0 collective-permute-done.21
  98.9 0.7 add_bitcast_fusion
  (13 shorter events, 0.2 us)
Async XLA Ops:
  0.6 12.9 %collective-permute-start.1 = (bf16[1,40,2048]{2,1,0:T(8,128)(2,1)}, bf16[1,40,2048]{2,1,0:T(8,128)(2,1)S(1)}, u32[]{:S(2)}, u32[]{:S(2)}) collective-permute-start(bf16[1,40,2048]{2,1,0:T(8,128)(2,1)} %bitcast.9), channel_id=1, source_target_pairs={{0,8},{4,12},{8,0},{12,4},{16,24},{20,28},{24,16},{28,20},{1,9},{5... | collective-permute-start | bytes 491528 | tf_op jit(solution)/shard_map/ppermute | solution.py:387
  3.7 9.8 %collective-permute-start.2 = (bf16[1,40,2048]{2,1,0:T(8,128)(2,1)}, bf16[1,40,2048]{2,1,0:T(8,128)(2,1)S(1)}, u32[]{:S(2)}, u32[]{:S(2)}) collective-permute-start(bf16[1,40,2048]{2,1,0:T(8,128)(2,1)} %bitcast.10), channel_id=1, source_target_pairs={{0,4},{4,0},{8,12},{12,8},{16,20},{20,16},{24,28},{28,24},{1,5},{5... | collective-permute-start | bytes 491528 | tf_op jit(solution)/shard_map/ppermute | solution.py:387
  5.2 10.0 %collective-permute-start = (bf16[1,40,2048]{2,1,0:T(8,128)(2,1)}, bf16[1,40,2048]{2,1,0:T(8,128)(2,1)S(1)}, u32[]{:S(2)}, u32[]{:S(2)}) collective-permute-start(bf16[1,40,2048]{2,1,0:T(8,128)(2,1)} %bitcast.11), channel_id=1, source_target_pairs={{0,16},{4,20},{8,24},{12,28},{16,0},{20,4},{24,8},{28,12},{1,17},{... | collective-permute-start | bytes 491528 | tf_op jit(solution)/shard_map/ppermute | solution.py:387
  8.5 12.8 %copy-start.3 = (bf16[40,2048]{1,0:T(8,128)(2,1)S(1)}, bf16[40,2048]{1,0:T(8,128)(2,1)}, u32[]{:S(2)}) copy-start(bf16[40,2048]{1,0:T(8,128)(2,1)} %param.8) | copy-start | bytes 491524
  8.5 13.8 %copy-start = (bf16[320,3328]{1,0:T(8,128)(2,1)S(1)}, bf16[320,3328]{1,0:T(8,128)(2,1)}, u32[]{:S(2)}) copy-start(bf16[320,3328]{1,0:T(8,128)(2,1)} %param.10) | copy-start | bytes 6389764
  8.5 13.8 %copy-start.1 = (bf16[320,3328]{1,0:T(8,128)(2,1)S(1)}, bf16[320,3328]{1,0:T(8,128)(2,1)}, u32[]{:S(2)}) copy-start(bf16[320,3328]{1,0:T(8,128)(2,1)} %param.11) | copy-start | bytes 6389764
  15.2 11.7 %copy-start.2 = (bf16[40,2048]{1,0:T(8,128)(2,1)S(1)}, bf16[40,2048]{1,0:T(8,128)(2,1)}, u32[]{:S(2)}) copy-start(bf16[40,2048]{1,0:T(8,128)(2,1)} %param.9) | copy-start | bytes 491524
  15.3 5.4 %collective-permute-start.3 = (bf16[1,40,2048]{2,1,0:T(8,128)(2,1)S(1)}, bf16[1,40,2048]{2,1,0:T(8,128)(2,1)S(1)}, u32[]{:S(2)}, u32[]{:S(2)}) collective-permute-start(bf16[1,40,2048]{2,1,0:T(8,128)(2,1)S(1)} %shard_map.112.refs_1_), channel_id=1, source_target_pairs={{0,8},{4,12},{8,0},{12,4},{16,24},{20,28},{24,16},{28,20},{1,9},{5... | collective-permute-start | bytes 491528 | tf_op jit(solution)/shard_map/ppermute | solution.py:387
  15.3 10.7 %collective-permute-start.4 = (bf16[1,40,2048]{2,1,0:T(8,128)(2,1)S(1)}, bf16[1,40,2048]{2,1,0:T(8,128)(2,1)S(1)}, u32[]{:S(2)}, u32[]{:S(2)}) collective-permute-start(bf16[1,40,2048]{2,1,0:T(8,128)(2,1)S(1)} %shard_map.112.refs_1_), channel_id=1, source_target_pairs={{0,4},{4,0},{8,12},{12,8},{16,20},{20,16},{24,28},{28,24},{1,5},{5... | collective-permute-start | bytes 491528 | tf_op jit(solution)/shard_map/ppermute | solution.py:387
  16.1 9.9 %collective-permute-start.5 = (bf16[1,40,2048]{2,1,0:T(8,128)(2,1)S(1)}, bf16[1,40,2048]{2,1,0:T(8,128)(2,1)S(1)}, u32[]{:S(2)}, u32[]{:S(2)}) collective-permute-start(bf16[1,40,2048]{2,1,0:T(8,128)(2,1)S(1)} %collective-permute-done.1.refs_2_), channel_id=1, source_target_pairs={{0,4},{4,0},{8,12},{12,8},{16,20},{20,16},{24,28},{28,24},{1,5},{5... | collective-permute-start | bytes 491528 | tf_op jit(solution)/shard_map/ppermute | solution.py:387
  20.6 6.3 %collective-permute-start.6 = (bf16[1,40,2048]{2,1,0:T(8,128)(2,1)S(1)}, bf16[1,40,2048]{2,1,0:T(8,128)(2,1)S(1)}, u32[]{:S(2)}, u32[]{:S(2)}) collective-permute-start(bf16[1,40,2048]{2,1,0:T(8,128)(2,1)S(1)} %collective-permute-done.3.refs_4_.refs_3_.refs_1_), channel_id=1, source_target_pairs={{0,4},{4,0},{8,12},{12,8},{16,20},{20,16},{24,28},{28,24},{1,5},{5... | collective-permute-start | bytes 491528 | tf_op jit(solution)/shard_map/ppermute | solution.py:387
  21.2 8.5 %collective-permute-start.7 = (bf16[1,40,2048]{2,1,0:T(8,128)(2,1)S(1)}, bf16[1,40,2048]{2,1,0:T(8,128)(2,1)S(1)}, u32[]{:S(2)}, u32[]{:S(2)}) collective-permute-start(bf16[1,40,2048]{2,1,0:T(8,128)(2,1)S(1)} %shard_map.116.refs_0_), channel_id=1, source_target_pairs={{0,16},{4,20},{8,24},{12,28},{16,0},{20,4},{24,8},{28,12},{1,17},{... | collective-permute-start | bytes 491528 | tf_op jit(solution)/shard_map/ppermute | solution.py:387
  29.6 3.3 %collective-permute-start.9 = (bf16[160,1664]{1,0:T(8,128)(2,1)S(1)}, bf16[160,1664]{1,0:T(8,128)(2,1)S(1)}, u32[]{:S(2)}, u32[]{:S(2)}) collective-permute-start(bf16[160,1664]{1,0:T(8,128)(2,1)S(1)} %get-tuple-element.44.refs_3_), channel_id=1, source_target_pairs={{0,1},{1,0},{2,3},{3,2},{4,5},{5,4},{6,7},{7,6},{8,9},{9,8},{10,11... | collective-permute-start | bytes 1597448 | tf_op jit(solution)/shard_map/ppermute | solution.py:387
  32.4 2.6 %collective-permute-start.8 = (bf16[160,1664]{1,0:T(8,128)(2,1)S(1)}, bf16[160,1664]{1,0:T(8,128)(2,1)S(1)}, u32[]{:S(2)}, u32[]{:S(2)}) collective-permute-start(bf16[160,1664]{1,0:T(8,128)(2,1)S(1)} %get-tuple-element.46), channel_id=1, source_target_pairs={{0,1},{1,0},{2,3},{3,2},{4,5},{5,4},{6,7},{7,6},{8,9},{9,8},{10,11... | collective-permute-start | bytes 1597448 | tf_op jit(solution)/shard_map/ppermute | solution.py:387
  33.0 19.4 %collective-permute-start.14 = (bf16[160,1664]{1,0:T(8,128)(2,1)S(1)}, bf16[160,1664]{1,0:T(8,128)(2,1)S(1)}, u32[]{:S(2)}, u32[]{:S(2)}) collective-permute-start(bf16[160,1664]{1,0:T(8,128)(2,1)S(1)} %shard_map.118.refs_2_), channel_id=1, source_target_pairs={{0,2},{1,3},{2,0},{3,1},{4,6},{5,7},{6,4},{7,5},{8,10},{9,11},{10,... | collective-permute-start | bytes 1597448 | tf_op jit(solution)/shard_map/ppermute | solution.py:387
  35.1 23.6 %collective-permute-start.10 = (bf16[160,1664]{1,0:T(8,128)(2,1)S(1)}, bf16[160,1664]{1,0:T(8,128)(2,1)S(1)}, u32[]{:S(2)}, u32[]{:S(2)}) collective-permute-start(bf16[160,1664]{1,0:T(8,128)(2,1)S(1)} %shard_map.119.refs_6_), channel_id=1, source_target_pairs={{0,2},{1,3},{2,0},{3,1},{4,6},{5,7},{6,4},{7,5},{8,10},{9,11},{10,... | collective-permute-start | bytes 1597448 | tf_op jit(solution)/shard_map/ppermute | solution.py:387
  36.5 15.9 %collective-permute-start.11 = (bf16[2,40,2048]{2,1,0:T(8,128)(2,1)S(1)}, bf16[2,40,2048]{2,1,0:T(8,128)(2,1)S(1)}, u32[]{:S(2)}, u32[]{:S(2)}) collective-permute-start(bf16[2,40,2048]{2,1,0:T(8,128)(2,1)S(1)} %shard_map.121), channel_id=1, source_target_pairs={{0,4},{4,0},{8,12},{12,8},{16,20},{20,16},{24,28},{28,24},{1,5},{5... | collective-permute-start | bytes 983048 | tf_op jit(solution)/shard_map/ppermute | solution.py:387
  37.1 15.3 %collective-permute-start.12 = (bf16[2,40,2048]{2,1,0:T(8,128)(2,1)S(1)}, bf16[2,40,2048]{2,1,0:T(8,128)(2,1)S(1)}, u32[]{:S(2)}, u32[]{:S(2)}) collective-permute-start(bf16[2,40,2048]{2,1,0:T(8,128)(2,1)S(1)} %shard_map.121), channel_id=1, source_target_pairs={{0,8},{4,12},{8,0},{12,4},{16,24},{20,28},{24,16},{28,20},{1,9},{5... | collective-permute-start | bytes 983048 | tf_op jit(solution)/shard_map/ppermute | solution.py:387
  52.9 7.1 %collective-permute-start.15 = (bf16[2,160,1664]{2,1,0:T(8,128)(2,1)S(1)}, bf16[2,160,1664]{2,1,0:T(8,128)(2,1)S(1)}, u32[]{:S(2)}, u32[]{:S(2)}) collective-permute-start(bf16[2,160,1664]{2,1,0:T(8,128)(2,1)S(1)} %shard_map.123.refs_3_), channel_id=1, source_target_pairs={{0,1},{1,0},{2,3},{3,2},{4,5},{5,4},{6,7},{7,6},{8,9},{9,8},{10,11... | collective-permute-start | bytes 3194888 | tf_op jit(solution)/shard_map/ppermute | solution.py:387
  59.0 2.7 %collective-permute-start.13 = (bf16[2,160,1664]{2,1,0:T(8,128)(2,1)S(1)}, bf16[2,160,1664]{2,1,0:T(8,128)(2,1)S(1)}, u32[]{:S(2)}, u32[]{:S(2)}) collective-permute-start(bf16[2,160,1664]{2,1,0:T(8,128)(2,1)S(1)} %shard_map.122.refs_1_), channel_id=1, source_target_pairs={{0,1},{1,0},{2,3},{3,2},{4,5},{5,4},{6,7},{7,6},{8,9},{9,8},{10,11... | collective-permute-start | bytes 3194888 | tf_op jit(solution)/shard_map/ppermute | solution.py:387
  59.1 14.8 %collective-permute-start.17 = (bf16[2,40,2048]{2,1,0:T(8,128)(2,1)S(1)}, bf16[2,40,2048]{2,1,0:T(8,128)(2,1)S(1)}, u32[]{:S(2)}, u32[]{:S(2)}) collective-permute-start(bf16[2,40,2048]{2,1,0:T(8,128)(2,1)S(1)} %collective-permute-done.12.refs_7_.refs_2_), channel_id=1, source_target_pairs={{0,4},{4,0},{8,12},{12,8},{16,20},{20,16},{24,28},{28,24},{1,5},{5... | collective-permute-start | bytes 983048 | tf_op jit(solution)/shard_map/ppermute | solution.py:387
  66.7 14.5 %collective-permute-start.16 = (bf16[2,2,40,1024]{3,2,1,0:T(8,128)(2,1)S(1)}, bf16[2,2,40,1024]{3,2,1,0:T(8,128)(2,1)S(1)}, u32[]{:S(2)}, u32[]{:S(2)}) collective-permute-start(bf16[2,2,40,1024]{3,2,1,0:T(8,128)(2,1)S(1)} %get-tuple-element.56), channel_id=1, source_target_pairs={{0,4},{4,0},{8,12},{12,8},{16,20},{20,16},{24,28},{28,24},{1,5},{5... | collective-permute-start | bytes 983048 | tf_op jit(solution)/shard_map/ppermute | solution.py:387
  72.1 9.5 %collective-permute-start.19 = (bf16[2,2,40,1024]{3,2,1,0:T(8,128)(2,1)S(1)}, bf16[2,2,40,1024]{3,2,1,0:T(8,128)(2,1)S(1)}, u32[]{:S(2)}, u32[]{:S(2)}) collective-permute-start(bf16[2,2,40,1024]{3,2,1,0:T(8,128)(2,1)S(1)} %get-tuple-element.65), channel_id=1, source_target_pairs={{0,8},{4,12},{8,0},{12,4},{16,24},{20,28},{24,16},{28,20},{1,9},{5... | collective-permute-start | bytes 983048 | tf_op jit(solution)/shard_map/ppermute | solution.py:387
  81.2 7.0 %collective-permute-start.18 = (bf16[2,40,1024]{2,1,0:T(8,128)(2,1)S(1)}, bf16[2,40,1024]{2,1,0:T(8,128)(2,1)S(1)}, u32[]{:S(2)}, u32[]{:S(2)}) collective-permute-start(bf16[2,40,1024]{2,1,0:T(8,128)(2,1)S(1)} %get-tuple-element.63.refs_3_.refs_4_), channel_id=1, source_target_pairs={{0,8},{4,12},{8,0},{12,4},{16,24},{20,28},{24,16},{28,20},{1,9},{5... | collective-permute-start | bytes 491528 | tf_op jit(solution)/shard_map/ppermute | solution.py:387
  81.7 6.5 %collective-permute-start.20 = (bf16[2,40,1024]{2,1,0:T(8,128)(2,1)S(1)}, bf16[2,40,1024]{2,1,0:T(8,128)(2,1)S(1)}, u32[]{:S(2)}, u32[]{:S(2)}) collective-permute-start(bf16[2,40,1024]{2,1,0:T(8,128)(2,1)S(1)} %get-tuple-element.67.refs_5_), channel_id=1, source_target_pairs={{0,4},{4,0},{8,12},{12,8},{16,20},{20,16},{24,28},{28,24},{1,5},{5... | collective-permute-start | bytes 491528 | tf_op jit(solution)/shard_map/ppermute | solution.py:387
  88.3 10.6 %collective-permute-start.21 = (bf16[1,40,2048]{2,1,0:T(8,128)(2,1)S(1)}, bf16[1,40,2048]{2,1,0:T(8,128)(2,1)S(1)}, u32[]{:S(2)}, u32[]{:S(2)}) collective-permute-start(bf16[1,40,2048]{2,1,0:T(8,128)(2,1)S(1)} %get-tuple-element.71.refs_3_), channel_id=1, source_target_pairs={{0,16},{4,20},{8,24},{12,28},{16,0},{20,4},{24,8},{28,12},{1,17},{... | collective-permute-start | bytes 491528 | tf_op jit(solution)/shard_map/ppermute | solution.py:387
